TPU v7x, 32 devices: a whole 2x2x4 slice. The times are simulated.
32 devices in a mesh: rows: 4 (over x, core), cols: 8 (over z, y).
Axes of the slice: x: 2, y: 2, z: 4, core: 2. Of those that a mesh axis runs over, the one named last changes fastest.
Arguments:
- slab: float32 [32768, 2048], P('rows', 'cols'), may hold values from -6 to 6
- sign_bits: int32 [32768], P('rows'), may hold values from 0 to 1
- sample_rows: int32 [4096], replicated, may hold values from 0 to 32767, as said below
Outputs:
- gram: float32 [2048, 2048], P('rows', 'cols')
Inputs may be any that keep to these rules, and one draw needn't show every extreme that they name: `sample_rows`: Ascending; repeats may occur. At most 2048 indices fall in any one device's aligned block of 8192 rows, and some block holds exactly 2048.
All inputs are finite; a program needn't handle non-finite values.
Results may differ from a plain program's by a relative error of at most 0.000071.
Values sent between devices are 32-bit elements; how exact they have to be, the bound alone decides.
No kernel may reach another device: no remote copies, remote signals or barrier semaphores. Data moves between devices by JAX's collectives and lax.ppermute only.
A program may use at most 64 MiB of HBM per device.

v0:
```python
import jax
import jax.numpy as jnp
from jax import lax
from jax.sharding import PartitionSpec as P


def parity_table(length):
    index_list = jnp.arange(length, dtype=jnp.int32)
    common = index_list[:, None] & index_list[None, :]
    parity = jnp.zeros((length, length), jnp.int32)
    for bit_number in range(max(length.bit_length() - 1, 0)):
        parity = parity + (common >> bit_number & 1)
    return (1 - 2 * (parity % 2)).astype(jnp.float32)


def local_transform(slab, sign_bits):
    height, columns = slab.shape
    flipped = slab * (1 - 2 * sign_bits).astype(jnp.float32)[:, None]
    blocks = flipped.reshape(height // 128, 128, columns)
    inside = jnp.einsum("ij,qjc->qic", parity_table(128), blocks, precision=lax.Precision.HIGHEST)
    outside = jnp.einsum(
        "pq,qic->pic", parity_table(height // 128), inside, precision=lax.Precision.HIGHEST
    )
    return outside.reshape(height, columns)


def column_product(portion, own_rows):
    return lax.dot_general(
        portion,
        own_rows,
        (((0,), (0,)), ((), ())),
        precision=lax.Precision.HIGHEST,
        preferred_element_type=jnp.float32,
    )


def shards(slab, sign_bits, sample_rows):
    mixed_rows = local_transform(slab, sign_bits)
    height = mixed_rows.shape[0]
    groups = lax.axis_size("rows")
    my_index = lax.axis_index("rows")
    samples = sample_rows.shape[0]
    factor = 1.0 / (samples * height * groups)
    owners = sample_rows // height
    offsets = sample_rows - owners * height
    picked = jnp.take(mixed_rows, offsets, axis=0)
    common = owners & my_index
    parity = jnp.zeros_like(common)
    for bit_number in range(groups.bit_length() - 1):
        parity = parity + (common >> bit_number & 1)
    signed = (1 - 2 * (parity % 2)).astype(jnp.float32)
    own_rows = lax.psum_scatter(picked * signed[:, None], "rows", scatter_dimension=0, tiled=True)
    terms = column_product(lax.all_gather(own_rows, "cols", axis=1, tiled=True), own_rows)
    return lax.psum_scatter(terms * factor, "rows", scatter_dimension=0, tiled=True)


def solution(mesh):
    return jax.shard_map(
        shards,
        mesh=mesh,
        in_specs=(P("rows", "cols"), P("rows"), P()),
        out_specs=P("rows", "cols"),
        check_vma=False,
    )
```

profile of v0, /device:TPU:18, one launch (start us, length us, event | category | flops | bytes accessed | tf_op | source)
XLA Modules:
  0.0 304.9 jit_solution(10831982224220921979)
XLA Ops:
  6.5 0.0 reduce-scatter.3.cloned.1.call-start
  6.5 0.8 subtract_convert_fusion
  7.3 4.1 %broadcast_multiply_fusion = f32[8192,256]{1,0:T(8,128)S(1)} fusion(f32[8192,256]{1,0:T(8,128)} %param.3, f32[8192]{0:T(1024)S(1)} %subtract_convert_fusion), kind=kLoop, calls=%fused_computation.4 | loop fusion | flops 2097152 | bytes 16809984 | tf_op jit(solution)/shard_map/mul | solution.py:18
  11.4 15.6 %fusion.7 = f32[64,256,128]{2,1,0:T(8,128)} fusion(f32[64,128,256]{2,1,0:T(8,128)S(1)} %bitcast.15), kind=kOutput, calls=%fused_computation.14 | convolution fusion | flops 3221798912 | bytes 16777216 | tf_op jit(solution)/shard_map/ij,qjc->qic/dot_general | solution.py:20
  27.0 9.2 %copy.5 = f32[64,256,128]{1,0,2:T(8,128)} copy(f32[64,256,128]{2,1,0:T(8,128)} %fusion.7) | data formatting | bytes 16777216 | tf_op jit(solution)/shard_map/ij,qjc->qic/dot_general | solution.py:20
  36.2 10.2 %fusion = f32[64,128,256]{2,0,1:T(8,128)S(1)} fusion(f32[64,256,128]{1,0,2:T(8,128)} %copy.5), kind=kOutput, calls=%fused_computation.1 | convolution fusion | flops 1610743808 | bytes 16777216 | tf_op jit(solution)/shard_map/pq,qic->pic/dot_general | solution.py:21
  46.5 0.0 copy-start
  46.5 8.1 %copy.4 = f32[64,128,256]{2,1,0:T(8,128)} copy(f32[64,128,256]{2,0,1:T(8,128)S(1)} %fusion) | data formatting | bytes 16777216 | tf_op jit(solution)/shard_map/pq,qic->pic/dot_general | solution.py:21
  54.6 0.0 copy-done
  54.6 19.4 %gather_fusion = f32[4096,256]{1,0:T(8,128)} fusion(f32[8192,256]{1,0:T(8,128)} %bitcast.14, s32[4096]{0:T(1024)S(1)} %get-tuple-element.6), kind=kCustom, calls=%fused_computation | custom fusion | bytes 8404992 | tf_op jit(solution)/shard_map/jit(_take)/gather | solution.py:46
  74.0 5.3 %select_multiply_fusion = f32[4096,256]{1,0:T(8,128)} fusion(f32[4096,256]{1,0:T(8,128)} %gather_fusion, f32[4096]{0:T(1024)S(1)} %get-tuple-element.5, pred[4096]{0:T(1024)(128)(4,1)S(1)} %compare_and_fusion), kind=kLoop, calls=%fused_computation.3 | loop fusion | flops 2097152 | bytes 8409088 | tf_op jit(solution)/shard_map/mul | solution.py:52
  79.3 0.0 reduce-scatter.3.cloned.1.call-update
  79.3 0.0 all-gather.2.cloned.1.call-start
  79.4 44.8 %reduce-scatter.3.cloned.1.call-done = f32[1024,256]{1,0:T(8,128)} async-done(((f32[4096,256]{1,0:T(8,128)}), f32[1024,256]{1,0:T(8,128)}) %reduce-scatter.3.cloned.1.call-update) | async-done | bytes 1048592 | tf_op jit(solution)/shard_map/reduce_scatter | solution.py:52
  124.1 0.0 all-gather.2.cloned.1.call-update
  124.2 0.0 reduce-scatter.5.cloned.1.call-start
  124.2 127.6 %all-gather.2.cloned.1.call-done = f32[1024,2048]{1,0:T(8,128)} async-done(((f32[1024,256]{1,0:T(8,128)}), f32[1024,2048]{1,0:T(8,128)}) %all-gather.2.cloned.1.call-update) | async-done | bytes 8388624 | tf_op jit(solution)/shard_map/all_gather | solution.py:53
  251.8 16.8 %convolution_multiply_fusion = f32[2048,256]{1,0:T(8,128)} fusion(f32[1024,2048]{1,0:T(8,128)} %all-gather.2.cloned.1.call-done, f32[1024,256]{1,0:T(8,128)} %reduce-scatter.3.cloned.1.call-done), kind=kOutput, calls=%fused_computation.5 | convolution fusion | flops 6442975232 | bytes 11534336 | tf_op jit(solution)/shard_map/dot_general | solution.py:28
  268.6 0.0 reduce-scatter.5.cloned.1.call-update
  268.7 29.7 %reduce-scatter.5.cloned.1.call-done = f32[512,256]{1,0:T(8,128)} async-done(((f32[2048,256]{1,0:T(8,128)}), f32[512,256]{1,0:T(8,128)}) %reduce-scatter.5.cloned.1.call-update) | async-done | bytes 524304 | tf_op jit(solution)/shard_map/reduce_scatter | solution.py:54
  (2 shorter events, 0.1 us)
Async XLA Ops:
  6.5 117.6 %reduce-scatter.3.cloned.1.call-start = ((), (), s32[]{:S(2)}) async-start(), calls=%async_computation.2 | async-start | bytes 5242880 | tf_op jit(solution)/shard_map/reduce_scatter | solution.py:52
  46.5 8.1 %copy-start = (s32[4096]{0:T(1024)S(1)}, s32[4096]{0:T(1024)}, u32[]{:S(2)}) copy-start(s32[4096]{0:T(1024)} %param.5) | copy-start | bytes 49156
  79.3 172.5 %all-gather.2.cloned.1.call-start = ((), (), s32[]{:S(2)}) async-start(), calls=%async_computation.3 | async-start | bytes 9437184 | tf_op jit(solution)/shard_map/all_gather | solution.py:53
  124.2 174.3 %reduce-scatter.5.cloned.1.call-start = ((), (), s32[]{:S(2)}) async-start(), calls=%async_computation.4 | async-start | bytes 2621440 | tf_op jit(solution)/shard_map/reduce_scatter | solution.py:54
Sparse Core Ops, SparseCore 0:
  79.5 44.6 reduce-scatter.2
  126.4 125.4 all-gather.1
  268.8 29.5 reduce-scatter.4
where the time goes:
time: 308 us; the launch traced here: 305 us
  waiting for transfers between devices  202 us (66%)
  matrix products  42.7 us (14%)
  local copies, waits for them, and re-layouts  36.7 us (12%)
  between operations  13.1 us (4%)
  other arithmetic  10.2 us (3%)
    all_gather x1, waiting for transfers between devices, shards(): lax.all_gather(own_rows, 'cols', axis=1, tiled=True)  128 us
    reduce_scatter x1, waiting for transfers between devices, shards(): lax.psum_scatter(picked * signed[:, None], 'rows', scatter_dimension=0, t...  44.8 us
    reduce_scatter x1, waiting for transfers between devices, shards(): lax.psum_scatter(terms * factor, 'rows', scatter_dimension=0, tiled=True)  29.7 us
    gather x1, local copies, waits for them, and re-layouts, shards(): picked = jnp.take(mixed_rows, offsets, axis=0)  19.4 us
    dot_general x1, matrix products, column_product(): lax.dot_general(portion, own_rows, (((0,), (0,)), ((), ())), precision=la...  16.8 us
    dot_general x1, matrix products, local_transform(): jnp.einsum('ij,qjc->qic', parity_table(128), blocks, precision=lax.Precis...  15.6 us
    dot_general x1, matrix products, local_transform(): jnp.einsum('pq,qic->pic', parity_table(height // 128), inside, precision=...  10.2 us
    dot_general x1, local copies, waits for them, and re-layouts, local_transform(): jnp.einsum('ij,qjc->qic', parity_table(128), blocks, precision=lax.Precis...  9.2 us
  transfers between devices with their start and end apart: 3, of which 3 were waited for; matrix products, arithmetic and copies ran while one was open for 0% of the time, Pallas kernels for 0%

commit v1 on v0

v1 whole, which is shorter than its diff:
```python
import functools

import jax
import jax.numpy as jnp
from jax import lax
from jax.experimental import pallas as pl
from jax.experimental.pallas import tpu as pltpu
from jax.sharding import PartitionSpec as P

LANES = 128
INNER = 128
AXES = ("rows", "cols")


def bit_reverse(value, bits):
    return sum(((value >> at) & 1) << (bits - 1 - at) for at in range(bits))


def butterflies(parts):
    stride = 1
    while stride < len(parts):
        for at in range(len(parts)):
            if not at & stride:
                low, high = parts[at], parts[at + stride]
                parts[at], parts[at + stride] = low + high, low - high
        stride *= 2
    return parts


def transform_and_pick(groups, me_ref, index_ref, slab_ref, flip_ref, keep_ref, send_ref, mixed):
    step, steps = pl.program_id(0), mixed.shape[0] // 2 // slab_ref.shape[0]
    block = slab_ref.shape[0]
    height = block * steps
    base = step * block

    row = lax.broadcasted_iota(jnp.int32, (INNER, 2 * INNER), 0)
    col = lax.broadcasted_iota(jnp.int32, (INNER, 2 * INNER), 1) & (INNER - 1)
    common = row & col
    for shift in (4, 2, 1):
        common = common ^ (common >> shift)
    table = (1 - 2 * (common & 1)).astype(jnp.float32)

    inner_blocks = block // INNER
    for at in range(inner_blocks):
        flip = flip_ref[0, at : at + 1, :]
        signed = (table * jnp.concatenate([flip, flip], axis=1)).astype(jnp.bfloat16)
        values = slab_ref[at * INNER : (at + 1) * INNER, :]
        high = values.astype(jnp.bfloat16)
        low = (values - high.astype(jnp.float32)).astype(jnp.bfloat16)
        mixed[pl.ds(pl.multiple_of(base + at * INNER, INNER), INNER), :] = jnp.dot(
            signed, jnp.concatenate([high, low], axis=0), preferred_element_type=jnp.float32
        )

    def combine(starts, negate):
        parts = butterflies([mixed[pl.ds(pl.multiple_of(s, 8), 8), :] for s in starts])
        for s, part in zip(starts, parts):
            mixed[pl.ds(pl.multiple_of(s, 8), 8), :] = part
            if negate:
                mixed[pl.ds(pl.multiple_of(s + height, 8), 8), :] = -part

    @pl.loop(0, INNER // 8, unroll=4)
    def _(tile):
        combine([base + at * INNER + tile * 8 for at in range(inner_blocks)], False)

    @pl.when(step == steps - 1)
    def _():
        @pl.loop(0, block // 8, unroll=4)
        def _(tile):
            combine([at * block + tile * 8 for at in range(steps)], True)

        count = index_ref.shape[0] // groups
        bits = groups.bit_length() - 1
        half = max(groups // 2, 1)
        for place in range(groups):
            out = keep_ref if place < half else send_ref
            start = (me_ref[0] ^ bit_reverse(place, bits)) * count
            to = (place % half) * count

            @pl.loop(0, count // 16)
            def _(chunk):
                for at in range(16):
                    source = index_ref[start + chunk * 16 + at]
                    out[pl.ds(to + chunk * 16 + at, 1), :] = mixed[pl.ds(source, 1), :]


def picked_strip(slab, flips, index, me, groups, strip):
    height = slab.shape[0]
    samples = index.shape[0]
    block = min(1024, height)
    half = jax.ShapeDtypeStruct((samples // 2, LANES), jnp.float32)
    return pl.pallas_call(
        functools.partial(transform_and_pick, groups),
        out_shape=(half, half),
        grid_spec=pltpu.PrefetchScalarGridSpec(
            num_scalar_prefetch=2,
            grid=(height // block,),
            in_specs=[
                pl.BlockSpec((block, LANES), lambda step, *_: (step, strip)),
                pl.BlockSpec((1, block // INNER, INNER), lambda step, *_: (step, 0, 0)),
            ],
            out_specs=[pl.BlockSpec((samples // 2, LANES), lambda step, *_: (0, 0))] * 2,
            scratch_shapes=[pltpu.VMEM((2 * height, LANES), jnp.float32)],
        ),
        compiler_params=pltpu.CompilerParams(vmem_limit_bytes=40 * 1024 * 1024),
        cost_estimate=pl.CostEstimate(
            flops=4 * height * INNER * LANES, bytes_accessed=4 * LANES * (height + samples), transcendentals=0
        ),
        name="transform_and_pick",
    )(me, index, slab, flips)


def column_product(portion, own_rows):
    return lax.dot_general(
        portion,
        own_rows,
        (((0,), (0,)), ((), ())),
        precision=lax.Precision.HIGH,
        preferred_element_type=jnp.float32,
    )


def shards(slab, sign_bits, sample_rows):
    height, width = slab.shape
    groups = lax.axis_size("rows")
    me = lax.axis_index("rows")
    samples = sample_rows.shape[0]
    factor = 1.0 / (samples * height * groups)
    bits = groups.bit_length() - 1

    owners = sample_rows // height
    common = owners & me
    parity = jnp.zeros_like(common)
    for at in range(bits):
        parity = parity ^ ((common >> at) & 1)
    index = sample_rows - owners * height + parity * height
    block = min(1024, height)
    flips = (1 - 2 * sign_bits).astype(jnp.float32).reshape(height // block, block // INNER, INNER)
    me_array = me.reshape(1)

    strips = []
    for strip in range(width // LANES):
        keep, send = picked_strip(slab, flips, index, me_array, groups, strip)
        for at in range(bits):
            pairs = [(r, r ^ (1 << at)) for r in range(groups)]
            got = lax.ppermute(send, "rows", pairs)
            half = keep.shape[0] // 2
            if at < bits - 1:
                keep, send = keep[:half] + got[:half], keep[half:] + got[half:]
            else:
                keep = keep + got
        strips.append(keep)
    own_rows = jnp.concatenate(strips, axis=1)
    terms = column_product(lax.all_gather(own_rows, "cols", axis=1, tiled=True), own_rows)
    return lax.psum_scatter(terms * factor, "rows", scatter_dimension=0, tiled=True)


def solution(mesh):
    return jax.shard_map(
        shards,
        mesh=mesh,
        in_specs=(P("rows", "cols"), P("rows"), P()),
        out_specs=P("rows", "cols"),
        check_vma=False,
    )
```

time: 308 us -> 234 us (0.76)
  local copies, waits for them, and re-layouts: 36.7 us -> 3.38 us
  matrix products: 42.7 us -> 10.6 us
  waiting for transfers between devices: 202 us -> 179 us
  Pallas kernels: 0 us -> 20 us
  other arithmetic: 10.2 us -> 2.98 us
    reduce_scatter x1 -> x0, waiting for transfers between devices: 44.8 us -> none  [shards(): lax.psum_scatter(picked * signed[:, None], 'rows', scatter_dimension=0, t...]
    dot_general x2 -> x0, matrix products: 25.8 us -> none  [the longest x1 15.6 us: local_transform(): jnp.einsum('ij,qjc->qic', parity_table(128), blocks, precision=lax.Precis...]
    ppermute x0 -> x4, waiting for transfers between devices: none -> 23.8 us  [shards(): got = lax.ppermute(send, 'rows', pairs)]
    pallas_call x0 -> x2, Pallas kernels: none -> 20 us  [picked_strip(): pl.pallas_call(functools.partial(transform_and_pick, groups), out_shape=(...]
    gather x1 -> x0, local copies, waits for them, and re-layouts: 19.4 us -> none  [shards(): picked = jnp.take(mixed_rows, offsets, axis=0)]
    dot_general x2 -> x0, local copies, waits for them, and re-layouts: 17.3 us -> none  [the longest x1 9.2 us: local_transform(): jnp.einsum('ij,qjc->qic', parity_table(128), blocks, precision=lax.Precis...]
    mul x2 -> x0, other arithmetic: 9.35 us -> none  [the longest x1 5.26 us: shards(): picked * signed[:, None]]
    dot_general x1, matrix products: 16.8 us -> 10.6 us  [column_product(): lax.dot_general(portion, own_rows, (((0,), (0,)), ((), ())), precision=la...]
  transfers between devices with their start and end apart: 3 -> 6, of which waited for: 3 -> 5; matrix products, arithmetic and copies ran while one was open for 0% -> 0% of each run, Pallas kernels for 0% -> 4%
where the time goes in v1:
time: 234 us; the launch traced here: 231 us
  waiting for transfers between devices  179 us (76%)
  Pallas kernels  20 us (9%)
  between operations  13.4 us (6%)
  matrix products  10.6 us (5%)
  local copies, waits for them, and re-layouts  3.38 us (1%)
  other arithmetic  2.98 us (1%)
    all_gather x1, waiting for transfers between devices, shards(): lax.all_gather(own_rows, 'cols', axis=1, tiled=True)  126 us
    reduce_scatter x1, waiting for transfers between devices, shards(): lax.psum_scatter(terms * factor, 'rows', scatter_dimension=0, tiled=True)  29.7 us
    ppermute x4, waiting for transfers between devices, shards(): got = lax.ppermute(send, 'rows', pairs)  23.8 us
    pallas_call x2, Pallas kernels, picked_strip(): pl.pallas_call(functools.partial(transform_and_pick, groups), out_shape=(...  20 us
    dot_general x1, matrix products, column_product(): lax.dot_general(portion, own_rows, (((0,), (0,)), ((), ())), precision=la...  10.6 us
  transfers between devices with their start and end apart: 6, of which 5 were waited for; matrix products, arithmetic and copies ran while one was open for 0% of the time, Pallas kernels for 4%

profile of v1, /device:TPU:18, one launch (start us, length us, event | category | flops | bytes accessed | tf_op | source)
XLA Modules:
  0.0 231.4 jit_solution(7587239902029948747)
XLA Ops:
  6.5 0.0 all-gather.2.cloned.1.call-start
  6.5 0.8 convert_bitcast_fusion.flip_ref
  7.3 0.7 multiply_add_fusion.index_ref
  8.0 0.0 copy-start
  8.1 3.4 %copy-done = f32[8192,256]{1,0:T(8,128)S(1)} copy-done((f32[8192,256]{1,0:T(8,128)S(1)}, f32[8192,256]{1,0:T(8,128)}, u32[]{:S(2)}) %copy-start) | copy-done | bytes 8388632
  11.4 10.0 %transform_and_pick.3 = (f32[2048,128]{1,0:T(8,128)S(1)}, f32[2048,128]{1,0:T(8,128)S(1)}) custom-call(s32[1]{0:T(128)} %bitcast.me_ref, s32[4096]{0:T(1024)S(1)} %multiply_add_fusion.index_ref, f32[8192,256]{1,0:T(8,128)S(1)} %copy-done, f32[8,8,128]{2,1,0:T(8,128)S(1)} %convert_bitcast_fusion.flip_ref), custom_call_target="tpu_custom_call" | custom-call | flops 536870912 | bytes 6291456 | tf_op jit(solution)/shard_map/transform_and_pick/pallas_call | solution.py:91
  21.4 0.1 collective-permute-start.2
  21.5 10.0 %transform_and_pick.2 = (f32[2048,128]{1,0:T(8,128)S(1)}, f32[2048,128]{1,0:T(8,128)S(1)}) custom-call(s32[1]{0:T(128)} %bitcast.me_ref, s32[4096]{0:T(1024)S(1)} %multiply_add_fusion.index_ref, f32[8192,256]{1,0:T(8,128)S(1)} %copy-done, f32[8,8,128]{2,1,0:T(8,128)S(1)} %convert_bitcast_fusion.flip_ref), custom_call_target="tpu_custom_call" | custom-call | flops 536870912 | bytes 6291456 | tf_op jit(solution)/shard_map/transform_and_pick/pallas_call | solution.py:91
  31.5 0.6 collective-permute-start
  32.1 0.0 collective-permute-done.2
  32.1 0.1 slice_add_fusion
  32.2 0.6 collective-permute-start.3
  32.8 1.6 collective-permute-done
  34.4 0.1 slice_add_fusion.2
  34.4 0.6 collective-permute-start.1
  35.0 12.0 %collective-permute-done.3 = f32[1024,128]{1,0:T(8,128)S(1)} collective-permute-done((f32[1024,128]{1,0:T(8,128)S(1)}, f32[1024,128]{1,0:T(8,128)S(1)}, u32[]{:S(2)}, u32[]{:S(2)}) %collective-permute-start.3) | collective-permute-done | bytes 524320 | tf_op jit(solution)/shard_map/ppermute | solution.py:145
  47.0 0.1 fusion
  47.1 10.2 %collective-permute-done.1 = f32[1024,128]{1,0:T(8,128)S(1)} collective-permute-done((f32[1024,128]{1,0:T(8,128)S(1)}, f32[1024,128]{1,0:T(8,128)S(1)}, u32[]{:S(2)}, u32[]{:S(2)}) %collective-permute-start.1) | collective-permute-done | bytes 524320 | tf_op jit(solution)/shard_map/ppermute | solution.py:145
  57.3 0.1 fusion.1
  57.4 1.1 pad_maximum_fusion
  58.5 0.0 all-gather.2.cloned.1.call-update
  58.6 0.0 reduce-scatter.2.cloned.1.call-start
  58.6 125.6 %all-gather.2.cloned.1.call-done = f32[1024,2048]{1,0:T(8,128)} async-done(((f32[1024,256]{1,0:T(8,128)}), f32[1024,2048]{1,0:T(8,128)}) %all-gather.2.cloned.1.call-update) | async-done | bytes 8388624 | tf_op jit(solution)/shard_map/all_gather | solution.py:153
  184.3 10.6 %convolution_multiply_fusion = f32[2048,256]{1,0:T(8,128)} fusion(f32[1024,2048]{1,0:T(8,128)} %all-gather.2.cloned.1.call-done, f32[1024,128]{1,0:T(8,128)S(1)} %fusion, f32[1024,128]{1,0:T(8,128)S(1)} %fusion.1), kind=kOutput, calls=%fused_computation | convolution fusion | flops 3222011904 | bytes 11534336 | tf_op jit(solution)/shard_map/dot_general | solution.py:113
  194.9 0.0 reduce-scatter.2.cloned.1.call-update
  194.9 29.7 %reduce-scatter.2.cloned.1.call-done = f32[512,256]{1,0:T(8,128)} async-done(((f32[2048,256]{1,0:T(8,128)}), f32[512,256]{1,0:T(8,128)}) %reduce-scatter.2.cloned.1.call-update) | async-done | bytes 524304 | tf_op jit(solution)/shard_map/reduce_scatter | solution.py:154
Async XLA Ops:
  6.5 177.7 %all-gather.2.cloned.1.call-start = ((), (), s32[]{:S(2)}) async-start(), calls=%async_computation.1 | async-start | bytes 9437184 | tf_op jit(solution)/shard_map/all_gather | solution.py:153
  8.0 3.4 %copy-start = (f32[8192,256]{1,0:T(8,128)S(1)}, f32[8192,256]{1,0:T(8,128)}, u32[]{:S(2)}) copy-start(f32[8192,256]{1,0:T(8,128)} %slab_ref.3) | copy-start | bytes 25165828
  21.4 10.7 %collective-permute-start.2 = (f32[2048,128]{1,0:T(8,128)S(1)}, f32[2048,128]{1,0:T(8,128)S(1)}, u32[]{:S(2)}, u32[]{:S(2)}) collective-permute-start(f32[2048,128]{1,0:T(8,128)S(1)} %get-tuple-element.12), channel_id=1, source_target_pairs={{0,8},{8,0},{16,24},{24,16},{1,9},{9,1},{17,25},{25,17},{2,10},{10... | collective-permute-start | bytes 3145736 | tf_op jit(solution)/shard_map/ppermute | solution.py:145
  31.5 2.8 %collective-permute-start = (f32[2048,128]{1,0:T(8,128)S(1)}, f32[2048,128]{1,0:T(8,128)S(1)}, u32[]{:S(2)}, u32[]{:S(2)}) collective-permute-start(f32[2048,128]{1,0:T(8,128)S(1)} %get-tuple-element.10), channel_id=1, source_target_pairs={{0,8},{8,0},{16,24},{24,16},{1,9},{9,1},{17,25},{25,17},{2,10},{10... | collective-permute-start | bytes 3145736 | tf_op jit(solution)/shard_map/ppermute | solution.py:145
  32.2 14.8 %collective-permute-start.3 = (f32[1024,128]{1,0:T(8,128)S(1)}, f32[1024,128]{1,0:T(8,128)S(1)}, u32[]{:S(2)}, u32[]{:S(2)}) collective-permute-start(f32[1024,128]{1,0:T(8,128)S(1)} %slice_add_fusion), channel_id=1, source_target_pairs={{0,16},{8,24},{16,0},{24,8},{1,17},{9,25},{17,1},{25,9},{2,18},{10... | collective-permute-start | bytes 1572872 | tf_op jit(solution)/shard_map/ppermute | solution.py:145
  34.4 22.9 %collective-permute-start.1 = (f32[1024,128]{1,0:T(8,128)S(1)}, f32[1024,128]{1,0:T(8,128)S(1)}, u32[]{:S(2)}, u32[]{:S(2)}) collective-permute-start(f32[1024,128]{1,0:T(8,128)S(1)} %slice_add_fusion.2), channel_id=1, source_target_pairs={{0,16},{8,24},{16,0},{24,8},{1,17},{9,25},{17,1},{25,9},{2,18},{10... | collective-permute-start | bytes 1572872 | tf_op jit(solution)/shard_map/ppermute | solution.py:145
  58.6 166.0 %reduce-scatter.2.cloned.1.call-start = ((), (), s32[]{:S(2)}) async-start(), calls=%async_computation.2 | async-start | bytes 2621440 | tf_op jit(solution)/shard_map/reduce_scatter | solution.py:154
Sparse Core Ops, SparseCore 0:
  58.7 125.5 all-gather.1
  195.0 29.5 reduce-scatter.1

commit v2 on v1

--- a/solution.py
+++ b/solution.py
@@ -109,20 +109,89 @@
     )(me, index, slab, flips)
 
 
-def column_product(portion, own_rows):
-    return lax.dot_general(
-        portion,
-        own_rows,
-        (((0,), (0,)), ((), ())),
-        precision=lax.Precision.HIGH,
-        preferred_element_type=jnp.float32,
-    )
+def two_parts(values):
+    high = values.astype(jnp.bfloat16)
+    return high, (values - high.astype(jnp.float32)).astype(jnp.bfloat16)
+
+
+def three_products(left, right):
+    dot = functools.partial(jnp.dot, preferred_element_type=jnp.float32)
+    return dot(left[0], right[0]) + dot(left[0], right[1]) + dot(left[1], right[0])
+
+
+def pair_products(groups, near, strips, spot_ref, *refs):
+    refs = list(refs)
+
+    def take(count):
+        taken, refs[:count] = refs[:count], []
+        return taken
+
+    plane = [[take(strips) for _ in range(2)] for _ in range(near)]
+    remote = [[take(strips) for _ in range(2)] for _ in range(groups - 1)]
+    keep_ref, send_ref, turned_high, turned_low = refs
+    me, at_plane, at_near = spot_ref[0], spot_ref[1], spot_ref[2]
+    half, width = keep_ref.shape[0], keep_ref.shape[2]
+    depth = plane[0][0][0].shape[0]
+    bits = groups.bit_length() - 1
+
+    def whole(parts):
+        return jnp.concatenate([part[...] for part in parts], axis=1)
+
+    for off in range(near):
+        rows = pl.ds(pl.multiple_of((at_near ^ off) * width, width), width)
+        for side in range(2):
+            for strip in range(strips):
+                high, low = two_parts(plane[off][side][strip][...].T)
+                where = pl.ds(pl.multiple_of((at_near ^ off) * width + strip * LANES, LANES), LANES)
+                turned_high[side, where, :] = high
+                turned_low[side, where, :] = low
+
+    def store(other, value):
+        place = bit_reverse(other ^ me, bits)
+
+        @pl.when(place < half)
+        def _():
+            keep_ref[place] = value
+
+        @pl.when(place >= half)
+        def _():
+            send_ref[place - half] = value
+
+    def product(side, parts):
+        return three_products((turned_high[side], turned_low[side]), two_parts(whole(parts)))
+
+    store(at_plane, product(0, plane[0][0]) + product(1, plane[0][1]))
+    for away in range(1, groups):
+        for side in range(2):
+            other = at_plane - away if side == 0 else at_plane + away
+
+            @pl.when((other >= 0) & (other < groups))
+            def _():
+                store(other, product(side, remote[away - 1][side]))
+
+
+def finish(factor, spot_ref, total_ref, direct_ref, *refs):
+    out_ref, turned = refs[-1], refs[:-1]
+    me, at_plane, at_near = spot_ref[0], spot_ref[1], spot_ref[2]
+    width = out_ref.shape[1]
+
+    @pl.when(me == at_plane)
+    def _():
+        out_ref[...] = total_ref[...] * factor
+
+    @pl.when(me != at_plane)
+    def _():
+        for off in range(len(turned) + 1):
+            rows = pl.ds(pl.multiple_of((at_near ^ off) * width, width), width)
+            part = total_ref[rows, :] if off == 0 else turned[off - 1][...]
+            out_ref[rows, :] = (direct_ref[rows, :] + part.T) * factor
 
 
 def shards(slab, sign_bits, sample_rows):
     height, width = slab.shape
-    groups = lax.axis_size("rows")
-    me = lax.axis_index("rows")
+    groups, columns = lax.axis_size("rows"), lax.axis_size("cols")
+    near = columns // groups
+    me, column = lax.axis_index("rows"), lax.axis_index("cols")
     samples = sample_rows.shape[0]
     factor = 1.0 / (samples * height * groups)
     bits = groups.bit_length() - 1
@@ -135,23 +204,74 @@
     index = sample_rows - owners * height + parity * height
     block = min(1024, height)
     flips = (1 - 2 * sign_bits).astype(jnp.float32).reshape(height // block, block // INNER, INNER)
-    me_array = me.reshape(1)
-
-    strips = []
-    for strip in range(width // LANES):
-        keep, send = picked_strip(slab, flips, index, me_array, groups, strip)
+    spot = jnp.stack([me, column // near, column % near]).astype(jnp.int32)
+
+    def halve(keep, send, at):
+        got = lax.ppermute(send, "rows", [(r, r ^ (1 << at)) for r in range(groups)])
+        half = keep.shape[0] // 2
+        if at == bits - 1:
+            return keep, got
+        return keep[:half] + got[:half], keep[half:] + got[half:]
+
+    strips = width // LANES
+    plane = [[[] for _ in range(2)] for _ in range(near)]
+    remote = [[[] for _ in range(2)] for _ in range(groups - 1)]
+    for strip in range(strips):
+        keep, send = picked_strip(slab, flips, index, spot, groups, strip)
         for at in range(bits):
-            pairs = [(r, r ^ (1 << at)) for r in range(groups)]
-            got = lax.ppermute(send, "rows", pairs)
-            half = keep.shape[0] // 2
-            if at < bits - 1:
-                keep, send = keep[:half] + got[:half], keep[half:] + got[half:]
-            else:
-                keep = keep + got
-        strips.append(keep)
-    own_rows = jnp.concatenate(strips, axis=1)
-    terms = column_product(lax.all_gather(own_rows, "cols", axis=1, tiled=True), own_rows)
-    return lax.psum_scatter(terms * factor, "rows", scatter_dimension=0, tiled=True)
+            keep, send = halve(keep, send, at)
+        half = keep.shape[0] // 2
+        own = [keep[:half] + send[:half], keep[half:] + send[half:]]
+        moving = list(own)
+        for away in range(1, groups):
+            moving[0] = lax.ppermute(moving[0], "cols", [(c, c + near) for c in range((away - 1) * near, columns - near)])
+            moving[1] = lax.ppermute(moving[1], "cols", [(c, c - near) for c in range(near, columns - (away - 1) * near)])
+            for side in range(2):
+                remote[away - 1][side].append(moving[side])
+        for side in range(2):
+            plane[0][side].append(own[side])
+            for off in range(1, near):
+                plane[off][side].append(lax.ppermute(own[side], "cols", [(c, c ^ off) for c in range(columns)]))
+
+    operands = [part for group in plane + remote for side in group for part in side]
+    depth = operands[0].shape[0]
+    half_sums = jax.ShapeDtypeStruct((groups // 2, near * width, width), jnp.float32)
+    vmem = pl.BlockSpec(memory_space=pltpu.VMEM)
+    smem = pl.BlockSpec(memory_space=pltpu.SMEM)
+    keep, send = pl.pallas_call(
+        functools.partial(pair_products, groups, near, strips),
+        out_shape=(half_sums, half_sums),
+        in_specs=[smem] + [vmem] * len(operands),
+        out_specs=(vmem, vmem),
+        scratch_shapes=[pltpu.VMEM((2, near * width, depth), jnp.bfloat16)] * 2,
+        compiler_params=pltpu.CompilerParams(vmem_limit_bytes=40 * 1024 * 1024),
+        name="pair_products",
+    )(spot, *operands)
+    for at in range(bits):
+        keep, send = halve(keep, send, at)
+    total = (keep + send)[0]
+
+    direct = lax.ppermute(
+        total,
+        AXES,
+        [
+            (r * columns + c, c // near * columns + r * near + c % near)
+            for r in range(groups)
+            for c in range(columns)
+        ],
+    )
+    turned = []
+    for off in range(1, near):
+        part = lax.dynamic_slice_in_dim(total, (column % near ^ off) * width, width, 0)
+        turned.append(lax.ppermute(part, "cols", [(c, c ^ off) for c in range(columns)]))
+    return pl.pallas_call(
+        functools.partial(finish, factor),
+        out_shape=jax.ShapeDtypeStruct((near * width, width), jnp.float32),
+        in_specs=[smem] + [vmem] * (2 + len(turned)),
+        out_specs=vmem,
+        compiler_params=pltpu.CompilerParams(vmem_limit_bytes=16 * 1024 * 1024),
+        name="finish",
+    )(spot, total, direct, *turned)
 
 
 def solution(mesh):

time: 234 us -> 135 us (0.58)
  the two profiles are of different devices: /device:TPU:18 before, /device:TPU:29 now
where the time goes in v2:
time: 135 us; the launch traced here: 134 us
  waiting for transfers between devices  76.9 us (57%)
  starting transfers between devices  25.8 us (19%)
  Pallas kernels  25.5 us (19%)
  local copies, waits for them, and re-layouts  3.41 us (3%)
  other arithmetic  2.07 us (2%)
    ppermute x6, waiting for transfers between devices, halve(): got = lax.ppermute(send, 'rows', [(r, r ^ 1 << at) for r in range(groups)])  30.7 us
    ppermute x6, waiting for transfers between devices, shards(): lax.ppermute(moving[0], 'cols', [(c, c + near) for c in range((away - 1)...  20.6 us
    pallas_call x2, Pallas kernels, picked_strip(): pl.pallas_call(functools.partial(transform_and_pick, groups), out_shape=(...  20 us
    ppermute x1, waiting for transfers between devices, shards(): lax.ppermute(total, AXES, [(r * columns + c, c // near * columns + r * ne...  18.6 us
    ppermute x6, starting transfers between devices, shards(): lax.ppermute(moving[0], 'cols', [(c, c + near) for c in range((away - 1)...  7.71 us
    ppermute x6, starting transfers between devices, shards(): lax.ppermute(moving[1], 'cols', [(c, c - near) for c in range(near, colum...  6.9 us
    ppermute x6, starting transfers between devices, halve(): got = lax.ppermute(send, 'rows', [(r, r ^ 1 << at) for r in range(groups)])  6.88 us
    ppermute x1, waiting for transfers between devices, shards(): lax.ppermute(part, 'cols', [(c, c ^ off) for c in range(columns)])  6.39 us
  transfers between devices with their start and end apart: 24, of which 13 were waited for; matrix products, arithmetic and copies ran while one was open for 0% of the time, Pallas kernels for 7%

profile of v2, /device:TPU:29, one launch (start us, length us, event | category | flops | bytes accessed | tf_op | source)
XLA Modules:
  0.0 134.0 jit_solution(484125463372274383)
XLA Ops:
  0.0 0.8 convert_bitcast_fusion.flip_ref
  1.6 3.4 %copy-done = f32[8192,256]{1,0:T(8,128)S(1)} copy-done((f32[8192,256]{1,0:T(8,128)S(1)}, f32[8192,256]{1,0:T(8,128)}, u32[]{:S(2)}) %copy-start) | copy-done | bytes 8388632
  5.0 10.0 %transform_and_pick.3 = (f32[2048,128]{1,0:T(8,128)S(1)}, f32[2048,128]{1,0:T(8,128)S(1)}) custom-call(s32[3]{0:T(128)S(1)} %pad_add_fusion.me_ref.spot_ref, s32[4096]{0:T(1024)S(1)} %multiply_add_fusion.index_ref, f32[8192,256]{1,0:T(8,128)S(1)} %copy-done, f32[8,8,128]{2,1,0:T(8,128)S(1)} %convert_bitcast_fusion.flip_ref), custom_call_target="tpu_custom_call" | custom-call | flops 536870912 | bytes 6291456 | tf_op jit(solution)/shard_map/transform_and_pick/pallas_call | solution.py:91
  15.7 10.0 %transform_and_pick.2 = (f32[2048,128]{1,0:T(8,128)S(1)}, f32[2048,128]{1,0:T(8,128)S(1)}) custom-call(s32[3]{0:T(128)S(1)} %pad_add_fusion.me_ref.spot_ref, s32[4096]{0:T(1024)S(1)} %multiply_add_fusion.index_ref, f32[8192,256]{1,0:T(8,128)S(1)} %copy-done, f32[8,8,128]{2,1,0:T(8,128)S(1)} %convert_bitcast_fusion.flip_ref), custom_call_target="tpu_custom_call" | custom-call | flops 536870912 | bytes 6291456 | tf_op jit(solution)/shard_map/transform_and_pick/pallas_call | solution.py:91
  25.9 1.3 collective-permute-start.3
  27.2 1.2 collective-permute-done
  28.6 1.3 collective-permute-start.1
  29.9 9.1 %collective-permute-done.3 = f32[1024,128]{1,0:T(8,128)S(1)} collective-permute-done((f32[1024,128]{1,0:T(8,128)S(1)}, f32[1024,128]{1,0:T(8,128)S(1)}, u32[]{:S(2)}, u32[]{:S(2)}) %collective-permute-start.3) | collective-permute-done | bytes 524320 | tf_op jit(solution)/shard_map/ppermute | solution.py:210
  39.1 2.1 %collective-permute-start.11 = (f32[512,128]{1,0:T(8,128)S(1)}, f32[512,128]{1,0:T(8,128)S(1)}, u32[]{:S(2)}, u32[]{:S(2)}) collective-permute-start(f32[512,128]{1,0:T(8,128)S(1)} %get-tuple-element.21.refs_3_), channel_id=1, source_target_pairs={{2,0},{3,1},{4,2},{5,3},{6,4},{7,5},{10,8},{11,9},{12,10},{13,11},... | collective-permute-start | bytes 786440 | tf_op jit(solution)/shard_map/ppermute | solution.py:228
  41.4 1.3 collective-permute-start.9
  42.7 1.3 collective-permute-start.5
  44.1 6.2 %collective-permute-done.1 = f32[1024,128]{1,0:T(8,128)S(1)} collective-permute-done((f32[1024,128]{1,0:T(8,128)S(1)}, f32[1024,128]{1,0:T(8,128)S(1)}, u32[]{:S(2)}, u32[]{:S(2)}) %collective-permute-start.1) | collective-permute-done | bytes 524320 | tf_op jit(solution)/shard_map/ppermute | solution.py:210
  50.3 2.1 %collective-permute-start.10 = (f32[512,128]{1,0:T(8,128)S(1)}, f32[512,128]{1,0:T(8,128)S(1)}, u32[]{:S(2)}, u32[]{:S(2)}) collective-permute-start(f32[512,128]{1,0:T(8,128)S(1)} %get-tuple-element.23.refs_2_), channel_id=1, source_target_pairs={{2,0},{3,1},{4,2},{5,3},{6,4},{7,5},{10,8},{11,9},{12,10},{13,11},... | collective-permute-start | bytes 786440 | tf_op jit(solution)/shard_map/ppermute | solution.py:228
  52.4 1.3 collective-permute-start.8
  54.7 1.3 collective-permute-start.13
  57.3 3.2 %collective-permute-done.8.refs_8_ = f32[512,128]{1,0:T(8,128)S(1)} collective-permute-done((f32[512,128]{1,0:T(8,128)S(1)}, f32[512,128]{1,0:T(8,128)S(1)}, u32[]{:S(2)}, u32[]{:S(2)}) %collective-permute-start.8) | collective-permute-done | bytes 262176 | tf_op jit(solution)/shard_map/ppermute | solution.py:227
  60.5 1.3 collective-permute-start.12
  62.8 4.1 %collective-permute-done.13.refs_13_ = f32[512,128]{1,0:T(8,128)S(1)} collective-permute-done((f32[512,128]{1,0:T(8,128)S(1)}, f32[512,128]{1,0:T(8,128)S(1)}, u32[]{:S(2)}, u32[]{:S(2)}) %collective-permute-start.13) | collective-permute-done | bytes 262176 | tf_op jit(solution)/shard_map/ppermute | solution.py:227
  66.9 1.3 collective-permute-start.17
  68.8 3.3 %collective-permute-done.12.refs_12_ = f32[512,128]{1,0:T(8,128)S(1)} collective-permute-done((f32[512,128]{1,0:T(8,128)S(1)}, f32[512,128]{1,0:T(8,128)S(1)}, u32[]{:S(2)}, u32[]{:S(2)}) %collective-permute-start.12) | collective-permute-done | bytes 262176 | tf_op jit(solution)/shard_map/ppermute | solution.py:227
  72.2 1.3 collective-permute-start.16
  73.5 4.3 %collective-permute-done.17.refs_17_ = f32[512,128]{1,0:T(8,128)S(1)} collective-permute-done((f32[512,128]{1,0:T(8,128)S(1)}, f32[512,128]{1,0:T(8,128)S(1)}, u32[]{:S(2)}, u32[]{:S(2)}) %collective-permute-start.17) | collective-permute-done | bytes 262176 | tf_op jit(solution)/shard_map/ppermute | solution.py:227
  77.8 5.6 %collective-permute-done.16.refs_16_ = f32[512,128]{1,0:T(8,128)S(1)} collective-permute-done((f32[512,128]{1,0:T(8,128)S(1)}, f32[512,128]{1,0:T(8,128)S(1)}, u32[]{:S(2)}, u32[]{:S(2)}) %collective-permute-start.16) | collective-permute-done | bytes 262176 | tf_op jit(solution)/shard_map/ppermute | solution.py:227
  83.4 4.0 %pair_products.1 = (f32[2,512,256]{2,1,0:T(8,128)S(1)}, f32[2,512,256]{2,1,0:T(8,128)S(1)}) custom-call(s32[3]{0:T(128)S(1)} %pad_add_fusion.me_ref.spot_ref, f32[512,128]{1,0:T(8,128)S(1)} %get-tuple-element.24.refs_0_, f32[512,128]{1,0:T(8,128)S(1)} %get-tuple-element.22.refs_1_, f32[512,128]{1,0:T(8,128)S(1)} %get-tuple-element.23.refs_2_, ...), custom_call_target="tpu_custom_call" | custom-call | tf_op jit(solution)/shard_map/pair_products/pallas_call | solution.py:241
  87.4 2.1 %collective-permute-start.20 = (f32[2,512,256]{2,1,0:T(8,128)S(1)}, f32[2,512,256]{2,1,0:T(8,128)S(1)}, u32[]{:S(2)}, u32[]{:S(2)}) collective-permute-start(f32[2,512,256]{2,1,0:T(8,128)S(1)} %get-tuple-element.16), channel_id=1, source_target_pairs={{0,8},{8,0},{16,24},{24,16},{1,9},{9,1},{17,25},{25,17},{2,10},{10... | collective-permute-start | bytes 3145736 | tf_op jit(solution)/shard_map/ppermute | solution.py:210
  89.6 2.3 %collective-permute-done.20 = f32[2,512,256]{2,1,0:T(8,128)S(1)} collective-permute-done((f32[2,512,256]{2,1,0:T(8,128)S(1)}, f32[2,512,256]{2,1,0:T(8,128)S(1)}, u32[]{:S(2)}, u32[]{:S(2)}) %collective-permute-start.20) | collective-permute-done | bytes 1048608 | tf_op jit(solution)/shard_map/ppermute | solution.py:210
  91.9 1.3 collective-permute-start.21
  93.2 11.9 %collective-permute-done.21 = f32[1,512,256]{2,1,0:T(8,128)S(1)} collective-permute-done((f32[1,512,256]{2,1,0:T(8,128)S(1)}, f32[1,512,256]{2,1,0:T(8,128)S(1)}, u32[]{:S(2)}, u32[]{:S(2)}) %collective-permute-start.21) | collective-permute-done | bytes 524320 | tf_op jit(solution)/shard_map/ppermute | solution.py:210
  105.2 1.9 %collective-permute-start.22 = (f32[512,256]{1,0:T(8,128)S(1)}, f32[512,256]{1,0:T(8,128)S(1)}, u32[]{:S(2)}, u32[]{:S(2)}) collective-permute-start(f32[512,256]{1,0:T(8,128)S(1)} %bitcast.8), channel_id=1, source_target_pairs={{0,0},{1,1},{2,8},{3,9},{4,16},{5,17},{6,24},{7,25},{8,2},{9,3},{1... | collective-permute-start | bytes 1572872 | tf_op jit(solution)/shard_map/ppermute | solution.py:254
  107.5 6.4 %collective-permute-done.23.refs_0_ = f32[256,256]{1,0:T(8,128)S(1)} collective-permute-done((f32[256,256]{1,0:T(8,128)S(1)}, f32[256,256]{1,0:T(8,128)S(1)}, u32[]{:S(2)}, u32[]{:S(2)}) %collective-permute-start.23) | collective-permute-done | bytes 262176 | tf_op jit(solution)/shard_map/ppermute | solution.py:266
  113.9 18.6 %collective-permute-done.22.direct_ref = f32[512,256]{1,0:T(8,128)S(1)} collective-permute-done((f32[512,256]{1,0:T(8,128)S(1)}, f32[512,256]{1,0:T(8,128)S(1)}, u32[]{:S(2)}, u32[]{:S(2)}) %collective-permute-start.22) | collective-permute-done | bytes 524320 | tf_op jit(solution)/shard_map/ppermute | solution.py:254
  132.5 1.5 %finish.1 = f32[512,256]{1,0:T(8,128)} custom-call(s32[3]{0:T(128)S(1)} %pad_add_fusion.me_ref.spot_ref, f32[512,256]{1,0:T(8,128)S(1)} %bitcast.9, f32[512,256]{1,0:T(8,128)S(1)} %collective-permute-done.22.direct_ref, f32[256,256]{1,0:T(8,128)S(1)} %collective-permute-done.23.refs_0_), custom_call_target="tpu_custom_call" | custom-call | tf_op jit(solution)/shard_map/finish/pallas_call | solution.py:267
  (32 shorter events, 6.6 us)
Async XLA Ops:
  1.6 3.4 %copy-start = (f32[8192,256]{1,0:T(8,128)S(1)}, f32[8192,256]{1,0:T(8,128)}, u32[]{:S(2)}) copy-start(f32[8192,256]{1,0:T(8,128)} %slab_ref.3) | copy-start | bytes 25165828
  15.0 10.8 %collective-permute-start.2 = (f32[2048,128]{1,0:T(8,128)S(1)}, f32[2048,128]{1,0:T(8,128)S(1)}, u32[]{:S(2)}, u32[]{:S(2)}) collective-permute-start(f32[2048,128]{1,0:T(8,128)S(1)} %get-tuple-element.14), channel_id=1, source_target_pairs={{0,8},{8,0},{16,24},{24,16},{1,9},{9,1},{17,25},{25,17},{2,10},{10... | collective-permute-start | bytes 3145736 | tf_op jit(solution)/shard_map/ppermute | solution.py:210
  25.7 2.7 %collective-permute-start = (f32[2048,128]{1,0:T(8,128)S(1)}, f32[2048,128]{1,0:T(8,128)S(1)}, u32[]{:S(2)}, u32[]{:S(2)}) collective-permute-start(f32[2048,128]{1,0:T(8,128)S(1)} %get-tuple-element.12), channel_id=1, source_target_pairs={{0,8},{8,0},{16,24},{24,16},{1,9},{9,1},{17,25},{25,17},{2,10},{10... | collective-permute-start | bytes 3145736 | tf_op jit(solution)/shard_map/ppermute | solution.py:210
  25.9 13.1 %collective-permute-start.3 = (f32[1024,128]{1,0:T(8,128)S(1)}, f32[1024,128]{1,0:T(8,128)S(1)}, u32[]{:S(2)}, u32[]{:S(2)}) collective-permute-start(f32[1024,128]{1,0:T(8,128)S(1)} %get-tuple-element.18), channel_id=1, source_target_pairs={{0,16},{8,24},{16,0},{24,8},{1,17},{9,25},{17,1},{25,9},{2,18},{10... | collective-permute-start | bytes 1572872 | tf_op jit(solution)/shard_map/ppermute | solution.py:210
  28.6 21.7 %collective-permute-start.1 = (f32[1024,128]{1,0:T(8,128)S(1)}, f32[1024,128]{1,0:T(8,128)S(1)}, u32[]{:S(2)}, u32[]{:S(2)}) collective-permute-start(f32[1024,128]{1,0:T(8,128)S(1)} %get-tuple-element.20), channel_id=1, source_target_pairs={{0,16},{8,24},{16,0},{24,8},{1,17},{9,25},{17,1},{25,9},{2,18},{10... | collective-permute-start | bytes 1572872 | tf_op jit(solution)/shard_map/ppermute | solution.py:210
  39.1 13.4 %collective-permute-start.11 = (f32[512,128]{1,0:T(8,128)S(1)}, f32[512,128]{1,0:T(8,128)S(1)}, u32[]{:S(2)}, u32[]{:S(2)}) collective-permute-start(f32[512,128]{1,0:T(8,128)S(1)} %get-tuple-element.21.refs_3_), channel_id=1, source_target_pairs={{2,0},{3,1},{4,2},{5,3},{6,4},{7,5},{10,8},{11,9},{12,10},{13,11},... | collective-permute-start | bytes 786440 | tf_op jit(solution)/shard_map/ppermute | solution.py:228
  41.2 12.5 %collective-permute-start.7 = (f32[512,128]{1,0:T(8,128)S(1)}, f32[512,128]{1,0:T(8,128)S(1)}, u32[]{:S(2)}, u32[]{:S(2)}) collective-permute-start(f32[512,128]{1,0:T(8,128)S(1)} %get-tuple-element.21.refs_3_), channel_id=1, source_target_pairs={{0,1},{1,0},{2,3},{3,2},{4,5},{5,4},{6,7},{7,6},{8,9},{9,8},{10,11... | collective-permute-start | bytes 786440 | tf_op jit(solution)/shard_map/ppermute | solution.py:234
  41.4 12.6 %collective-permute-start.9 = (f32[512,128]{1,0:T(8,128)S(1)}, f32[512,128]{1,0:T(8,128)S(1)}, u32[]{:S(2)}, u32[]{:S(2)}) collective-permute-start(f32[512,128]{1,0:T(8,128)S(1)} %get-tuple-element.22.refs_1_), channel_id=1, source_target_pairs={{0,2},{1,3},{2,4},{3,5},{4,6},{5,7},{8,10},{9,11},{10,12},{11,13},... | collective-permute-start | bytes 786440 | tf_op jit(solution)/shard_map/ppermute | solution.py:227
  42.7 11.9 %collective-permute-start.5 = (f32[512,128]{1,0:T(8,128)S(1)}, f32[512,128]{1,0:T(8,128)S(1)}, u32[]{:S(2)}, u32[]{:S(2)}) collective-permute-start(f32[512,128]{1,0:T(8,128)S(1)} %get-tuple-element.22.refs_1_), channel_id=1, source_target_pairs={{0,1},{1,0},{2,3},{3,2},{4,5},{5,4},{6,7},{7,6},{8,9},{9,8},{10,11... | collective-permute-start | bytes 786440 | tf_op jit(solution)/shard_map/ppermute | solution.py:234
  50.3 6.4 %collective-permute-start.10 = (f32[512,128]{1,0:T(8,128)S(1)}, f32[512,128]{1,0:T(8,128)S(1)}, u32[]{:S(2)}, u32[]{:S(2)}) collective-permute-start(f32[512,128]{1,0:T(8,128)S(1)} %get-tuple-element.23.refs_2_), channel_id=1, source_target_pairs={{2,0},{3,1},{4,2},{5,3},{6,4},{7,5},{10,8},{11,9},{12,10},{13,11},... | collective-permute-start | bytes 786440 | tf_op jit(solution)/shard_map/ppermute | solution.py:228
  52.4 8.1 %collective-permute-start.8 = (f32[512,128]{1,0:T(8,128)S(1)}, f32[512,128]{1,0:T(8,128)S(1)}, u32[]{:S(2)}, u32[]{:S(2)}) collective-permute-start(f32[512,128]{1,0:T(8,128)S(1)} %get-tuple-element.24.refs_0_), channel_id=1, source_target_pairs={{0,2},{1,3},{2,4},{3,5},{4,6},{5,7},{8,10},{9,11},{10,12},{11,13},... | collective-permute-start | bytes 786440 | tf_op jit(solution)/shard_map/ppermute | solution.py:227
  53.7 8.1 %collective-permute-start.6 = (f32[512,128]{1,0:T(8,128)S(1)}, f32[512,128]{1,0:T(8,128)S(1)}, u32[]{:S(2)}, u32[]{:S(2)}) collective-permute-start(f32[512,128]{1,0:T(8,128)S(1)} %get-tuple-element.23.refs_2_), channel_id=1, source_target_pairs={{0,1},{1,0},{2,3},{3,2},{4,5},{5,4},{6,7},{7,6},{8,9},{9,8},{10,11... | collective-permute-start | bytes 786440 | tf_op jit(solution)/shard_map/ppermute | solution.py:234
  54.0 8.1 %collective-permute-start.15 = (f32[512,128]{1,0:T(8,128)S(1)}, f32[512,128]{1,0:T(8,128)S(1)}, u32[]{:S(2)}, u32[]{:S(2)}) collective-permute-start(f32[512,128]{1,0:T(8,128)S(1)} %collective-permute-done.11.refs_11_), channel_id=1, source_target_pairs={{2,0},{3,1},{4,2},{5,3},{10,8},{11,9},{12,10},{13,11},{18,16},{19,... | collective-permute-start | bytes 786440 | tf_op jit(solution)/shard_map/ppermute | solution.py:228
  54.7 12.2 %collective-permute-start.13 = (f32[512,128]{1,0:T(8,128)S(1)}, f32[512,128]{1,0:T(8,128)S(1)}, u32[]{:S(2)}, u32[]{:S(2)}) collective-permute-start(f32[512,128]{1,0:T(8,128)S(1)} %collective-permute-done.9.refs_9_), channel_id=1, source_target_pairs={{2,4},{3,5},{4,6},{5,7},{10,12},{11,13},{12,14},{13,15},{18,20},{1... | collective-permute-start | bytes 786440 | tf_op jit(solution)/shard_map/ppermute | solution.py:227
  56.6 11.5 %collective-permute-start.14 = (f32[512,128]{1,0:T(8,128)S(1)}, f32[512,128]{1,0:T(8,128)S(1)}, u32[]{:S(2)}, u32[]{:S(2)}) collective-permute-start(f32[512,128]{1,0:T(8,128)S(1)} %collective-permute-done.10.refs_10_), channel_id=1, source_target_pairs={{2,0},{3,1},{4,2},{5,3},{10,8},{11,9},{12,10},{13,11},{18,16},{19,... | collective-permute-start | bytes 786440 | tf_op jit(solution)/shard_map/ppermute | solution.py:228
  60.5 11.7 %collective-permute-start.12 = (f32[512,128]{1,0:T(8,128)S(1)}, f32[512,128]{1,0:T(8,128)S(1)}, u32[]{:S(2)}, u32[]{:S(2)}) collective-permute-start(f32[512,128]{1,0:T(8,128)S(1)} %collective-permute-done.8.refs_8_), channel_id=1, source_target_pairs={{2,4},{3,5},{4,6},{5,7},{10,12},{11,13},{12,14},{13,15},{18,20},{1... | collective-permute-start | bytes 786440 | tf_op jit(solution)/shard_map/ppermute | solution.py:227
  61.8 11.7 %collective-permute-start.4 = (f32[512,128]{1,0:T(8,128)S(1)}, f32[512,128]{1,0:T(8,128)S(1)}, u32[]{:S(2)}, u32[]{:S(2)}) collective-permute-start(f32[512,128]{1,0:T(8,128)S(1)} %get-tuple-element.24.refs_0_), channel_id=1, source_target_pairs={{0,1},{1,0},{2,3},{3,2},{4,5},{5,4},{6,7},{7,6},{8,9},{9,8},{10,11... | collective-permute-start | bytes 786440 | tf_op jit(solution)/shard_map/ppermute | solution.py:234
  62.1 11.4 %collective-permute-start.19 = (f32[512,128]{1,0:T(8,128)S(1)}, f32[512,128]{1,0:T(8,128)S(1)}, u32[]{:S(2)}, u32[]{:S(2)}) collective-permute-start(f32[512,128]{1,0:T(8,128)S(1)} %collective-permute-done.15.refs_15_), channel_id=1, source_target_pairs={{2,0},{3,1},{10,8},{11,9},{18,16},{19,17},{26,24},{27,25}} | collective-permute-start | bytes 786440 | tf_op jit(solution)/shard_map/ppermute | solution.py:228
  66.9 10.9 %collective-permute-start.17 = (f32[512,128]{1,0:T(8,128)S(1)}, f32[512,128]{1,0:T(8,128)S(1)}, u32[]{:S(2)}, u32[]{:S(2)}) collective-permute-start(f32[512,128]{1,0:T(8,128)S(1)} %collective-permute-done.13.refs_13_), channel_id=1, source_target_pairs={{4,6},{5,7},{12,14},{13,15},{20,22},{21,23},{28,30},{29,31}} | collective-permute-start | bytes 786440 | tf_op jit(solution)/shard_map/ppermute | solution.py:227
  68.2 9.7 %collective-permute-start.18 = (f32[512,128]{1,0:T(8,128)S(1)}, f32[512,128]{1,0:T(8,128)S(1)}, u32[]{:S(2)}, u32[]{:S(2)}) collective-permute-start(f32[512,128]{1,0:T(8,128)S(1)} %collective-permute-done.14.refs_14_), channel_id=1, source_target_pairs={{2,0},{3,1},{10,8},{11,9},{18,16},{19,17},{26,24},{27,25}} | collective-permute-start | bytes 786440 | tf_op jit(solution)/shard_map/ppermute | solution.py:228
  72.2 11.2 %collective-permute-start.16 = (f32[512,128]{1,0:T(8,128)S(1)}, f32[512,128]{1,0:T(8,128)S(1)}, u32[]{:S(2)}, u32[]{:S(2)}) collective-permute-start(f32[512,128]{1,0:T(8,128)S(1)} %collective-permute-done.12.refs_12_), channel_id=1, source_target_pairs={{4,6},{5,7},{12,14},{13,15},{20,22},{21,23},{28,30},{29,31}} | collective-permute-start | bytes 786440 | tf_op jit(solution)/shard_map/ppermute | solution.py:227
  87.4 4.4 %collective-permute-start.20 = (f32[2,512,256]{2,1,0:T(8,128)S(1)}, f32[2,512,256]{2,1,0:T(8,128)S(1)}, u32[]{:S(2)}, u32[]{:S(2)}) collective-permute-start(f32[2,512,256]{2,1,0:T(8,128)S(1)} %get-tuple-element.16), channel_id=1, source_target_pairs={{0,8},{8,0},{16,24},{24,16},{1,9},{9,1},{17,25},{25,17},{2,10},{10... | collective-permute-start | bytes 3145736 | tf_op jit(solution)/shard_map/ppermute | solution.py:210
  91.9 13.2 %collective-permute-start.21 = (f32[1,512,256]{2,1,0:T(8,128)S(1)}, f32[1,512,256]{2,1,0:T(8,128)S(1)}, u32[]{:S(2)}, u32[]{:S(2)}) collective-permute-start(f32[1,512,256]{2,1,0:T(8,128)S(1)} %slice_add_fusion), channel_id=1, source_target_pairs={{0,16},{8,24},{16,0},{24,8},{1,17},{9,25},{17,1},{25,9},{2,18},{10... | collective-permute-start | bytes 1572872 | tf_op jit(solution)/shard_map/ppermute | solution.py:210
  105.2 27.2 %collective-permute-start.22 = (f32[512,256]{1,0:T(8,128)S(1)}, f32[512,256]{1,0:T(8,128)S(1)}, u32[]{:S(2)}, u32[]{:S(2)}) collective-permute-start(f32[512,256]{1,0:T(8,128)S(1)} %bitcast.8), channel_id=1, source_target_pairs={{0,0},{1,1},{2,8},{3,9},{4,16},{5,17},{6,24},{7,25},{8,2},{9,3},{1... | collective-permute-start | bytes 1572872 | tf_op jit(solution)/shard_map/ppermute | solution.py:254
  107.2 6.7 %collective-permute-start.23 = (f32[256,256]{1,0:T(8,128)S(1)}, f32[256,256]{1,0:T(8,128)S(1)}, u32[]{:S(2)}, u32[]{:S(2)}) collective-permute-start(f32[256,256]{1,0:T(8,128)S(1)} %dynamic-slice_bitcast_fusion), channel_id=1, source_target_pairs={{0,1},{1,0},{2,3},{3,2},{4,5},{5,4},{6,7},{7,6},{8,9},{9,8},{10,11... | collective-permute-start | bytes 786440 | tf_op jit(solution)/shard_map/ppermute | solution.py:266

commit v3 on v1

v3 whole, which is shorter than its diff:
```python
import functools

import jax
import jax.numpy as jnp
from jax import lax
from jax.experimental import pallas as pl
from jax.experimental.pallas import tpu as pltpu
from jax.sharding import PartitionSpec as P

LANES = 128
INNER = 128
AXES = ("rows", "cols")


def bit_reverse(value, bits):
    return sum(((value >> at) & 1) << (bits - 1 - at) for at in range(bits))


def butterflies(parts):
    stride = 1
    while stride < len(parts):
        for at in range(len(parts)):
            if not at & stride:
                low, high = parts[at], parts[at + stride]
                parts[at], parts[at + stride] = low + high, low - high
        stride *= 2
    return parts


def transform_and_pick(groups, strip, spot_ref, index_ref, bits_ref, slab_ref, keep_ref, send_ref, mixed, arrived):
    height = slab_ref.shape[0]
    steps = arrived.shape[0]
    block = height // steps
    inner_blocks = block // INNER

    def fetch(step):
        rows = pl.ds(pl.multiple_of(step * block, block), block)
        return pltpu.make_async_copy(
            slab_ref.at[rows, pl.ds(strip * LANES, LANES)], mixed.at[rows, :], arrived.at[step]
        )

    for step in range(steps):
        fetch(step).start()

    row = lax.broadcasted_iota(jnp.int32, (INNER, 2 * INNER), 0)
    col = lax.broadcasted_iota(jnp.int32, (INNER, 2 * INNER), 1) & (INNER - 1)
    common = row & col
    for shift in (4, 2, 1):
        common = common ^ (common >> shift)
    table = (1 - 2 * (common & 1)).astype(jnp.float32)

    def combine(starts, negate):
        parts = butterflies([mixed[pl.ds(pl.multiple_of(s, 8), 8), :] for s in starts])
        for s, part in zip(starts, parts):
            mixed[pl.ds(pl.multiple_of(s, 8), 8), :] = part
            if negate:
                mixed[pl.ds(pl.multiple_of(s + height, 8), 8), :] = -part

    @pl.loop(0, steps)
    def _(step):
        base = step * block
        fetch(step).wait()
        flips = (1 - 2 * bits_ref[step]).astype(jnp.float32)
        for at in range(inner_blocks):
            rows = pl.ds(pl.multiple_of(base + at * INNER, INNER), INNER)
            flip = flips[at : at + 1, :]
            signed = (table * jnp.concatenate([flip, flip], axis=1)).astype(jnp.bfloat16)
            mixed[rows, :] = jnp.dot(
                signed, jnp.concatenate(two_parts(mixed[rows, :]), axis=0), preferred_element_type=jnp.float32
            )

        @pl.loop(0, INNER // 8, unroll=4)
        def _(tile):
            combine([base + at * INNER + tile * 8 for at in range(inner_blocks)], False)

    @pl.loop(0, block // 8, unroll=4)
    def _(tile):
        combine([at * block + tile * 8 for at in range(steps)], True)

    count = index_ref.shape[0] // groups
    bits = groups.bit_length() - 1
    half = groups // 2
    for place in range(groups):
        out = keep_ref if place < half else send_ref
        start = (spot_ref[0] ^ bit_reverse(place, bits)) * count
        to = (place % half) * count

        @pl.loop(0, count // 32)
        def _(chunk):
            for at in range(32):
                source = index_ref[start + chunk * 32 + at]
                out[pl.ds(to + chunk * 32 + at, 1), :] = mixed[pl.ds(source, 1), :]


VMEM = pl.BlockSpec(memory_space=pltpu.VMEM)
SMEM = pl.BlockSpec(memory_space=pltpu.SMEM)
MIB = 1024 * 1024


def picked_strip(slab, sign_bits, index, spot, groups, strip):
    height = slab.shape[0]
    samples = index.shape[0]
    steps = sign_bits.shape[0]
    half = jax.ShapeDtypeStruct((samples // 2, LANES), jnp.float32)
    return pl.pallas_call(
        functools.partial(transform_and_pick, groups, strip),
        out_shape=(half, half),
        in_specs=[SMEM, SMEM, VMEM, pl.BlockSpec(memory_space=pl.ANY)],
        out_specs=(VMEM, VMEM),
        scratch_shapes=[pltpu.VMEM((2 * height, LANES), jnp.float32), pltpu.SemaphoreType.DMA((steps,))],
        compiler_params=pltpu.CompilerParams(vmem_limit_bytes=56 * MIB),
        cost_estimate=pl.CostEstimate(
            flops=16 * height * INNER * LANES, bytes_accessed=16 * LANES * (height + samples), transcendentals=0
        ),
        name="transform_and_pick",
    )(spot, index, sign_bits, slab)


def two_parts(values):
    high = values.astype(jnp.bfloat16)
    return high, (values - high.astype(jnp.float32)).astype(jnp.bfloat16)


def three_products(left, right):
    dot = functools.partial(jnp.dot, preferred_element_type=jnp.float32)
    return dot(left[0], right[0]) + dot(left[0], right[1]) + dot(left[1], right[0])


def turn_plane(near, strips, spot_ref, *refs):
    parts, (high_ref, low_ref, own_ref) = refs[:-3], refs[-3:]
    width = own_ref.shape[1]
    for off in range(near):
        for strip in range(strips):
            high, low = two_parts(parts[off * strips + strip][...].T)
            where = pl.ds(pl.multiple_of((spot_ref[2] ^ off) * width + strip * LANES, LANES), LANES)
            high_ref[where, :] = high
            low_ref[where, :] = low
    own = jnp.concatenate([part[...] for part in parts[:strips]], axis=1)
    own_ref[...] = three_products((high_ref[...], low_ref[...]), two_parts(own))


def pair_products(groups, strip, spot_ref, high_ref, low_ref, own_ref, *refs):
    remote, (keep_ref, send_ref) = refs[:-2], refs[-2:]
    me, at_plane = spot_ref[0], spot_ref[1]
    half = keep_ref.shape[0]
    bits = groups.bit_length() - 1
    back = 1 - 2 * (me & 1)

    def store(other, value):
        place = bit_reverse(other ^ me, bits)

        @pl.when(place < half)
        def _():
            keep_ref[place] = value()

        @pl.when(place >= half)
        def _():
            send_ref[place - half] = value()

    store(at_plane, lambda: own_ref[:, strip * LANES : (strip + 1) * LANES])
    for away in range(1, groups):
        below, above = at_plane - away * back, at_plane + away * back

        @pl.when((below >= 0) & (below < groups))
        def _():
            product = three_products((high_ref[...], low_ref[...]), two_parts(remote[away - 1][...]))
            store(below, lambda: product)

        @pl.when((above >= 0) & (above < groups))
        def _():
            store(above, lambda: jnp.zeros(keep_ref.shape[1:], jnp.float32))


def finish(factor, near, strips, spot_ref, *refs):
    totals, directs, turned, out_ref = refs[:strips], refs[strips : 2 * strips], refs[2 * strips : -1], refs[-1]
    me, at_plane, at_near = spot_ref[0], spot_ref[1], spot_ref[2]
    width = out_ref.shape[1]

    @pl.when(me == at_plane)
    def _():
        for strip in range(strips):
            out_ref[:, strip * LANES : (strip + 1) * LANES] = totals[strip][...] * factor

    @pl.when(me != at_plane)
    def _():
        direct = jnp.concatenate([part[...] for part in directs], axis=1) * factor
        out_ref[...] = direct
        for off in range(near):
            start = pl.multiple_of((at_near ^ off) * width, width)
            for strip in range(strips):
                part = totals[strip][pl.ds(start, width), :] if off == 0 else turned[(off - 1) * strips + strip][...]
                rows = pl.ds(pl.multiple_of(start + strip * LANES, LANES), LANES)
                out_ref[rows, :] = out_ref[rows, :] + part.T * factor


def shards(slab, sign_bits, sample_rows):
    height, width = slab.shape
    groups, columns = lax.axis_size("rows"), lax.axis_size("cols")
    near = columns // groups
    strips = width // LANES
    me, column = lax.axis_index("rows"), lax.axis_index("cols")
    samples = sample_rows.shape[0]
    factor = 1.0 / (samples * height * groups)
    bits = groups.bit_length() - 1

    owners = sample_rows // height
    common = owners & me
    parity = jnp.zeros_like(common)
    for at in range(bits):
        parity = parity ^ ((common >> at) & 1)
    index = sample_rows - owners * height + parity * height
    block = min(1024, height)
    sign_bits = sign_bits.reshape(height // block, block // INNER, INNER)
    spot = jnp.stack([me, column // near, column % near]).astype(jnp.int32)

    def halve(keep, send, at):
        got = lax.ppermute(send, "rows", [(r, r ^ (1 << at)) for r in range(groups)])
        half = keep.shape[0] // 2
        if at == bits - 1:
            return keep, got
        return keep[:half] + got[:half], keep[half:] + got[half:]

    def onward(r, c):
        to = c + near if r % 2 == 0 else c - near
        return (r, to) if 0 <= to < columns else (r ^ 1, c)

    def pairs(to):
        ends = [(r, c, *to(r, c)) for r in range(groups) for c in range(columns)]
        return [(r * columns + c, r_to * columns + c_to) for r, c, r_to, c_to in ends]

    ring = pairs(onward)
    mirror = pairs(lambda r, c: (c // near, r * near + c % near))

    plane = [[] for _ in range(near)]
    remote = []
    for strip in range(strips):
        keep, send = picked_strip(slab, sign_bits, index, spot, groups, strip)
        for at in range(bits):
            keep, send = halve(keep, send, at)
            if at == 0:
                index, send = lax.optimization_barrier((index, send))
        own = keep + send
        moving, passed = own, []
        for away in range(1, groups):
            moving = lax.ppermute(moving, AXES, ring)
            passed.append(moving)
        remote.append(passed)
        plane[0].append(own)
        for off in range(1, near):
            plane[off].append(lax.ppermute(own, "cols", [(c, c ^ off) for c in range(columns)]))

    parts = [part for side in plane for part in side]
    depth = samples // groups
    turned = jax.ShapeDtypeStruct((near * width, depth), jnp.bfloat16)
    high, low, own_sums = pl.pallas_call(
        functools.partial(turn_plane, near, strips),
        out_shape=(turned, turned, jax.ShapeDtypeStruct((near * width, width), jnp.float32)),
        in_specs=[SMEM] + [VMEM] * len(parts),
        out_specs=(VMEM,) * 3,
        compiler_params=pltpu.CompilerParams(vmem_limit_bytes=32 * MIB),
        name="turn_plane",
    )(spot, *parts)

    half_sums = jax.ShapeDtypeStruct((groups // 2, near * width, LANES), jnp.float32)
    totals, directs, sideways = [], [], [[] for _ in range(1, near)]
    for strip in range(strips):
        keep, send = pl.pallas_call(
            functools.partial(pair_products, groups, strip),
            out_shape=(half_sums, half_sums),
            in_specs=[SMEM] + [VMEM] * (3 + len(remote[strip])),
            out_specs=(VMEM, VMEM),
            compiler_params=pltpu.CompilerParams(vmem_limit_bytes=32 * MIB),
            name="pair_products",
        )(spot, high, low, own_sums, *remote[strip])
        for at in range(bits):
            keep, send = halve(keep, send, at)
        total = (keep + send)[0]
        totals.append(total)
        directs.append(lax.ppermute(total, AXES, mirror))
        for off in range(1, near):
            part = lax.dynamic_slice_in_dim(total, (column % near ^ off) * width, width, 0)
            sideways[off - 1].append(lax.ppermute(part, "cols", [(c, c ^ off) for c in range(columns)]))

    last = totals + directs + [part for side in sideways for part in side]
    return pl.pallas_call(
        functools.partial(finish, factor, near, strips),
        out_shape=jax.ShapeDtypeStruct((near * width, width), jnp.float32),
        in_specs=[SMEM] + [VMEM] * len(last),
        out_specs=VMEM,
        compiler_params=pltpu.CompilerParams(vmem_limit_bytes=16 * MIB),
        name="finish",
    )(spot, *last)


def solution(mesh):
    return jax.shard_map(
        shards,
        mesh=mesh,
        in_specs=(P("rows", "cols"), P("rows"), P()),
        out_specs=P("rows", "cols"),
        check_vma=False,
    )
```

time: 234 us -> 136 us (0.58)
  the two profiles are of different devices: /device:TPU:18 before, /device:TPU:6 now
where the time goes in v3:
time: 136 us; the launch traced here: 135 us
  waiting for transfers between devices  70.8 us (52%)
  starting transfers between devices  31.5 us (23%)
  Pallas kernels  27.5 us (20%)
  other arithmetic  5.55 us (4%)
    ppermute x8, waiting for transfers between devices, halve(): got = lax.ppermute(send, 'rows', [(r, r ^ 1 << at) for r in range(groups)])  32.7 us
    pallas_call x2, Pallas kernels, picked_strip(): pl.pallas_call(functools.partial(transform_and_pick, groups, strip), out_...  22.5 us
    ppermute x2, waiting for transfers between devices, shards(): directs.append(lax.ppermute(total, AXES, mirror))  13.9 us
    ppermute x6, starting transfers between devices, shards(): moving = lax.ppermute(moving, AXES, ring)  12.2 us
    ppermute x2, waiting for transfers between devices, shards(): lax.ppermute(own, 'cols', [(c, c ^ off) for c in range(columns)])  11.9 us
    ppermute x6, waiting for transfers between devices, shards(): moving = lax.ppermute(moving, AXES, ring)  9.37 us
    ppermute x2, starting transfers between devices, shards(): directs.append(lax.ppermute(total, AXES, mirror))  8.87 us
    ppermute x8, starting transfers between devices, halve(): got = lax.ppermute(send, 'rows', [(r, r ^ 1 << at) for r in range(groups)])  6.2 us
  transfers between devices with their start and end apart: 20, of which 15 were waited for; matrix products, arithmetic and copies ran while one was open for 2% of the time, Pallas kernels for 3%

profile of v3, /device:TPU:6, one launch (start us, length us, event | category | flops | bytes accessed | tf_op | source)
XLA Modules:
  0.0 135.5 jit_solution(16982367932002781953)
XLA Ops:
  0.0 1.3 multiply_add_fusion.index_ref
  1.9 11.2 %transform_and_pick.2 = (f32[2048,128]{1,0:T(8,128)}, f32[2048,128]{1,0:T(8,128)}) custom-call(s32[3]{0:T(128)} %pad_add_fusion.spot_ref, s32[4096]{0:T(1024)} %multiply_add_fusion.index_ref, s32[8,8,128]{2,1,0:T(8,128)} %bitcast.14, f32[8192,256]{1,0:T(8,128)} %slab_ref.3), custom_call_target="tpu_custom_call" | custom-call | flops 2147483648 | bytes 25165824 | tf_op jit(solution)/shard_map/transform_and_pick/pallas_call | solution.py:105
  13.3 2.9 %collective-permute-done = f32[2048,128]{1,0:T(8,128)S(1)} collective-permute-done((f32[2048,128]{1,0:T(8,128)}, f32[2048,128]{1,0:T(8,128)S(1)}, u32[]{:S(2)}, u32[]{:S(2)}) %collective-permute-start) | collective-permute-done | bytes 1048608 | tf_op jit(solution)/shard_map/ppermute | solution.py:217
  16.1 1.1 slice_add_fusion.2
  17.2 11.2 %transform_and_pick.3 = (f32[2048,128]{1,0:T(8,128)}, f32[2048,128]{1,0:T(8,128)}) custom-call(s32[3]{0:T(128)} %pad_add_fusion.spot_ref, s32[4096]{0:T(1024)} %multiply_add_fusion.index_ref, s32[8,8,128]{2,1,0:T(8,128)} %bitcast.15, f32[8192,256]{1,0:T(8,128)} %slab_ref.3), custom_call_target="tpu_custom_call" | custom-call | flops 2147483648 | bytes 25165824 | tf_op jit(solution)/shard_map/transform_and_pick/pallas_call | solution.py:105
  29.2 2.2 %collective-permute-done.2 = f32[2048,128]{1,0:T(8,128)S(1)} collective-permute-done((f32[2048,128]{1,0:T(8,128)}, f32[2048,128]{1,0:T(8,128)S(1)}, u32[]{:S(2)}, u32[]{:S(2)}) %collective-permute-start.2) | collective-permute-done | bytes 1048608 | tf_op jit(solution)/shard_map/ppermute | solution.py:217
  31.4 1.1 slice_add_fusion
  33.1 10.3 %collective-permute-done.1 = f32[1024,128]{1,0:T(8,128)S(1)} collective-permute-done((f32[1024,128]{1,0:T(8,128)S(1)}, f32[1024,128]{1,0:T(8,128)S(1)}, u32[]{:S(2)}, u32[]{:S(2)}) %collective-permute-start.1) | collective-permute-done | bytes 524320 | tf_op jit(solution)/shard_map/ppermute | solution.py:217
  43.5 1.6 %collective-permute-start.6 = (f32[1024,128]{1,0:T(8,128)S(1)}, f32[1024,128]{1,0:T(8,128)S(1)}, u32[]{:S(2)}, u32[]{:S(2)}) collective-permute-start(f32[1024,128]{1,0:T(8,128)S(1)} %fusion.1.refs_0_), channel_id=1, source_target_pairs={{0,2},{1,3},{2,4},{3,5},{4,6},{5,7},{6,14},{7,15},{8,0},{9,1},{10,... | collective-permute-start | bytes 1572872 | tf_op jit(solution)/shard_map/ppermute | solution.py:245
  45.1 9.0 %collective-permute-done.3 = f32[1024,128]{1,0:T(8,128)S(1)} collective-permute-done((f32[1024,128]{1,0:T(8,128)S(1)}, f32[1024,128]{1,0:T(8,128)S(1)}, u32[]{:S(2)}, u32[]{:S(2)}) %collective-permute-start.3) | collective-permute-done | bytes 524320 | tf_op jit(solution)/shard_map/ppermute | solution.py:217
  54.1 1.1 fusion.refs_1_
  55.2 1.6 %collective-permute-start.11 = (f32[1024,128]{1,0:T(8,128)S(1)}, f32[1024,128]{1,0:T(8,128)S(1)}, u32[]{:S(2)}, u32[]{:S(2)}) collective-permute-start(f32[1024,128]{1,0:T(8,128)S(1)} %fusion.refs_1_), channel_id=1, source_target_pairs={{0,2},{1,3},{2,4},{3,5},{4,6},{5,7},{6,14},{7,15},{8,0},{9,1},{10,... | collective-permute-start | bytes 1572872 | tf_op jit(solution)/shard_map/ppermute | solution.py:245
  56.9 1.6 %collective-permute-start.7 = (f32[1024,128]{1,0:T(8,128)S(1)}, f32[1024,128]{1,0:T(8,128)S(1)}, u32[]{:S(2)}, u32[]{:S(2)}) collective-permute-start(f32[1024,128]{1,0:T(8,128)S(1)} %collective-permute-done.6.refs_0_), channel_id=1, source_target_pairs={{0,2},{1,3},{2,4},{3,5},{4,6},{5,7},{6,14},{7,15},{8,0},{9,1},{10,... | collective-permute-start | bytes 1572872 | tf_op jit(solution)/shard_map/ppermute | solution.py:245
  58.4 5.1 %collective-permute-done.11.refs_0_ = f32[1024,128]{1,0:T(8,128)S(1)} collective-permute-done((f32[1024,128]{1,0:T(8,128)S(1)}, f32[1024,128]{1,0:T(8,128)S(1)}, u32[]{:S(2)}, u32[]{:S(2)}) %collective-permute-start.11) | collective-permute-done | bytes 524320 | tf_op jit(solution)/shard_map/ppermute | solution.py:245
  63.5 2.5 %collective-permute-start.12 = (f32[1024,128]{1,0:T(8,128)S(1)}, f32[1024,128]{1,0:T(8,128)S(1)}, u32[]{:S(2)}, u32[]{:S(2)}) collective-permute-start(f32[1024,128]{1,0:T(8,128)S(1)} %collective-permute-done.11.refs_0_), channel_id=1, source_target_pairs={{0,2},{1,3},{2,4},{3,5},{4,6},{5,7},{6,14},{7,15},{8,0},{9,1},{10,... | collective-permute-start | bytes 1572872 | tf_op jit(solution)/shard_map/ppermute | solution.py:245
  66.5 1.5 %collective-permute-start.5 = (f32[1024,128]{1,0:T(8,128)S(1)}, f32[1024,128]{1,0:T(8,128)S(1)}, u32[]{:S(2)}, u32[]{:S(2)}) collective-permute-start(f32[1024,128]{1,0:T(8,128)S(1)} %fusion.refs_1_), channel_id=1, source_target_pairs={{0,1},{1,0},{2,3},{3,2},{4,5},{5,4},{6,7},{7,6},{8,9},{9,8},{10,11... | collective-permute-start | bytes 1572872 | tf_op jit(solution)/shard_map/ppermute | solution.py:250
  68.1 1.1 collective-permute-done.7.refs_1_
  69.2 2.5 %collective-permute-start.8 = (f32[1024,128]{1,0:T(8,128)S(1)}, f32[1024,128]{1,0:T(8,128)S(1)}, u32[]{:S(2)}, u32[]{:S(2)}) collective-permute-start(f32[1024,128]{1,0:T(8,128)S(1)} %collective-permute-done.7.refs_1_), channel_id=1, source_target_pairs={{0,2},{1,3},{2,4},{3,5},{4,6},{5,7},{6,14},{7,15},{8,0},{9,1},{10,... | collective-permute-start | bytes 1572872 | tf_op jit(solution)/shard_map/ppermute | solution.py:245
  71.6 3.1 %collective-permute-done.12.refs_1_ = f32[1024,128]{1,0:T(8,128)S(1)} collective-permute-done((f32[1024,128]{1,0:T(8,128)S(1)}, f32[1024,128]{1,0:T(8,128)S(1)}, u32[]{:S(2)}, u32[]{:S(2)}) %collective-permute-start.12) | collective-permute-done | bytes 524320 | tf_op jit(solution)/shard_map/ppermute | solution.py:245
  74.8 2.5 %collective-permute-start.13 = (f32[1024,128]{1,0:T(8,128)S(1)}, f32[1024,128]{1,0:T(8,128)S(1)}, u32[]{:S(2)}, u32[]{:S(2)}) collective-permute-start(f32[1024,128]{1,0:T(8,128)S(1)} %collective-permute-done.12.refs_1_), channel_id=1, source_target_pairs={{0,2},{1,3},{2,4},{3,5},{4,6},{5,7},{6,14},{7,15},{8,0},{9,1},{10,... | collective-permute-start | bytes 1572872 | tf_op jit(solution)/shard_map/ppermute | solution.py:245
  77.3 3.6 %collective-permute-done.4.refs_2_ = f32[1024,128]{1,0:T(8,128)S(1)} collective-permute-done((f32[1024,128]{1,0:T(8,128)S(1)}, f32[1024,128]{1,0:T(8,128)S(1)}, u32[]{:S(2)}, u32[]{:S(2)}) %collective-permute-start.4) | collective-permute-done | bytes 524320 | tf_op jit(solution)/shard_map/ppermute | solution.py:250
  80.9 8.2 %collective-permute-done.5.refs_3_ = f32[1024,128]{1,0:T(8,128)S(1)} collective-permute-done((f32[1024,128]{1,0:T(8,128)S(1)}, f32[1024,128]{1,0:T(8,128)S(1)}, u32[]{:S(2)}, u32[]{:S(2)}) %collective-permute-start.5) | collective-permute-done | bytes 524320 | tf_op jit(solution)/shard_map/ppermute | solution.py:250
  89.1 2.1 %turn_plane.1 = (bf16[512,1024]{1,0:T(8,128)(2,1)S(1)}, bf16[512,1024]{1,0:T(8,128)(2,1)S(1)}, f32[512,256]{1,0:T(8,128)S(1)}) custom-call(s32[3]{0:T(128)S(1)} %copy-done, f32[1024,128]{1,0:T(8,128)S(1)} %fusion.1.refs_0_, f32[1024,128]{1,0:T(8,128)S(1)} %fusion.refs_1_, f32[1024,128]{1,0:T(8,128)S(1)} %collective-permute-done.4.refs_2_, ...), custom_call_target="tpu_custom_call" | custom-call | tf_op jit(solution)/shard_map/turn_plane/pallas_call | solution.py:255
  92.7 3.4 %collective-permute-start.14 = (f32[2,512,128]{2,1,0:T(8,128)S(1)}, f32[2,512,128]{2,1,0:T(8,128)S(1)}, u32[]{:S(2)}, u32[]{:S(2)}) collective-permute-start(f32[2,512,128]{2,1,0:T(8,128)S(1)} %get-tuple-element.32), channel_id=1, source_target_pairs={{0,8},{8,0},{16,24},{24,16},{1,9},{9,1},{17,25},{25,17},{2,10},{10... | collective-permute-start | bytes 1572872 | tf_op jit(solution)/shard_map/ppermute | solution.py:217
  98.4 7.0 %collective-permute-done.10 = f32[1,512,128]{2,1,0:T(8,128)S(1)} collective-permute-done((f32[1,512,128]{2,1,0:T(8,128)S(1)}, f32[1,512,128]{2,1,0:T(8,128)S(1)}, u32[]{:S(2)}, u32[]{:S(2)}) %collective-permute-start.10) | collective-permute-done | bytes 262176 | tf_op jit(solution)/shard_map/ppermute | solution.py:217
  105.5 4.2 %collective-permute-start.16 = (f32[512,128]{1,0:T(8,128)S(1)}, f32[512,128]{1,0:T(8,128)S(1)}, u32[]{:S(2)}, u32[]{:S(2)}) collective-permute-start(f32[512,128]{1,0:T(8,128)S(1)} %bitcast.10), channel_id=1, source_target_pairs={{0,0},{1,1},{2,8},{3,9},{4,16},{5,17},{6,24},{7,25},{8,2},{9,3},{1... | collective-permute-start | bytes 786440 | tf_op jit(solution)/shard_map/ppermute | solution.py:279
  110.2 4.7 %collective-permute-start.17 = (f32[512,128]{1,0:T(8,128)S(1)}, f32[512,128]{1,0:T(8,128)S(1)}, u32[]{:S(2)}, u32[]{:S(2)}) collective-permute-start(f32[512,128]{1,0:T(8,128)S(1)} %bitcast.12), channel_id=1, source_target_pairs={{0,0},{1,1},{2,8},{3,9},{4,16},{5,17},{6,24},{7,25},{8,2},{9,3},{1... | collective-permute-start | bytes 786440 | tf_op jit(solution)/shard_map/ppermute | solution.py:279
  115.5 1.6 %collective-permute-start.19 = (f32[256,128]{1,0:T(8,128)S(1)}, f32[256,128]{1,0:T(8,128)S(1)}, u32[]{:S(2)}, u32[]{:S(2)}) collective-permute-start(f32[256,128]{1,0:T(8,128)S(1)} %dynamic-slice_bitcast_fusion), channel_id=1, source_target_pairs={{0,1},{1,0},{2,3},{3,2},{4,5},{5,4},{6,7},{7,6},{8,9},{9,8},{10,11... | collective-permute-start | bytes 393224 | tf_op jit(solution)/shard_map/ppermute | solution.py:282
  117.1 2.9 %collective-permute-done.18.refs_4_ = f32[256,128]{1,0:T(8,128)S(1)} collective-permute-done((f32[256,128]{1,0:T(8,128)S(1)}, f32[256,128]{1,0:T(8,128)S(1)}, u32[]{:S(2)}, u32[]{:S(2)}) %collective-permute-start.18) | collective-permute-done | bytes 131104 | tf_op jit(solution)/shard_map/ppermute | solution.py:282
  119.9 9.7 %collective-permute-done.16.refs_2_ = f32[512,128]{1,0:T(8,128)S(1)} collective-permute-done((f32[512,128]{1,0:T(8,128)S(1)}, f32[512,128]{1,0:T(8,128)S(1)}, u32[]{:S(2)}, u32[]{:S(2)}) %collective-permute-start.16) | collective-permute-done | bytes 262176 | tf_op jit(solution)/shard_map/ppermute | solution.py:279
  129.7 4.2 %collective-permute-done.17.refs_3_ = f32[512,128]{1,0:T(8,128)S(1)} collective-permute-done((f32[512,128]{1,0:T(8,128)S(1)}, f32[512,128]{1,0:T(8,128)S(1)}, u32[]{:S(2)}, u32[]{:S(2)}) %collective-permute-start.17) | collective-permute-done | bytes 262176 | tf_op jit(solution)/shard_map/ppermute | solution.py:279
  133.9 1.6 %finish.1 = f32[512,256]{1,0:T(8,128)} custom-call(s32[3]{0:T(128)S(1)} %copy-done, f32[512,128]{1,0:T(8,128)S(1)} %bitcast.11, f32[512,128]{1,0:T(8,128)S(1)} %bitcast.13, f32[512,128]{1,0:T(8,128)S(1)} %collective-permute-done.16.refs_2_, f32[512,128]{1,0:T(8,128)S(1)} %collective-permute-done.17.refs_3_, f32[256,128]{1,0:T(8,128)S(1)} %collective-permute-done.18.refs_4_, ...), custom_call_target="tpu_custom_call" | custom-call | tf_op jit(solution)/shard_map/finish/pallas_call | solution.py:285
  (30 shorter events, 7.4 us)
Async XLA Ops:
  13.2 30.2 %copy-start.1 = (f32[2048,128]{1,0:T(8,128)S(1)}, f32[2048,128]{1,0:T(8,128)}, u32[]{:S(2)}) copy-start(f32[2048,128]{1,0:T(8,128)} %get-tuple-element.19) | copy-start | bytes 3145732
  13.2 75.9 %copy-start = (s32[3]{0:T(128)S(1)}, s32[3]{0:T(128)}, u32[]{:S(2)}) copy-start(s32[3]{0:T(128)} %pad_add_fusion.spot_ref) | copy-start | bytes 40
  13.2 2.9 %collective-permute-start = (f32[2048,128]{1,0:T(8,128)}, f32[2048,128]{1,0:T(8,128)S(1)}, u32[]{:S(2)}, u32[]{:S(2)}) collective-permute-start(f32[2048,128]{1,0:T(8,128)} %get-tuple-element.20), channel_id=1, source_target_pairs={{0,8},{8,0},{16,24},{24,16},{1,9},{9,1},{17,25},{25,17},{2,10},{10... | collective-permute-start | bytes 3145736 | tf_op jit(solution)/shard_map/ppermute | solution.py:217
  28.5 2.9 %collective-permute-start.2 = (f32[2048,128]{1,0:T(8,128)}, f32[2048,128]{1,0:T(8,128)S(1)}, u32[]{:S(2)}, u32[]{:S(2)}) collective-permute-start(f32[2048,128]{1,0:T(8,128)} %get-tuple-element.24), channel_id=1, source_target_pairs={{0,8},{8,0},{16,24},{24,16},{1,9},{9,1},{17,25},{25,17},{2,10},{10... | collective-permute-start | bytes 3145736 | tf_op jit(solution)/shard_map/ppermute | solution.py:217
  28.7 14.8 %collective-permute-start.1 = (f32[1024,128]{1,0:T(8,128)S(1)}, f32[1024,128]{1,0:T(8,128)S(1)}, u32[]{:S(2)}, u32[]{:S(2)}) collective-permute-start(f32[1024,128]{1,0:T(8,128)S(1)} %slice_add_fusion.2), channel_id=1, source_target_pairs={{0,16},{8,24},{16,0},{24,8},{1,17},{9,25},{17,1},{25,9},{2,18},{10... | collective-permute-start | bytes 1572872 | tf_op jit(solution)/shard_map/ppermute | solution.py:217
  32.5 21.6 %collective-permute-start.3 = (f32[1024,128]{1,0:T(8,128)S(1)}, f32[1024,128]{1,0:T(8,128)S(1)}, u32[]{:S(2)}, u32[]{:S(2)}) collective-permute-start(f32[1024,128]{1,0:T(8,128)S(1)} %slice_add_fusion), channel_id=1, source_target_pairs={{0,16},{8,24},{16,0},{24,8},{1,17},{9,25},{17,1},{25,9},{2,18},{10... | collective-permute-start | bytes 1572872 | tf_op jit(solution)/shard_map/ppermute | solution.py:217
  43.5 13.3 %collective-permute-start.6 = (f32[1024,128]{1,0:T(8,128)S(1)}, f32[1024,128]{1,0:T(8,128)S(1)}, u32[]{:S(2)}, u32[]{:S(2)}) collective-permute-start(f32[1024,128]{1,0:T(8,128)S(1)} %fusion.1.refs_0_), channel_id=1, source_target_pairs={{0,2},{1,3},{2,4},{3,5},{4,6},{5,7},{6,14},{7,15},{8,0},{9,1},{10,... | collective-permute-start | bytes 1572872 | tf_op jit(solution)/shard_map/ppermute | solution.py:245
  55.2 8.3 %collective-permute-start.11 = (f32[1024,128]{1,0:T(8,128)S(1)}, f32[1024,128]{1,0:T(8,128)S(1)}, u32[]{:S(2)}, u32[]{:S(2)}) collective-permute-start(f32[1024,128]{1,0:T(8,128)S(1)} %fusion.refs_1_), channel_id=1, source_target_pairs={{0,2},{1,3},{2,4},{3,5},{4,6},{5,7},{6,14},{7,15},{8,0},{9,1},{10,... | collective-permute-start | bytes 1572872 | tf_op jit(solution)/shard_map/ppermute | solution.py:245
  56.9 12.3 %collective-permute-start.7 = (f32[1024,128]{1,0:T(8,128)S(1)}, f32[1024,128]{1,0:T(8,128)S(1)}, u32[]{:S(2)}, u32[]{:S(2)}) collective-permute-start(f32[1024,128]{1,0:T(8,128)S(1)} %collective-permute-done.6.refs_0_), channel_id=1, source_target_pairs={{0,2},{1,3},{2,4},{3,5},{4,6},{5,7},{6,14},{7,15},{8,0},{9,1},{10,... | collective-permute-start | bytes 1572872 | tf_op jit(solution)/shard_map/ppermute | solution.py:245
  63.5 11.2 %collective-permute-start.12 = (f32[1024,128]{1,0:T(8,128)S(1)}, f32[1024,128]{1,0:T(8,128)S(1)}, u32[]{:S(2)}, u32[]{:S(2)}) collective-permute-start(f32[1024,128]{1,0:T(8,128)S(1)} %collective-permute-done.11.refs_0_), channel_id=1, source_target_pairs={{0,2},{1,3},{2,4},{3,5},{4,6},{5,7},{6,14},{7,15},{8,0},{9,1},{10,... | collective-permute-start | bytes 1572872 | tf_op jit(solution)/shard_map/ppermute | solution.py:245
  66.0 14.9 %collective-permute-start.4 = (f32[1024,128]{1,0:T(8,128)S(1)}, f32[1024,128]{1,0:T(8,128)S(1)}, u32[]{:S(2)}, u32[]{:S(2)}) collective-permute-start(f32[1024,128]{1,0:T(8,128)S(1)} %fusion.1.refs_0_), channel_id=1, source_target_pairs={{0,1},{1,0},{2,3},{3,2},{4,5},{5,4},{6,7},{7,6},{8,9},{9,8},{10,11... | collective-permute-start | bytes 1572872 | tf_op jit(solution)/shard_map/ppermute | solution.py:250
  66.5 22.6 %collective-permute-start.5 = (f32[1024,128]{1,0:T(8,128)S(1)}, f32[1024,128]{1,0:T(8,128)S(1)}, u32[]{:S(2)}, u32[]{:S(2)}) collective-permute-start(f32[1024,128]{1,0:T(8,128)S(1)} %fusion.refs_1_), channel_id=1, source_target_pairs={{0,1},{1,0},{2,3},{3,2},{4,5},{5,4},{6,7},{7,6},{8,9},{9,8},{10,11... | collective-permute-start | bytes 1572872 | tf_op jit(solution)/shard_map/ppermute | solution.py:250
  69.2 22.1 %collective-permute-start.8 = (f32[1024,128]{1,0:T(8,128)S(1)}, f32[1024,128]{1,0:T(8,128)S(1)}, u32[]{:S(2)}, u32[]{:S(2)}) collective-permute-start(f32[1024,128]{1,0:T(8,128)S(1)} %collective-permute-done.7.refs_1_), channel_id=1, source_target_pairs={{0,2},{1,3},{2,4},{3,5},{4,6},{5,7},{6,14},{7,15},{8,0},{9,1},{10,... | collective-permute-start | bytes 1572872 | tf_op jit(solution)/shard_map/ppermute | solution.py:245
  74.8 17.2 %collective-permute-start.13 = (f32[1024,128]{1,0:T(8,128)S(1)}, f32[1024,128]{1,0:T(8,128)S(1)}, u32[]{:S(2)}, u32[]{:S(2)}) collective-permute-start(f32[1024,128]{1,0:T(8,128)S(1)} %collective-permute-done.12.refs_1_), channel_id=1, source_target_pairs={{0,2},{1,3},{2,4},{3,5},{4,6},{5,7},{6,14},{7,15},{8,0},{9,1},{10,... | collective-permute-start | bytes 1572872 | tf_op jit(solution)/shard_map/ppermute | solution.py:245
  91.9 4.2 %collective-permute-start.9 = (f32[2,512,128]{2,1,0:T(8,128)S(1)}, f32[2,512,128]{2,1,0:T(8,128)S(1)}, u32[]{:S(2)}, u32[]{:S(2)}) collective-permute-start(f32[2,512,128]{2,1,0:T(8,128)S(1)} %get-tuple-element.30), channel_id=1, source_target_pairs={{0,8},{8,0},{16,24},{24,16},{1,9},{9,1},{17,25},{25,17},{2,10},{10... | collective-permute-start | bytes 1572872 | tf_op jit(solution)/shard_map/ppermute | solution.py:217
  92.7 5.0 %collective-permute-start.14 = (f32[2,512,128]{2,1,0:T(8,128)S(1)}, f32[2,512,128]{2,1,0:T(8,128)S(1)}, u32[]{:S(2)}, u32[]{:S(2)}) collective-permute-start(f32[2,512,128]{2,1,0:T(8,128)S(1)} %get-tuple-element.32), channel_id=1, source_target_pairs={{0,8},{8,0},{16,24},{24,16},{1,9},{9,1},{17,25},{25,17},{2,10},{10... | collective-permute-start | bytes 1572872 | tf_op jit(solution)/shard_map/ppermute | solution.py:217
  96.2 9.2 %collective-permute-start.10 = (f32[1,512,128]{2,1,0:T(8,128)S(1)}, f32[1,512,128]{2,1,0:T(8,128)S(1)}, u32[]{:S(2)}, u32[]{:S(2)}) collective-permute-start(f32[1,512,128]{2,1,0:T(8,128)S(1)} %slice_add_fusion.6), channel_id=1, source_target_pairs={{0,16},{8,24},{16,0},{24,8},{1,17},{9,25},{17,1},{25,9},{2,18},{10... | collective-permute-start | bytes 786440 | tf_op jit(solution)/shard_map/ppermute | solution.py:217
  97.7 12.4 %collective-permute-start.15 = (f32[1,512,128]{2,1,0:T(8,128)S(1)}, f32[1,512,128]{2,1,0:T(8,128)S(1)}, u32[]{:S(2)}, u32[]{:S(2)}) collective-permute-start(f32[1,512,128]{2,1,0:T(8,128)S(1)} %slice_add_fusion.4), channel_id=1, source_target_pairs={{0,16},{8,24},{16,0},{24,8},{1,17},{9,25},{17,1},{25,9},{2,18},{10... | collective-permute-start | bytes 786440 | tf_op jit(solution)/shard_map/ppermute | solution.py:217
  105.5 24.2 %collective-permute-start.16 = (f32[512,128]{1,0:T(8,128)S(1)}, f32[512,128]{1,0:T(8,128)S(1)}, u32[]{:S(2)}, u32[]{:S(2)}) collective-permute-start(f32[512,128]{1,0:T(8,128)S(1)} %bitcast.10), channel_id=1, source_target_pairs={{0,0},{1,1},{2,8},{3,9},{4,16},{5,17},{6,24},{7,25},{8,2},{9,3},{1... | collective-permute-start | bytes 786440 | tf_op jit(solution)/shard_map/ppermute | solution.py:279
  110.2 23.7 %collective-permute-start.17 = (f32[512,128]{1,0:T(8,128)S(1)}, f32[512,128]{1,0:T(8,128)S(1)}, u32[]{:S(2)}, u32[]{:S(2)}) collective-permute-start(f32[512,128]{1,0:T(8,128)S(1)} %bitcast.12), channel_id=1, source_target_pairs={{0,0},{1,1},{2,8},{3,9},{4,16},{5,17},{6,24},{7,25},{8,2},{9,3},{1... | collective-permute-start | bytes 786440 | tf_op jit(solution)/shard_map/ppermute | solution.py:279
  114.9 5.0 %collective-permute-start.18 = (f32[256,128]{1,0:T(8,128)S(1)}, f32[256,128]{1,0:T(8,128)S(1)}, u32[]{:S(2)}, u32[]{:S(2)}) collective-permute-start(f32[256,128]{1,0:T(8,128)S(1)} %dynamic-slice_bitcast_fusion.1), channel_id=1, source_target_pairs={{0,1},{1,0},{2,3},{3,2},{4,5},{5,4},{6,7},{7,6},{8,9},{9,8},{10,11... | collective-permute-start | bytes 393224 | tf_op jit(solution)/shard_map/ppermute | solution.py:282
  115.5 14.2 %collective-permute-start.19 = (f32[256,128]{1,0:T(8,128)S(1)}, f32[256,128]{1,0:T(8,128)S(1)}, u32[]{:S(2)}, u32[]{:S(2)}) collective-permute-start(f32[256,128]{1,0:T(8,128)S(1)} %dynamic-slice_bitcast_fusion), channel_id=1, source_target_pairs={{0,1},{1,0},{2,3},{3,2},{4,5},{5,4},{6,7},{7,6},{8,9},{9,8},{10,11... | collective-permute-start | bytes 393224 | tf_op jit(solution)/shard_map/ppermute | solution.py:282

commit v4 on v3

--- a/solution.py
+++ b/solution.py
@@ -27,20 +27,11 @@
     return parts
 
 
-def transform_and_pick(groups, strip, spot_ref, index_ref, bits_ref, slab_ref, keep_ref, send_ref, mixed, arrived):
+def transform_and_pick(groups, strip, spot_ref, index_ref, bits_ref, slab_ref, keep_ref, send_ref, mixed):
     height = slab_ref.shape[0]
-    steps = arrived.shape[0]
+    steps, inner_blocks = bits_ref.shape[0], bits_ref.shape[1]
     block = height // steps
-    inner_blocks = block // INNER
-
-    def fetch(step):
-        rows = pl.ds(pl.multiple_of(step * block, block), block)
-        return pltpu.make_async_copy(
-            slab_ref.at[rows, pl.ds(strip * LANES, LANES)], mixed.at[rows, :], arrived.at[step]
-        )
-
-    for step in range(steps):
-        fetch(step).start()
+    columns = slice(strip * LANES, (strip + 1) * LANES)
 
     row = lax.broadcasted_iota(jnp.int32, (INNER, 2 * INNER), 0)
     col = lax.broadcasted_iota(jnp.int32, (INNER, 2 * INNER), 1) & (INNER - 1)
@@ -59,14 +50,13 @@
     @pl.loop(0, steps)
     def _(step):
         base = step * block
-        fetch(step).wait()
         flips = (1 - 2 * bits_ref[step]).astype(jnp.float32)
         for at in range(inner_blocks):
             rows = pl.ds(pl.multiple_of(base + at * INNER, INNER), INNER)
             flip = flips[at : at + 1, :]
             signed = (table * jnp.concatenate([flip, flip], axis=1)).astype(jnp.bfloat16)
             mixed[rows, :] = jnp.dot(
-                signed, jnp.concatenate(two_parts(mixed[rows, :]), axis=0), preferred_element_type=jnp.float32
+                signed, jnp.concatenate(two_parts(slab_ref[rows, columns]), axis=0), preferred_element_type=jnp.float32
             )
 
         @pl.loop(0, INNER // 8, unroll=4)
@@ -80,16 +70,17 @@
     count = index_ref.shape[0] // groups
     bits = groups.bit_length() - 1
     half = groups // 2
+    unroll = min(128, count)
     for place in range(groups):
         out = keep_ref if place < half else send_ref
         start = (spot_ref[0] ^ bit_reverse(place, bits)) * count
         to = (place % half) * count
 
-        @pl.loop(0, count // 32)
+        @pl.loop(0, count // unroll)
         def _(chunk):
-            for at in range(32):
-                source = index_ref[start + chunk * 32 + at]
-                out[pl.ds(to + chunk * 32 + at, 1), :] = mixed[pl.ds(source, 1), :]
+            for at in range(unroll):
+                source = index_ref[start + chunk * unroll + at]
+                out[pl.ds(to + chunk * unroll + at, 1), :] = mixed[pl.ds(source, 1), :]
 
 
 VMEM = pl.BlockSpec(memory_space=pltpu.VMEM)
@@ -100,15 +91,14 @@
 def picked_strip(slab, sign_bits, index, spot, groups, strip):
     height = slab.shape[0]
     samples = index.shape[0]
-    steps = sign_bits.shape[0]
     half = jax.ShapeDtypeStruct((samples // 2, LANES), jnp.float32)
     return pl.pallas_call(
         functools.partial(transform_and_pick, groups, strip),
         out_shape=(half, half),
-        in_specs=[SMEM, SMEM, VMEM, pl.BlockSpec(memory_space=pl.ANY)],
+        in_specs=[SMEM, SMEM, VMEM, VMEM],
         out_specs=(VMEM, VMEM),
-        scratch_shapes=[pltpu.VMEM((2 * height, LANES), jnp.float32), pltpu.SemaphoreType.DMA((steps,))],
-        compiler_params=pltpu.CompilerParams(vmem_limit_bytes=56 * MIB),
+        scratch_shapes=[pltpu.VMEM((2 * height, LANES), jnp.float32)],
+        compiler_params=pltpu.CompilerParams(vmem_limit_bytes=32 * MIB),
         cost_estimate=pl.CostEstimate(
             flops=16 * height * INNER * LANES, bytes_accessed=16 * LANES * (height + samples), transcendentals=0
         ),
@@ -220,6 +210,9 @@
             return keep, got
         return keep[:half] + got[:half], keep[half:] + got[half:]
 
+    def after(value, earlier):
+        return lax.optimization_barrier((value, earlier))
+
     def onward(r, c):
         to = c + near if r % 2 == 0 else c - near
         return (r, to) if 0 <= to < columns else (r ^ 1, c)
@@ -235,13 +228,21 @@
     remote = []
     for strip in range(strips):
         keep, send = picked_strip(slab, sign_bits, index, spot, groups, strip)
+        if strip:
+            send, plane[0][-1] = after(send, plane[0][-1])
         for at in range(bits):
             keep, send = halve(keep, send, at)
             if at == 0:
-                index, send = lax.optimization_barrier((index, send))
+                index, send = after(index, send)
+        if strip:
+            send, remote[-1][0] = after(send, remote[-1][0])
+            for side in plane[1:]:
+                send, side[-1] = after(send, side[-1])
         own = keep + send
         moving, passed = own, []
         for away in range(1, groups):
+            if strip and away > 1:
+                moving, remote[-1][away - 1] = after(moving, remote[-1][away - 1])
             moving = lax.ppermute(moving, AXES, ring)
             passed.append(moving)
         remote.append(passed)
@@ -264,6 +265,8 @@
     half_sums = jax.ShapeDtypeStruct((groups // 2, near * width, LANES), jnp.float32)
     totals, directs, sideways = [], [], [[] for _ in range(1, near)]
     for strip in range(strips):
+        if strip:
+            remote[strip][-1], totals[-1] = after(remote[strip][-1], totals[-1])
         keep, send = pl.pallas_call(
             functools.partial(pair_products, groups, strip),
             out_shape=(half_sums, half_sums),

time: 136 us -> 117 us (0.86)
  the two profiles are of different devices: /device:TPU:6 before, /device:TPU:17 now
where the time goes in v4:
time: 117 us
  waiting for transfers between devices  68.1 us (58%)
  Pallas kernels  23.6 us (20%)
  starting transfers between devices  19.7 us (17%)
  local copies, waits for them, and re-layouts  4.17 us (4%)
  other arithmetic  1.24 us (1%)
    ppermute x8, waiting for transfers between devices, halve(): got = lax.ppermute(send, 'rows', [(r, r ^ 1 << at) for r in range(groups)])  34.3 us
    ppermute x6, waiting for transfers between devices, shards(): moving = lax.ppermute(moving, AXES, ring)  17.7 us
    pallas_call x2, Pallas kernels, picked_strip(): pl.pallas_call(functools.partial(transform_and_pick, groups, strip), out_...  16.7 us
    ppermute x8, starting transfers between devices, halve(): got = lax.ppermute(send, 'rows', [(r, r ^ 1 << at) for r in range(groups)])  10.9 us
    ppermute x2, waiting for transfers between devices, shards(): directs.append(lax.ppermute(total, AXES, mirror))  8.1 us
    ppermute x2, waiting for transfers between devices, shards(): lax.ppermute(part, 'cols', [(c, c ^ off) for c in range(columns)])  5 us
    unnamed x4, local copies, waits for them, and re-layouts  4.14 us
    ppermute x2, starting transfers between devices, shards(): directs.append(lax.ppermute(total, AXES, mirror))  3.83 us
  transfers between devices with their start and end apart: 20, of which 18 were waited for; matrix products, arithmetic and copies ran while one was open for 0% of the time, Pallas kernels for 9%

profile of v4, /device:TPU:17, one launch (start us, length us, event | category | flops | bytes accessed | tf_op | source)
XLA Modules:
  0.0 117.0 jit_solution(11998795722241628537)
XLA Ops:
  0.8 3.4 %copy-done = f32[8192,256]{1,0:T(8,128)S(1)} copy-done((f32[8192,256]{1,0:T(8,128)S(1)}, f32[8192,256]{1,0:T(8,128)}, u32[]{:S(2)}) %copy-start) | copy-done | bytes 8388632
  5.0 8.4 %transform_and_pick.2 = (f32[2048,128]{1,0:T(8,128)S(1)}, f32[2048,128]{1,0:T(8,128)S(1)}) custom-call(s32[3]{0:T(128)S(1)} %pad_add_fusion.spot_ref, s32[4096]{0:T(1024)S(1)} %multiply_add_fusion.index_ref, s32[8,8,128]{2,1,0:T(8,128)S(1)} %bitcast.14, f32[8192,256]{1,0:T(8,128)S(1)} %copy-done), custom_call_target="tpu_custom_call" | custom-call | flops 2147483648 | bytes 25165824 | tf_op jit(solution)/shard_map/transform_and_pick/pallas_call | solution.py:95
  14.1 2.3 %collective-permute-done = f32[2048,128]{1,0:T(8,128)S(1)} collective-permute-done((f32[2048,128]{1,0:T(8,128)S(1)}, f32[2048,128]{1,0:T(8,128)S(1)}, u32[]{:S(2)}, u32[]{:S(2)}) %collective-permute-start) | collective-permute-done | bytes 1048608 | tf_op jit(solution)/shard_map/ppermute | solution.py:207
  16.4 1.3 %collective-permute-start.1 = (f32[1024,128]{1,0:T(8,128)S(1)}, f32[1024,128]{1,0:T(8,128)S(1)}, u32[]{:S(2)}, u32[]{:S(2)}) collective-permute-start(f32[1024,128]{1,0:T(8,128)S(1)} %slice_add_fusion.3), channel_id=1, source_target_pairs={{0,16},{8,24},{16,0},{24,8},{1,17},{9,25},{17,1},{25,9},{2,18},{10... | collective-permute-start | bytes 1572872 | tf_op jit(solution)/shard_map/ppermute | solution.py:207
  17.7 8.3 %transform_and_pick.3 = (f32[2048,128]{1,0:T(8,128)S(1)}, f32[2048,128]{1,0:T(8,128)S(1)}) custom-call(s32[3]{0:T(128)S(1)} %pad_add_fusion.spot_ref, s32[4096]{0:T(1024)S(1)} %multiply_add_fusion.index_ref, s32[8,8,128]{2,1,0:T(8,128)S(1)} %bitcast.15, f32[8192,256]{1,0:T(8,128)S(1)} %copy-done), custom_call_target="tpu_custom_call" | custom-call | flops 2147483648 | bytes 25165824 | tf_op jit(solution)/shard_map/transform_and_pick/pallas_call | solution.py:95
  26.0 3.6 %collective-permute-done.1 = f32[1024,128]{1,0:T(8,128)S(1)} collective-permute-done((f32[1024,128]{1,0:T(8,128)S(1)}, f32[1024,128]{1,0:T(8,128)S(1)}, u32[]{:S(2)}, u32[]{:S(2)}) %collective-permute-start.1) | collective-permute-done | bytes 524320 | tf_op jit(solution)/shard_map/ppermute | solution.py:207
  29.7 1.3 %collective-permute-start.2 = (f32[2048,128]{1,0:T(8,128)S(1)}, f32[2048,128]{1,0:T(8,128)S(1)}, u32[]{:S(2)}, u32[]{:S(2)}) collective-permute-start(f32[2048,128]{1,0:T(8,128)S(1)} %get-tuple-element.37), channel_id=1, source_target_pairs={{0,8},{8,0},{16,24},{24,16},{1,9},{9,1},{17,25},{25,17},{2,10},{10... | collective-permute-start | bytes 3145736 | tf_op jit(solution)/shard_map/ppermute | solution.py:207
  31.1 2.1 %collective-permute-done.2 = f32[2048,128]{1,0:T(8,128)S(1)} collective-permute-done((f32[2048,128]{1,0:T(8,128)S(1)}, f32[2048,128]{1,0:T(8,128)S(1)}, u32[]{:S(2)}, u32[]{:S(2)}) %collective-permute-start.2) | collective-permute-done | bytes 1048608 | tf_op jit(solution)/shard_map/ppermute | solution.py:207
  33.3 1.3 %collective-permute-start.3 = (f32[1024,128]{1,0:T(8,128)S(1)}, f32[1024,128]{1,0:T(8,128)S(1)}, u32[]{:S(2)}, u32[]{:S(2)}) collective-permute-start(f32[1024,128]{1,0:T(8,128)S(1)} %slice_add_fusion), channel_id=1, source_target_pairs={{0,16},{8,24},{16,0},{24,8},{1,17},{9,25},{17,1},{25,9},{2,18},{10... | collective-permute-start | bytes 1572872 | tf_op jit(solution)/shard_map/ppermute | solution.py:207
  34.6 1.2 %collective-permute-start.5 = (f32[1024,128]{1,0:T(8,128)S(1)}, f32[1024,128]{1,0:T(8,128)S(1)}, u32[]{:S(2)}, u32[]{:S(2)}) collective-permute-start(f32[1024,128]{1,0:T(8,128)S(1)} %fusion.1.refs_0_), channel_id=1, source_target_pairs={{0,1},{1,0},{2,3},{3,2},{4,5},{5,4},{6,7},{7,6},{8,9},{9,8},{10,11... | collective-permute-start | bytes 1572872 | tf_op jit(solution)/shard_map/ppermute | solution.py:251
  35.8 3.5 %collective-permute-done.4.refs_0_ = f32[1024,128]{1,0:T(8,128)S(1)} collective-permute-done((f32[1024,128]{1,0:T(8,128)S(1)}, f32[1024,128]{1,0:T(8,128)S(1)}, u32[]{:S(2)}, u32[]{:S(2)}) %collective-permute-start.4) | collective-permute-done | bytes 524320 | tf_op jit(solution)/shard_map/ppermute | solution.py:246
  39.5 7.1 %collective-permute-done.3 = f32[1024,128]{1,0:T(8,128)S(1)} collective-permute-done((f32[1024,128]{1,0:T(8,128)S(1)}, f32[1024,128]{1,0:T(8,128)S(1)}, u32[]{:S(2)}, u32[]{:S(2)}) %collective-permute-start.3) | collective-permute-done | bytes 524320 | tf_op jit(solution)/shard_map/ppermute | solution.py:207
  47.8 1.2 %collective-permute-start.11 = (f32[1024,128]{1,0:T(8,128)S(1)}, f32[1024,128]{1,0:T(8,128)S(1)}, u32[]{:S(2)}, u32[]{:S(2)}) collective-permute-start(f32[1024,128]{1,0:T(8,128)S(1)} %fusion.refs_1_), channel_id=1, source_target_pairs={{0,1},{1,0},{2,3},{3,2},{4,5},{5,4},{6,7},{7,6},{8,9},{9,8},{10,11... | collective-permute-start | bytes 1572872 | tf_op jit(solution)/shard_map/ppermute | solution.py:251
  49.1 6.7 %collective-permute-done.6.refs_0_ = f32[1024,128]{1,0:T(8,128)S(1)} collective-permute-done((f32[1024,128]{1,0:T(8,128)S(1)}, f32[1024,128]{1,0:T(8,128)S(1)}, u32[]{:S(2)}, u32[]{:S(2)}) %collective-permute-start.6) | collective-permute-done | bytes 524320 | tf_op jit(solution)/shard_map/ppermute | solution.py:246
  56.0 2.2 %collective-permute-done.11.refs_3_ = f32[1024,128]{1,0:T(8,128)S(1)} collective-permute-done((f32[1024,128]{1,0:T(8,128)S(1)}, f32[1024,128]{1,0:T(8,128)S(1)}, u32[]{:S(2)}, u32[]{:S(2)}) %collective-permute-start.11) | collective-permute-done | bytes 524320 | tf_op jit(solution)/shard_map/ppermute | solution.py:251
  58.2 2.1 %turn_plane.1 = (bf16[512,1024]{1,0:T(8,128)(2,1)S(1)}, bf16[512,1024]{1,0:T(8,128)(2,1)S(1)}, f32[512,256]{1,0:T(8,128)S(1)}) custom-call(s32[3]{0:T(128)S(1)} %pad_add_fusion.spot_ref, f32[1024,128]{1,0:T(8,128)S(1)} %fusion.1.refs_0_, f32[1024,128]{1,0:T(8,128)S(1)} %fusion.refs_1_, f32[1024,128]{1,0:T(8,128)S(1)} %collective-permute-done.5.refs_2_, ...), custom_call_target="tpu_custom_call" | custom-call | tf_op jit(solution)/shard_map/turn_plane/pallas_call | solution.py:256
  61.5 5.6 %collective-permute-done.8.refs_1_ = f32[1024,128]{1,0:T(8,128)S(1)} collective-permute-done((f32[1024,128]{1,0:T(8,128)S(1)}, f32[1024,128]{1,0:T(8,128)S(1)}, u32[]{:S(2)}, u32[]{:S(2)}) %collective-permute-start.8) | collective-permute-done | bytes 524320 | tf_op jit(solution)/shard_map/ppermute | solution.py:246
  67.1 1.6 %pair_products.2 = (f32[2,512,128]{2,1,0:T(8,128)S(1)}, f32[2,512,128]{2,1,0:T(8,128)S(1)}) custom-call(s32[3]{0:T(128)S(1)} %pad_add_fusion.spot_ref, bf16[512,1024]{1,0:T(8,128)(2,1)S(1)} %get-tuple-element.45.high_ref, bf16[512,1024]{1,0:T(8,128)(2,1)S(1)} %get-tuple-element.46.low_ref, f32[512,256]{1,0:T(8,128)S(1)} %get-tuple-element.47.own_ref, ...), custom_call_target="tpu_custom_call" | custom-call | tf_op jit(solution)/shard_map/pair_products/pallas_call | solution.py:270
  68.7 3.4 %collective-permute-start.12 = (f32[2,512,128]{2,1,0:T(8,128)S(1)}, f32[2,512,128]{2,1,0:T(8,128)S(1)}, u32[]{:S(2)}, u32[]{:S(2)}) collective-permute-start(f32[2,512,128]{2,1,0:T(8,128)S(1)} %get-tuple-element.52), channel_id=1, source_target_pairs={{0,8},{8,0},{16,24},{24,16},{1,9},{9,1},{17,25},{25,17},{2,10},{10... | collective-permute-start | bytes 1572872 | tf_op jit(solution)/shard_map/ppermute | solution.py:207
  72.1 1.5 %collective-permute-done.12 = f32[2,512,128]{2,1,0:T(8,128)S(1)} collective-permute-done((f32[2,512,128]{2,1,0:T(8,128)S(1)}, f32[2,512,128]{2,1,0:T(8,128)S(1)}, u32[]{:S(2)}, u32[]{:S(2)}) %collective-permute-start.12) | collective-permute-done | bytes 524320 | tf_op jit(solution)/shard_map/ppermute | solution.py:207
  74.0 6.5 %collective-permute-done.13 = f32[1,512,128]{2,1,0:T(8,128)S(1)} collective-permute-done((f32[1,512,128]{2,1,0:T(8,128)S(1)}, f32[1,512,128]{2,1,0:T(8,128)S(1)}, u32[]{:S(2)}, u32[]{:S(2)}) %collective-permute-start.13) | collective-permute-done | bytes 262176 | tf_op jit(solution)/shard_map/ppermute | solution.py:207
  81.2 1.6 %pair_products.3 = (f32[2,512,128]{2,1,0:T(8,128)S(1)}, f32[2,512,128]{2,1,0:T(8,128)S(1)}) custom-call(s32[3]{0:T(128)S(1)} %pad_add_fusion.spot_ref, bf16[512,1024]{1,0:T(8,128)(2,1)S(1)} %get-tuple-element.45.high_ref, bf16[512,1024]{1,0:T(8,128)(2,1)S(1)} %get-tuple-element.46.low_ref, f32[512,256]{1,0:T(8,128)S(1)} %get-tuple-element.47.own_ref, ...), custom_call_target="tpu_custom_call" | custom-call | tf_op jit(solution)/shard_map/pair_products/pallas_call | solution.py:270
  82.9 2.3 %collective-permute-start.14 = (f32[2,512,128]{2,1,0:T(8,128)S(1)}, f32[2,512,128]{2,1,0:T(8,128)S(1)}, u32[]{:S(2)}, u32[]{:S(2)}) collective-permute-start(f32[2,512,128]{2,1,0:T(8,128)S(1)} %get-tuple-element.56), channel_id=1, source_target_pairs={{0,8},{8,0},{16,24},{24,16},{1,9},{9,1},{17,25},{25,17},{2,10},{10... | collective-permute-start | bytes 1572872 | tf_op jit(solution)/shard_map/ppermute | solution.py:207
  85.2 1.5 %collective-permute-done.14 = f32[2,512,128]{2,1,0:T(8,128)S(1)} collective-permute-done((f32[2,512,128]{2,1,0:T(8,128)S(1)}, f32[2,512,128]{2,1,0:T(8,128)S(1)}, u32[]{:S(2)}, u32[]{:S(2)}) %collective-permute-start.14) | collective-permute-done | bytes 524320 | tf_op jit(solution)/shard_map/ppermute | solution.py:207
  87.1 1.9 %collective-permute-start.16 = (f32[512,128]{1,0:T(8,128)S(1)}, f32[512,128]{1,0:T(8,128)S(1)}, u32[]{:S(2)}, u32[]{:S(2)}) collective-permute-start(f32[512,128]{1,0:T(8,128)S(1)} %bitcast.10), channel_id=1, source_target_pairs={{0,0},{1,1},{2,8},{3,9},{4,16},{5,17},{6,24},{7,25},{8,2},{9,3},{1... | collective-permute-start | bytes 786440 | tf_op jit(solution)/shard_map/ppermute | solution.py:282
  89.0 9.6 %collective-permute-done.15 = f32[1,512,128]{2,1,0:T(8,128)S(1)} collective-permute-done((f32[1,512,128]{2,1,0:T(8,128)S(1)}, f32[1,512,128]{2,1,0:T(8,128)S(1)}, u32[]{:S(2)}, u32[]{:S(2)}) %collective-permute-start.15) | collective-permute-done | bytes 262176 | tf_op jit(solution)/shard_map/ppermute | solution.py:207
  98.7 1.9 %collective-permute-start.17 = (f32[512,128]{1,0:T(8,128)S(1)}, f32[512,128]{1,0:T(8,128)S(1)}, u32[]{:S(2)}, u32[]{:S(2)}) collective-permute-start(f32[512,128]{1,0:T(8,128)S(1)} %bitcast.12), channel_id=1, source_target_pairs={{0,0},{1,1},{2,8},{3,9},{4,16},{5,17},{6,24},{7,25},{8,2},{9,3},{1... | collective-permute-start | bytes 786440 | tf_op jit(solution)/shard_map/ppermute | solution.py:282
  100.7 1.3 %collective-permute-start.18 = (f32[256,128]{1,0:T(8,128)S(1)}, f32[256,128]{1,0:T(8,128)S(1)}, u32[]{:S(2)}, u32[]{:S(2)}) collective-permute-start(f32[256,128]{1,0:T(8,128)S(1)} %dynamic-slice_bitcast_fusion.1), channel_id=1, source_target_pairs={{0,1},{1,0},{2,3},{3,2},{4,5},{5,4},{6,7},{7,6},{8,9},{9,8},{10,11... | collective-permute-start | bytes 393224 | tf_op jit(solution)/shard_map/ppermute | solution.py:285
  102.3 2.3 %collective-permute-done.18.refs_4_ = f32[256,128]{1,0:T(8,128)S(1)} collective-permute-done((f32[256,128]{1,0:T(8,128)S(1)}, f32[256,128]{1,0:T(8,128)S(1)}, u32[]{:S(2)}, u32[]{:S(2)}) %collective-permute-start.18) | collective-permute-done | bytes 131104 | tf_op jit(solution)/shard_map/ppermute | solution.py:285
  104.6 2.7 %collective-permute-done.19.refs_5_ = f32[256,128]{1,0:T(8,128)S(1)} collective-permute-done((f32[256,128]{1,0:T(8,128)S(1)}, f32[256,128]{1,0:T(8,128)S(1)}, u32[]{:S(2)}, u32[]{:S(2)}) %collective-permute-start.19) | collective-permute-done | bytes 131104 | tf_op jit(solution)/shard_map/ppermute | solution.py:285
  107.3 8.1 %collective-permute-done.17.refs_3_ = f32[512,128]{1,0:T(8,128)S(1)} collective-permute-done((f32[512,128]{1,0:T(8,128)S(1)}, f32[512,128]{1,0:T(8,128)S(1)}, u32[]{:S(2)}, u32[]{:S(2)}) %collective-permute-start.17) | collective-permute-done | bytes 262176 | tf_op jit(solution)/shard_map/ppermute | solution.py:282
  115.4 1.6 %finish.1 = f32[512,256]{1,0:T(8,128)} custom-call(s32[3]{0:T(128)S(1)} %pad_add_fusion.spot_ref, f32[512,128]{1,0:T(8,128)S(1)} %bitcast.11, f32[512,128]{1,0:T(8,128)S(1)} %bitcast.13, f32[512,128]{1,0:T(8,128)S(1)} %collective-permute-done.16.refs_2_, f32[512,128]{1,0:T(8,128)S(1)} %collective-permute-done.17.refs_3_, ...), custom_call_target="tpu_custom_call" | custom-call | tf_op jit(solution)/shard_map/finish/pallas_call | solution.py:288
  (30 shorter events, 7.3 us)
Async XLA Ops:
  0.8 3.4 %copy-start = (f32[8192,256]{1,0:T(8,128)S(1)}, f32[8192,256]{1,0:T(8,128)}, u32[]{:S(2)}) copy-start(f32[8192,256]{1,0:T(8,128)} %slab_ref.3) | copy-start | bytes 25165828
  4.2 0.8 copy-start.1
  13.3 3.0 %collective-permute-start = (f32[2048,128]{1,0:T(8,128)S(1)}, f32[2048,128]{1,0:T(8,128)S(1)}, u32[]{:S(2)}, u32[]{:S(2)}) collective-permute-start(f32[2048,128]{1,0:T(8,128)S(1)} %get-tuple-element.32), channel_id=1, source_target_pairs={{0,8},{8,0},{16,24},{24,16},{1,9},{9,1},{17,25},{25,17},{2,10},{10... | collective-permute-start | bytes 3145736 | tf_op jit(solution)/shard_map/ppermute | solution.py:207
  16.4 13.2 %collective-permute-start.1 = (f32[1024,128]{1,0:T(8,128)S(1)}, f32[1024,128]{1,0:T(8,128)S(1)}, u32[]{:S(2)}, u32[]{:S(2)}) collective-permute-start(f32[1024,128]{1,0:T(8,128)S(1)} %slice_add_fusion.3), channel_id=1, source_target_pairs={{0,16},{8,24},{16,0},{24,8},{1,17},{9,25},{17,1},{25,9},{2,18},{10... | collective-permute-start | bytes 1572872 | tf_op jit(solution)/shard_map/ppermute | solution.py:207
  29.7 3.6 %collective-permute-start.2 = (f32[2048,128]{1,0:T(8,128)S(1)}, f32[2048,128]{1,0:T(8,128)S(1)}, u32[]{:S(2)}, u32[]{:S(2)}) collective-permute-start(f32[2048,128]{1,0:T(8,128)S(1)} %get-tuple-element.37), channel_id=1, source_target_pairs={{0,8},{8,0},{16,24},{24,16},{1,9},{9,1},{17,25},{25,17},{2,10},{10... | collective-permute-start | bytes 3145736 | tf_op jit(solution)/shard_map/ppermute | solution.py:207
  31.0 8.3 %collective-permute-start.4 = (f32[1024,128]{1,0:T(8,128)S(1)}, f32[1024,128]{1,0:T(8,128)S(1)}, u32[]{:S(2)}, u32[]{:S(2)}) collective-permute-start(f32[1024,128]{1,0:T(8,128)S(1)} %fusion.1.refs_0_), channel_id=1, source_target_pairs={{0,2},{1,3},{2,4},{3,5},{4,6},{5,7},{6,14},{7,15},{8,0},{9,1},{10,... | collective-permute-start | bytes 1572872 | tf_op jit(solution)/shard_map/ppermute | solution.py:246
  33.3 13.2 %collective-permute-start.3 = (f32[1024,128]{1,0:T(8,128)S(1)}, f32[1024,128]{1,0:T(8,128)S(1)}, u32[]{:S(2)}, u32[]{:S(2)}) collective-permute-start(f32[1024,128]{1,0:T(8,128)S(1)} %slice_add_fusion), channel_id=1, source_target_pairs={{0,16},{8,24},{16,0},{24,8},{1,17},{9,25},{17,1},{25,9},{2,18},{10... | collective-permute-start | bytes 1572872 | tf_op jit(solution)/shard_map/ppermute | solution.py:207
  34.6 12.8 %collective-permute-start.5 = (f32[1024,128]{1,0:T(8,128)S(1)}, f32[1024,128]{1,0:T(8,128)S(1)}, u32[]{:S(2)}, u32[]{:S(2)}) collective-permute-start(f32[1024,128]{1,0:T(8,128)S(1)} %fusion.1.refs_0_), channel_id=1, source_target_pairs={{0,1},{1,0},{2,3},{3,2},{4,5},{5,4},{6,7},{7,6},{8,9},{9,8},{10,11... | collective-permute-start | bytes 1572872 | tf_op jit(solution)/shard_map/ppermute | solution.py:251
  39.3 8.4 %collective-permute-start.7 = (f32[1024,128]{1,0:T(8,128)S(1)}, f32[1024,128]{1,0:T(8,128)S(1)}, u32[]{:S(2)}, u32[]{:S(2)}) collective-permute-start(f32[1024,128]{1,0:T(8,128)S(1)} %collective-permute-done.4.refs_0_), channel_id=1, source_target_pairs={{0,2},{1,3},{2,4},{3,5},{4,6},{5,7},{6,14},{7,15},{8,0},{9,1},{10,... | collective-permute-start | bytes 1572872 | tf_op jit(solution)/shard_map/ppermute | solution.py:246
  47.5 8.3 %collective-permute-start.6 = (f32[1024,128]{1,0:T(8,128)S(1)}, f32[1024,128]{1,0:T(8,128)S(1)}, u32[]{:S(2)}, u32[]{:S(2)}) collective-permute-start(f32[1024,128]{1,0:T(8,128)S(1)} %fusion.refs_1_), channel_id=1, source_target_pairs={{0,2},{1,3},{2,4},{3,5},{4,6},{5,7},{6,14},{7,15},{8,0},{9,1},{10,... | collective-permute-start | bytes 1572872 | tf_op jit(solution)/shard_map/ppermute | solution.py:246
  47.7 13.8 %collective-permute-start.9 = (f32[1024,128]{1,0:T(8,128)S(1)}, f32[1024,128]{1,0:T(8,128)S(1)}, u32[]{:S(2)}, u32[]{:S(2)}) collective-permute-start(f32[1024,128]{1,0:T(8,128)S(1)} %collective-permute-done.7.refs_1_), channel_id=1, source_target_pairs={{0,2},{1,3},{2,4},{3,5},{4,6},{5,7},{6,14},{7,15},{8,0},{9,1},{10,... | collective-permute-start | bytes 1572872 | tf_op jit(solution)/shard_map/ppermute | solution.py:246
  47.8 10.3 %collective-permute-start.11 = (f32[1024,128]{1,0:T(8,128)S(1)}, f32[1024,128]{1,0:T(8,128)S(1)}, u32[]{:S(2)}, u32[]{:S(2)}) collective-permute-start(f32[1024,128]{1,0:T(8,128)S(1)} %fusion.refs_1_), channel_id=1, source_target_pairs={{0,1},{1,0},{2,3},{3,2},{4,5},{5,4},{6,7},{7,6},{8,9},{9,8},{10,11... | collective-permute-start | bytes 1572872 | tf_op jit(solution)/shard_map/ppermute | solution.py:251
  55.8 11.2 %collective-permute-start.8 = (f32[1024,128]{1,0:T(8,128)S(1)}, f32[1024,128]{1,0:T(8,128)S(1)}, u32[]{:S(2)}, u32[]{:S(2)}) collective-permute-start(f32[1024,128]{1,0:T(8,128)S(1)} %collective-permute-done.6.refs_0_), channel_id=1, source_target_pairs={{0,2},{1,3},{2,4},{3,5},{4,6},{5,7},{6,14},{7,15},{8,0},{9,1},{10,... | collective-permute-start | bytes 1572872 | tf_op jit(solution)/shard_map/ppermute | solution.py:246
  68.7 5.0 %collective-permute-start.12 = (f32[2,512,128]{2,1,0:T(8,128)S(1)}, f32[2,512,128]{2,1,0:T(8,128)S(1)}, u32[]{:S(2)}, u32[]{:S(2)}) collective-permute-start(f32[2,512,128]{2,1,0:T(8,128)S(1)} %get-tuple-element.52), channel_id=1, source_target_pairs={{0,8},{8,0},{16,24},{24,16},{1,9},{9,1},{17,25},{25,17},{2,10},{10... | collective-permute-start | bytes 1572872 | tf_op jit(solution)/shard_map/ppermute | solution.py:207
  72.1 9.1 %collective-permute-start.10 = (f32[1024,128]{1,0:T(8,128)S(1)}, f32[1024,128]{1,0:T(8,128)S(1)}, u32[]{:S(2)}, u32[]{:S(2)}) collective-permute-start(f32[1024,128]{1,0:T(8,128)S(1)} %collective-permute-done.8.refs_1_), channel_id=1, source_target_pairs={{0,2},{1,3},{2,4},{3,5},{4,6},{5,7},{6,14},{7,15},{8,0},{9,1},{10,... | collective-permute-start | bytes 1572872 | tf_op jit(solution)/shard_map/ppermute | solution.py:246
  73.7 6.8 %collective-permute-start.13 = (f32[1,512,128]{2,1,0:T(8,128)S(1)}, f32[1,512,128]{2,1,0:T(8,128)S(1)}, u32[]{:S(2)}, u32[]{:S(2)}) collective-permute-start(f32[1,512,128]{2,1,0:T(8,128)S(1)} %slice_add_fusion.6), channel_id=1, source_target_pairs={{0,16},{8,24},{16,0},{24,8},{1,17},{9,25},{17,1},{25,9},{2,18},{10... | collective-permute-start | bytes 786440 | tf_op jit(solution)/shard_map/ppermute | solution.py:207
  82.9 3.9 %collective-permute-start.14 = (f32[2,512,128]{2,1,0:T(8,128)S(1)}, f32[2,512,128]{2,1,0:T(8,128)S(1)}, u32[]{:S(2)}, u32[]{:S(2)}) collective-permute-start(f32[2,512,128]{2,1,0:T(8,128)S(1)} %get-tuple-element.56), channel_id=1, source_target_pairs={{0,8},{8,0},{16,24},{24,16},{1,9},{9,1},{17,25},{25,17},{2,10},{10... | collective-permute-start | bytes 1572872 | tf_op jit(solution)/shard_map/ppermute | solution.py:207
  86.8 11.9 %collective-permute-start.15 = (f32[1,512,128]{2,1,0:T(8,128)S(1)}, f32[1,512,128]{2,1,0:T(8,128)S(1)}, u32[]{:S(2)}, u32[]{:S(2)}) collective-permute-start(f32[1,512,128]{2,1,0:T(8,128)S(1)} %slice_add_fusion.4), channel_id=1, source_target_pairs={{0,16},{8,24},{16,0},{24,8},{1,17},{9,25},{17,1},{25,9},{2,18},{10... | collective-permute-start | bytes 786440 | tf_op jit(solution)/shard_map/ppermute | solution.py:207
  87.1 17.5 %collective-permute-start.16 = (f32[512,128]{1,0:T(8,128)S(1)}, f32[512,128]{1,0:T(8,128)S(1)}, u32[]{:S(2)}, u32[]{:S(2)}) collective-permute-start(f32[512,128]{1,0:T(8,128)S(1)} %bitcast.10), channel_id=1, source_target_pairs={{0,0},{1,1},{2,8},{3,9},{4,16},{5,17},{6,24},{7,25},{8,2},{9,3},{1... | collective-permute-start | bytes 786440 | tf_op jit(solution)/shard_map/ppermute | solution.py:282
  98.7 16.7 %collective-permute-start.17 = (f32[512,128]{1,0:T(8,128)S(1)}, f32[512,128]{1,0:T(8,128)S(1)}, u32[]{:S(2)}, u32[]{:S(2)}) collective-permute-start(f32[512,128]{1,0:T(8,128)S(1)} %bitcast.12), channel_id=1, source_target_pairs={{0,0},{1,1},{2,8},{3,9},{4,16},{5,17},{6,24},{7,25},{8,2},{9,3},{1... | collective-permute-start | bytes 786440 | tf_op jit(solution)/shard_map/ppermute | solution.py:282
  100.7 3.9 %collective-permute-start.18 = (f32[256,128]{1,0:T(8,128)S(1)}, f32[256,128]{1,0:T(8,128)S(1)}, u32[]{:S(2)}, u32[]{:S(2)}) collective-permute-start(f32[256,128]{1,0:T(8,128)S(1)} %dynamic-slice_bitcast_fusion.1), channel_id=1, source_target_pairs={{0,1},{1,0},{2,3},{3,2},{4,5},{5,4},{6,7},{7,6},{8,9},{9,8},{10,11... | collective-permute-start | bytes 393224 | tf_op jit(solution)/shard_map/ppermute | solution.py:285
  102.0 5.3 %collective-permute-start.19 = (f32[256,128]{1,0:T(8,128)S(1)}, f32[256,128]{1,0:T(8,128)S(1)}, u32[]{:S(2)}, u32[]{:S(2)}) collective-permute-start(f32[256,128]{1,0:T(8,128)S(1)} %dynamic-slice_bitcast_fusion), channel_id=1, source_target_pairs={{0,1},{1,0},{2,3},{3,2},{4,5},{5,4},{6,7},{7,6},{8,9},{9,8},{10,11... | collective-permute-start | bytes 393224 | tf_op jit(solution)/shard_map/ppermute | solution.py:285

commit v5 on v4

--- a/solution.py
+++ b/solution.py
@@ -129,7 +129,7 @@
     own_ref[...] = three_products((high_ref[...], low_ref[...]), two_parts(own))
 
 
-def pair_products(groups, strip, spot_ref, high_ref, low_ref, own_ref, *refs):
+def pair_products(groups, strip, flip, spot_ref, high_ref, low_ref, own_ref, *refs):
     remote, (keep_ref, send_ref) = refs[:-2], refs[-2:]
     me, at_plane = spot_ref[0], spot_ref[1]
     half = keep_ref.shape[0]
@@ -137,7 +137,7 @@
     back = 1 - 2 * (me & 1)
 
     def store(other, value):
-        place = bit_reverse(other ^ me, bits)
+        place = bit_reverse(other ^ me ^ flip, bits)
 
         @pl.when(place < half)
         def _():
@@ -161,26 +161,17 @@
             store(above, lambda: jnp.zeros(keep_ref.shape[1:], jnp.float32))
 
 
-def finish(factor, near, strips, spot_ref, *refs):
-    totals, directs, turned, out_ref = refs[:strips], refs[strips : 2 * strips], refs[2 * strips : -1], refs[-1]
-    me, at_plane, at_near = spot_ref[0], spot_ref[1], spot_ref[2]
+def finish(factor, strips, spot_ref, *refs):
+    directs, turned, out_ref = refs[:strips], refs[strips:-1], refs[-1]
     width = out_ref.shape[1]
-
-    @pl.when(me == at_plane)
+    for at, part in enumerate(turned):
+        start = (spot_ref[2] ^ (at // strips)) * width + at % strips * LANES
+        out_ref[pl.ds(pl.multiple_of(start, LANES), LANES), :] = part[...].T * factor
+
+    @pl.when(spot_ref[0] != spot_ref[1])
     def _():
-        for strip in range(strips):
-            out_ref[:, strip * LANES : (strip + 1) * LANES] = totals[strip][...] * factor
-
-    @pl.when(me != at_plane)
-    def _():
-        direct = jnp.concatenate([part[...] for part in directs], axis=1) * factor
-        out_ref[...] = direct
-        for off in range(near):
-            start = pl.multiple_of((at_near ^ off) * width, width)
-            for strip in range(strips):
-                part = totals[strip][pl.ds(start, width), :] if off == 0 else turned[(off - 1) * strips + strip][...]
-                rows = pl.ds(pl.multiple_of(start + strip * LANES, LANES), LANES)
-                out_ref[rows, :] = out_ref[rows, :] + part.T * factor
+        direct = jnp.concatenate([part[...] for part in directs], axis=1)
+        out_ref[...] = out_ref[...] + direct * factor
 
 
 def shards(slab, sign_bits, sample_rows):
@@ -222,7 +213,6 @@
         return [(r * columns + c, r_to * columns + c_to) for r, c, r_to, c_to in ends]
 
     ring = pairs(onward)
-    mirror = pairs(lambda r, c: (c // near, r * near + c % near))
 
     plane = [[] for _ in range(near)]
     remote = []
@@ -263,30 +253,33 @@
     )(spot, *parts)
 
     half_sums = jax.ShapeDtypeStruct((groups // 2, near * width, LANES), jnp.float32)
-    totals, directs, sideways = [], [], [[] for _ in range(1, near)]
+    totals, directs, sideways = [], [], [[] for _ in range(near)]
     for strip in range(strips):
-        if strip:
-            remote[strip][-1], totals[-1] = after(remote[strip][-1], totals[-1])
+        flip = strip % 2 * (groups // 2)
         keep, send = pl.pallas_call(
-            functools.partial(pair_products, groups, strip),
+            functools.partial(pair_products, groups, strip, flip),
             out_shape=(half_sums, half_sums),
             in_specs=[SMEM] + [VMEM] * (3 + len(remote[strip])),
             out_specs=(VMEM, VMEM),
             compiler_params=pltpu.CompilerParams(vmem_limit_bytes=32 * MIB),
             name="pair_products",
         )(spot, high, low, own_sums, *remote[strip])
+        if strip:
+            send, totals[-1] = after(send, totals[-1])
         for at in range(bits):
             keep, send = halve(keep, send, at)
         total = (keep + send)[0]
         totals.append(total)
-        directs.append(lax.ppermute(total, AXES, mirror))
-        for off in range(1, near):
+        directs.append(lax.ppermute(total, AXES, pairs(lambda r, c: (c // near, (r ^ flip) * near + c % near))))
+        for off in range(near):
             part = lax.dynamic_slice_in_dim(total, (column % near ^ off) * width, width, 0)
-            sideways[off - 1].append(lax.ppermute(part, "cols", [(c, c ^ off) for c in range(columns)]))
-
-    last = totals + directs + [part for side in sideways for part in side]
+            if off or flip:
+                part = lax.ppermute(part, AXES, pairs(lambda r, c: (r ^ flip, c ^ off)))
+            sideways[off].append(part)
+
+    last = directs + [part for side in sideways for part in side]
     return pl.pallas_call(
-        functools.partial(finish, factor, near, strips),
+        functools.partial(finish, factor, strips),
         out_shape=jax.ShapeDtypeStruct((near * width, width), jnp.float32),
         in_specs=[SMEM] + [VMEM] * len(last),
         out_specs=VMEM,

time: 117 us -> 113 us (0.966)
  the two profiles are of different devices: /device:TPU:17 before, /device:TPU:18 now
where the time goes in v5:
time: 113 us
  waiting for transfers between devices  59.3 us (52%)
  Pallas kernels  25.5 us (23%)
  starting transfers between devices  22.7 us (20%)
  local copies, waits for them, and re-layouts  4.19 us (4%)
  other arithmetic  1.24 us (1%)
    ppermute x8, waiting for transfers between devices, halve(): got = lax.ppermute(send, 'rows', [(r, r ^ 1 << at) for r in range(groups)])  26.2 us
    ppermute x6, waiting for transfers between devices, shards(): moving = lax.ppermute(moving, AXES, ring)  18.5 us
    pallas_call x2, Pallas kernels, picked_strip(): pl.pallas_call(functools.partial(transform_and_pick, groups, strip), out_...  16.7 us
    ppermute x3, waiting for transfers between devices, shards(): part = lax.ppermute(part, AXES, pairs(lambda r, c: (r ^ flip, c ^ off)))  11 us
    ppermute x6, starting transfers between devices, shards(): moving = lax.ppermute(moving, AXES, ring)  10.2 us
    pallas_call x2, Pallas kernels, shards(): pl.pallas_call(functools.partial(pair_products, groups, strip, flip), out...  5.21 us
    ppermute x8, starting transfers between devices, halve(): got = lax.ppermute(send, 'rows', [(r, r ^ 1 << at) for r in range(groups)])  4.6 us
    unnamed x4, local copies, waits for them, and re-layouts  4.14 us
  transfers between devices with their start and end apart: 21, of which 15 were waited for; matrix products, arithmetic and copies ran while one was open for 0% of the time, Pallas kernels for 12%

profile of v5, /device:TPU:18, one launch (start us, length us, event | category | flops | bytes accessed | tf_op | source)
XLA Modules:
  0.0 113.1 jit_solution(17139532318902199032)
XLA Ops:
  0.8 3.4 %copy-done = f32[8192,256]{1,0:T(8,128)S(1)} copy-done((f32[8192,256]{1,0:T(8,128)S(1)}, f32[8192,256]{1,0:T(8,128)}, u32[]{:S(2)}) %copy-start) | copy-done | bytes 8388632
  5.0 8.4 %transform_and_pick.2 = (f32[2048,128]{1,0:T(8,128)S(1)}, f32[2048,128]{1,0:T(8,128)S(1)}) custom-call(s32[3]{0:T(128)S(1)} %pad_add_fusion.spot_ref, s32[4096]{0:T(1024)S(1)} %multiply_add_fusion.index_ref, s32[8,8,128]{2,1,0:T(8,128)S(1)} %bitcast.14, f32[8192,256]{1,0:T(8,128)S(1)} %copy-done), custom_call_target="tpu_custom_call" | custom-call | flops 2147483648 | bytes 25165824 | tf_op jit(solution)/shard_map/transform_and_pick/pallas_call | solution.py:95
  13.4 2.6 %collective-permute-done = f32[2048,128]{1,0:T(8,128)S(1)} collective-permute-done((f32[2048,128]{1,0:T(8,128)S(1)}, f32[2048,128]{1,0:T(8,128)S(1)}, u32[]{:S(2)}, u32[]{:S(2)}) %collective-permute-start) | collective-permute-done | bytes 1048608 | tf_op jit(solution)/shard_map/ppermute | solution.py:198
  16.7 8.3 %transform_and_pick.3 = (f32[2048,128]{1,0:T(8,128)S(1)}, f32[2048,128]{1,0:T(8,128)S(1)}) custom-call(s32[3]{0:T(128)S(1)} %pad_add_fusion.spot_ref, s32[4096]{0:T(1024)S(1)} %multiply_add_fusion.index_ref, s32[8,8,128]{2,1,0:T(8,128)S(1)} %bitcast.15, f32[8192,256]{1,0:T(8,128)S(1)} %copy-done), custom_call_target="tpu_custom_call" | custom-call | flops 2147483648 | bytes 25165824 | tf_op jit(solution)/shard_map/transform_and_pick/pallas_call | solution.py:95
  25.1 5.1 %collective-permute-done.1 = f32[1024,128]{1,0:T(8,128)S(1)} collective-permute-done((f32[1024,128]{1,0:T(8,128)S(1)}, f32[1024,128]{1,0:T(8,128)S(1)}, u32[]{:S(2)}, u32[]{:S(2)}) %collective-permute-start.1) | collective-permute-done | bytes 524320 | tf_op jit(solution)/shard_map/ppermute | solution.py:198
  30.3 1.6 %collective-permute-start.4 = (f32[1024,128]{1,0:T(8,128)S(1)}, f32[1024,128]{1,0:T(8,128)S(1)}, u32[]{:S(2)}, u32[]{:S(2)}) collective-permute-start(f32[1024,128]{1,0:T(8,128)S(1)} %fusion.1.refs_0_), channel_id=1, source_target_pairs={{0,2},{1,3},{2,4},{3,5},{4,6},{5,7},{6,14},{7,15},{8,0},{9,1},{10,... | collective-permute-start | bytes 1572872 | tf_op jit(solution)/shard_map/ppermute | solution.py:236
  31.9 1.1 collective-permute-done.2
  33.6 1.5 %collective-permute-start.5 = (f32[1024,128]{1,0:T(8,128)S(1)}, f32[1024,128]{1,0:T(8,128)S(1)}, u32[]{:S(2)}, u32[]{:S(2)}) collective-permute-start(f32[1024,128]{1,0:T(8,128)S(1)} %fusion.1.refs_0_), channel_id=1, source_target_pairs={{0,1},{1,0},{2,3},{3,2},{4,5},{5,4},{6,7},{7,6},{8,9},{9,8},{10,11... | collective-permute-start | bytes 1572872 | tf_op jit(solution)/shard_map/ppermute | solution.py:241
  35.1 4.4 %collective-permute-done.4.refs_0_ = f32[1024,128]{1,0:T(8,128)S(1)} collective-permute-done((f32[1024,128]{1,0:T(8,128)S(1)}, f32[1024,128]{1,0:T(8,128)S(1)}, u32[]{:S(2)}, u32[]{:S(2)}) %collective-permute-start.4) | collective-permute-done | bytes 524320 | tf_op jit(solution)/shard_map/ppermute | solution.py:236
  39.5 1.6 %collective-permute-start.8 = (f32[1024,128]{1,0:T(8,128)S(1)}, f32[1024,128]{1,0:T(8,128)S(1)}, u32[]{:S(2)}, u32[]{:S(2)}) collective-permute-start(f32[1024,128]{1,0:T(8,128)S(1)} %collective-permute-done.4.refs_0_), channel_id=1, source_target_pairs={{0,2},{1,3},{2,4},{3,5},{4,6},{5,7},{6,14},{7,15},{8,0},{9,1},{10,... | collective-permute-start | bytes 1572872 | tf_op jit(solution)/shard_map/ppermute | solution.py:236
  41.1 6.0 %collective-permute-done.3 = f32[1024,128]{1,0:T(8,128)S(1)} collective-permute-done((f32[1024,128]{1,0:T(8,128)S(1)}, f32[1024,128]{1,0:T(8,128)S(1)}, u32[]{:S(2)}, u32[]{:S(2)}) %collective-permute-start.3) | collective-permute-done | bytes 524320 | tf_op jit(solution)/shard_map/ppermute | solution.py:198
  47.4 1.6 %collective-permute-start.7 = (f32[1024,128]{1,0:T(8,128)S(1)}, f32[1024,128]{1,0:T(8,128)S(1)}, u32[]{:S(2)}, u32[]{:S(2)}) collective-permute-start(f32[1024,128]{1,0:T(8,128)S(1)} %fusion.refs_1_), channel_id=1, source_target_pairs={{0,2},{1,3},{2,4},{3,5},{4,6},{5,7},{6,14},{7,15},{8,0},{9,1},{10,... | collective-permute-start | bytes 1572872 | tf_op jit(solution)/shard_map/ppermute | solution.py:236
  49.0 1.3 %collective-permute-start.10 = (f32[1024,128]{1,0:T(8,128)S(1)}, f32[1024,128]{1,0:T(8,128)S(1)}, u32[]{:S(2)}, u32[]{:S(2)}) collective-permute-start(f32[1024,128]{1,0:T(8,128)S(1)} %collective-permute-done.8.refs_1_), channel_id=1, source_target_pairs={{0,2},{1,3},{2,4},{3,5},{4,6},{5,7},{6,14},{7,15},{8,0},{9,1},{10,... | collective-permute-start | bytes 1572872 | tf_op jit(solution)/shard_map/ppermute | solution.py:236
  50.3 1.5 %collective-permute-start.6 = (f32[1024,128]{1,0:T(8,128)S(1)}, f32[1024,128]{1,0:T(8,128)S(1)}, u32[]{:S(2)}, u32[]{:S(2)}) collective-permute-start(f32[1024,128]{1,0:T(8,128)S(1)} %fusion.refs_1_), channel_id=1, source_target_pairs={{0,1},{1,0},{2,3},{3,2},{4,5},{5,4},{6,7},{7,6},{8,9},{9,8},{10,11... | collective-permute-start | bytes 1572872 | tf_op jit(solution)/shard_map/ppermute | solution.py:241
  51.8 4.8 %collective-permute-done.7.refs_0_ = f32[1024,128]{1,0:T(8,128)S(1)} collective-permute-done((f32[1024,128]{1,0:T(8,128)S(1)}, f32[1024,128]{1,0:T(8,128)S(1)}, u32[]{:S(2)}, u32[]{:S(2)}) %collective-permute-start.7) | collective-permute-done | bytes 524320 | tf_op jit(solution)/shard_map/ppermute | solution.py:236
  56.6 1.6 %collective-permute-start.9 = (f32[1024,128]{1,0:T(8,128)S(1)}, f32[1024,128]{1,0:T(8,128)S(1)}, u32[]{:S(2)}, u32[]{:S(2)}) collective-permute-start(f32[1024,128]{1,0:T(8,128)S(1)} %collective-permute-done.7.refs_0_), channel_id=1, source_target_pairs={{0,2},{1,3},{2,4},{3,5},{4,6},{5,7},{6,14},{7,15},{8,0},{9,1},{10,... | collective-permute-start | bytes 1572872 | tf_op jit(solution)/shard_map/ppermute | solution.py:236
  58.2 3.3 %collective-permute-done.6.refs_3_ = f32[1024,128]{1,0:T(8,128)S(1)} collective-permute-done((f32[1024,128]{1,0:T(8,128)S(1)}, f32[1024,128]{1,0:T(8,128)S(1)}, u32[]{:S(2)}, u32[]{:S(2)}) %collective-permute-start.6) | collective-permute-done | bytes 524320 | tf_op jit(solution)/shard_map/ppermute | solution.py:241
  61.5 2.1 %turn_plane.1 = (bf16[512,1024]{1,0:T(8,128)(2,1)S(1)}, bf16[512,1024]{1,0:T(8,128)(2,1)S(1)}, f32[512,256]{1,0:T(8,128)S(1)}) custom-call(s32[3]{0:T(128)S(1)} %pad_add_fusion.spot_ref, f32[1024,128]{1,0:T(8,128)S(1)} %fusion.1.refs_0_, f32[1024,128]{1,0:T(8,128)S(1)} %fusion.refs_1_, f32[1024,128]{1,0:T(8,128)S(1)} %collective-permute-done.5.refs_2_, ...), custom_call_target="tpu_custom_call" | custom-call | tf_op jit(solution)/shard_map/turn_plane/pallas_call | solution.py:246
  63.6 4.2 %collective-permute-done.9.refs_1_ = f32[1024,128]{1,0:T(8,128)S(1)} collective-permute-done((f32[1024,128]{1,0:T(8,128)S(1)}, f32[1024,128]{1,0:T(8,128)S(1)}, u32[]{:S(2)}, u32[]{:S(2)}) %collective-permute-start.9) | collective-permute-done | bytes 524320 | tf_op jit(solution)/shard_map/ppermute | solution.py:236
  67.8 2.6 %pair_products.2 = (f32[2,512,128]{2,1,0:T(8,128)S(1)}, f32[2,512,128]{2,1,0:T(8,128)S(1)}) custom-call(s32[3]{0:T(128)S(1)} %pad_add_fusion.spot_ref, bf16[512,1024]{1,0:T(8,128)(2,1)S(1)} %get-tuple-element.42.high_ref, bf16[512,1024]{1,0:T(8,128)(2,1)S(1)} %get-tuple-element.43.low_ref, f32[512,256]{1,0:T(8,128)S(1)} %get-tuple-element.44.own_ref, ...), custom_call_target="tpu_custom_call" | custom-call | tf_op jit(solution)/shard_map/pair_products/pallas_call | solution.py:259
  70.5 2.6 %collective-permute-start.14 = (f32[1024,128]{1,0:T(8,128)S(1)}, f32[1024,128]{1,0:T(8,128)S(1)}, u32[]{:S(2)}, u32[]{:S(2)}) collective-permute-start(f32[1024,128]{1,0:T(8,128)S(1)} %collective-permute-done.9.refs_1_), channel_id=1, source_target_pairs={{0,2},{1,3},{2,4},{3,5},{4,6},{5,7},{6,14},{7,15},{8,0},{9,1},{10,... | collective-permute-start | bytes 1572872 | tf_op jit(solution)/shard_map/ppermute | solution.py:236
  73.1 1.6 %collective-permute-start.12 = (f32[1,512,128]{2,1,0:T(8,128)S(1)}, f32[1,512,128]{2,1,0:T(8,128)S(1)}, u32[]{:S(2)}, u32[]{:S(2)}) collective-permute-start(f32[1,512,128]{2,1,0:T(8,128)S(1)} %slice_add_fusion.6), channel_id=1, source_target_pairs={{0,16},{8,24},{16,0},{24,8},{1,17},{9,25},{17,1},{25,9},{2,18},{10... | collective-permute-start | bytes 786440 | tf_op jit(solution)/shard_map/ppermute | solution.py:198
  74.7 5.1 %collective-permute-done.14.refs_2_ = f32[1024,128]{1,0:T(8,128)S(1)} collective-permute-done((f32[1024,128]{1,0:T(8,128)S(1)}, f32[1024,128]{1,0:T(8,128)S(1)}, u32[]{:S(2)}, u32[]{:S(2)}) %collective-permute-start.14) | collective-permute-done | bytes 524320 | tf_op jit(solution)/shard_map/ppermute | solution.py:236
  79.8 2.6 %pair_products.3 = (f32[2,512,128]{2,1,0:T(8,128)S(1)}, f32[2,512,128]{2,1,0:T(8,128)S(1)}) custom-call(s32[3]{0:T(128)S(1)} %pad_add_fusion.spot_ref, bf16[512,1024]{1,0:T(8,128)(2,1)S(1)} %get-tuple-element.42.high_ref, bf16[512,1024]{1,0:T(8,128)(2,1)S(1)} %get-tuple-element.43.low_ref, f32[512,256]{1,0:T(8,128)S(1)} %get-tuple-element.44.own_ref, ...), custom_call_target="tpu_custom_call" | custom-call | tf_op jit(solution)/shard_map/pair_products/pallas_call | solution.py:259
  82.5 1.9 %collective-permute-done.15 = f32[2,512,128]{2,1,0:T(8,128)S(1)} collective-permute-done((f32[2,512,128]{2,1,0:T(8,128)S(1)}, f32[2,512,128]{2,1,0:T(8,128)S(1)}, u32[]{:S(2)}, u32[]{:S(2)}) %collective-permute-start.15) | collective-permute-done | bytes 524320 | tf_op jit(solution)/shard_map/ppermute | solution.py:198
  84.5 1.6 %collective-permute-start.16 = (f32[1,512,128]{2,1,0:T(8,128)S(1)}, f32[1,512,128]{2,1,0:T(8,128)S(1)}, u32[]{:S(2)}, u32[]{:S(2)}) collective-permute-start(f32[1,512,128]{2,1,0:T(8,128)S(1)} %slice_add_fusion.4), channel_id=1, source_target_pairs={{0,16},{8,24},{16,0},{24,8},{1,17},{9,25},{17,1},{25,9},{2,18},{10... | collective-permute-start | bytes 786440 | tf_op jit(solution)/shard_map/ppermute | solution.py:198
  86.7 9.6 %collective-permute-done.16 = f32[1,512,128]{2,1,0:T(8,128)S(1)} collective-permute-done((f32[1,512,128]{2,1,0:T(8,128)S(1)}, f32[1,512,128]{2,1,0:T(8,128)S(1)}, u32[]{:S(2)}, u32[]{:S(2)}) %collective-permute-start.16) | collective-permute-done | bytes 262176 | tf_op jit(solution)/shard_map/ppermute | solution.py:198
  96.4 1.6 %collective-permute-start.19 = (f32[256,128]{1,0:T(8,128)S(1)}, f32[256,128]{1,0:T(8,128)S(1)}, u32[]{:S(2)}, u32[]{:S(2)}) collective-permute-start(f32[256,128]{1,0:T(8,128)S(1)} %get-tuple-element.57), channel_id=1, source_target_pairs={{0,1},{1,0},{2,3},{3,2},{4,5},{5,4},{6,7},{7,6},{8,9},{9,8},{10,11... | collective-permute-start | bytes 393224 | tf_op jit(solution)/shard_map/ppermute | solution.py:277
  98.0 2.5 %collective-permute-start.18 = (f32[256,128]{1,0:T(8,128)S(1)}, f32[256,128]{1,0:T(8,128)S(1)}, u32[]{:S(2)}, u32[]{:S(2)}) collective-permute-start(f32[256,128]{1,0:T(8,128)S(1)} %get-tuple-element.56), channel_id=1, source_target_pairs={{0,16},{1,17},{2,18},{3,19},{4,20},{5,21},{6,22},{7,23},{8,24},{9,... | collective-permute-start | bytes 393224 | tf_op jit(solution)/shard_map/ppermute | solution.py:277
  101.4 7.9 %collective-permute-done.18.refs_3_ = f32[256,128]{1,0:T(8,128)S(1)} collective-permute-done((f32[256,128]{1,0:T(8,128)S(1)}, f32[256,128]{1,0:T(8,128)S(1)}, u32[]{:S(2)}, u32[]{:S(2)}) %collective-permute-start.18) | collective-permute-done | bytes 131104 | tf_op jit(solution)/shard_map/ppermute | solution.py:277
  109.3 2.2 %collective-permute-done.20.refs_5_ = f32[256,128]{1,0:T(8,128)S(1)} collective-permute-done((f32[256,128]{1,0:T(8,128)S(1)}, f32[256,128]{1,0:T(8,128)S(1)}, u32[]{:S(2)}, u32[]{:S(2)}) %collective-permute-start.20) | collective-permute-done | bytes 131104 | tf_op jit(solution)/shard_map/ppermute | solution.py:277
  111.5 1.5 %finish.1 = f32[512,256]{1,0:T(8,128)} custom-call(s32[3]{0:T(128)S(1)} %pad_add_fusion.spot_ref, f32[512,128]{1,0:T(8,128)S(1)} %collective-permute-done.13.refs_0_, f32[512,128]{1,0:T(8,128)S(1)} %collective-permute-done.17.refs_1_, f32[256,128]{1,0:T(8,128)S(1)} %get-tuple-element.58.refs_2_, f32[256,128]{1,0:T(8,128)S(1)} %collective-permute-done.18.refs_3_, ...), custom_call_target="tpu_custom_call" | custom-call | tf_op jit(solution)/shard_map/finish/pallas_call | solution.py:281
  (32 shorter events, 5.4 us)
Async XLA Ops:
  0.8 3.4 %copy-start = (f32[8192,256]{1,0:T(8,128)S(1)}, f32[8192,256]{1,0:T(8,128)}, u32[]{:S(2)}) copy-start(f32[8192,256]{1,0:T(8,128)} %slab_ref.3) | copy-start | bytes 25165828
  4.2 0.8 copy-start.1
  13.3 2.7 %collective-permute-start = (f32[2048,128]{1,0:T(8,128)S(1)}, f32[2048,128]{1,0:T(8,128)S(1)}, u32[]{:S(2)}, u32[]{:S(2)}) collective-permute-start(f32[2048,128]{1,0:T(8,128)S(1)} %get-tuple-element.31), channel_id=1, source_target_pairs={{0,8},{8,0},{16,24},{24,16},{1,9},{9,1},{17,25},{25,17},{2,10},{10... | collective-permute-start | bytes 3145736 | tf_op jit(solution)/shard_map/ppermute | solution.py:198
  16.1 14.0 %collective-permute-start.1 = (f32[1024,128]{1,0:T(8,128)S(1)}, f32[1024,128]{1,0:T(8,128)S(1)}, u32[]{:S(2)}, u32[]{:S(2)}) collective-permute-start(f32[1024,128]{1,0:T(8,128)S(1)} %slice_add_fusion.3), channel_id=1, source_target_pairs={{0,16},{8,24},{16,0},{24,8},{1,17},{9,25},{17,1},{25,9},{2,18},{10... | collective-permute-start | bytes 1572872 | tf_op jit(solution)/shard_map/ppermute | solution.py:198
  30.2 2.7 %collective-permute-start.2 = (f32[2048,128]{1,0:T(8,128)S(1)}, f32[2048,128]{1,0:T(8,128)S(1)}, u32[]{:S(2)}, u32[]{:S(2)}) collective-permute-start(f32[2048,128]{1,0:T(8,128)S(1)} %get-tuple-element.37), channel_id=1, source_target_pairs={{0,8},{8,0},{16,24},{24,16},{1,9},{9,1},{17,25},{25,17},{2,10},{10... | collective-permute-start | bytes 3145736 | tf_op jit(solution)/shard_map/ppermute | solution.py:198
  30.3 9.2 %collective-permute-start.4 = (f32[1024,128]{1,0:T(8,128)S(1)}, f32[1024,128]{1,0:T(8,128)S(1)}, u32[]{:S(2)}, u32[]{:S(2)}) collective-permute-start(f32[1024,128]{1,0:T(8,128)S(1)} %fusion.1.refs_0_), channel_id=1, source_target_pairs={{0,2},{1,3},{2,4},{3,5},{4,6},{5,7},{6,14},{7,15},{8,0},{9,1},{10,... | collective-permute-start | bytes 1572872 | tf_op jit(solution)/shard_map/ppermute | solution.py:236
  33.0 14.0 %collective-permute-start.3 = (f32[1024,128]{1,0:T(8,128)S(1)}, f32[1024,128]{1,0:T(8,128)S(1)}, u32[]{:S(2)}, u32[]{:S(2)}) collective-permute-start(f32[1024,128]{1,0:T(8,128)S(1)} %slice_add_fusion), channel_id=1, source_target_pairs={{0,16},{8,24},{16,0},{24,8},{1,17},{9,25},{17,1},{25,9},{2,18},{10... | collective-permute-start | bytes 1572872 | tf_op jit(solution)/shard_map/ppermute | solution.py:198
  33.6 13.7 %collective-permute-start.5 = (f32[1024,128]{1,0:T(8,128)S(1)}, f32[1024,128]{1,0:T(8,128)S(1)}, u32[]{:S(2)}, u32[]{:S(2)}) collective-permute-start(f32[1024,128]{1,0:T(8,128)S(1)} %fusion.1.refs_0_), channel_id=1, source_target_pairs={{0,1},{1,0},{2,3},{3,2},{4,5},{5,4},{6,7},{7,6},{8,9},{9,8},{10,11... | collective-permute-start | bytes 1572872 | tf_op jit(solution)/shard_map/ppermute | solution.py:241
  39.5 9.5 %collective-permute-start.8 = (f32[1024,128]{1,0:T(8,128)S(1)}, f32[1024,128]{1,0:T(8,128)S(1)}, u32[]{:S(2)}, u32[]{:S(2)}) collective-permute-start(f32[1024,128]{1,0:T(8,128)S(1)} %collective-permute-done.4.refs_0_), channel_id=1, source_target_pairs={{0,2},{1,3},{2,4},{3,5},{4,6},{5,7},{6,14},{7,15},{8,0},{9,1},{10,... | collective-permute-start | bytes 1572872 | tf_op jit(solution)/shard_map/ppermute | solution.py:236
  47.4 9.2 %collective-permute-start.7 = (f32[1024,128]{1,0:T(8,128)S(1)}, f32[1024,128]{1,0:T(8,128)S(1)}, u32[]{:S(2)}, u32[]{:S(2)}) collective-permute-start(f32[1024,128]{1,0:T(8,128)S(1)} %fusion.refs_1_), channel_id=1, source_target_pairs={{0,2},{1,3},{2,4},{3,5},{4,6},{5,7},{6,14},{7,15},{8,0},{9,1},{10,... | collective-permute-start | bytes 1572872 | tf_op jit(solution)/shard_map/ppermute | solution.py:236
  49.0 14.6 %collective-permute-start.10 = (f32[1024,128]{1,0:T(8,128)S(1)}, f32[1024,128]{1,0:T(8,128)S(1)}, u32[]{:S(2)}, u32[]{:S(2)}) collective-permute-start(f32[1024,128]{1,0:T(8,128)S(1)} %collective-permute-done.8.refs_1_), channel_id=1, source_target_pairs={{0,2},{1,3},{2,4},{3,5},{4,6},{5,7},{6,14},{7,15},{8,0},{9,1},{10,... | collective-permute-start | bytes 1572872 | tf_op jit(solution)/shard_map/ppermute | solution.py:236
  50.3 11.2 %collective-permute-start.6 = (f32[1024,128]{1,0:T(8,128)S(1)}, f32[1024,128]{1,0:T(8,128)S(1)}, u32[]{:S(2)}, u32[]{:S(2)}) collective-permute-start(f32[1024,128]{1,0:T(8,128)S(1)} %fusion.refs_1_), channel_id=1, source_target_pairs={{0,1},{1,0},{2,3},{3,2},{4,5},{5,4},{6,7},{7,6},{8,9},{9,8},{10,11... | collective-permute-start | bytes 1572872 | tf_op jit(solution)/shard_map/ppermute | solution.py:241
  56.6 11.2 %collective-permute-start.9 = (f32[1024,128]{1,0:T(8,128)S(1)}, f32[1024,128]{1,0:T(8,128)S(1)}, u32[]{:S(2)}, u32[]{:S(2)}) collective-permute-start(f32[1024,128]{1,0:T(8,128)S(1)} %collective-permute-done.7.refs_0_), channel_id=1, source_target_pairs={{0,2},{1,3},{2,4},{3,5},{4,6},{5,7},{6,14},{7,15},{8,0},{9,1},{10,... | collective-permute-start | bytes 1572872 | tf_op jit(solution)/shard_map/ppermute | solution.py:236
  70.4 2.6 %collective-permute-start.11 = (f32[2,512,128]{2,1,0:T(8,128)S(1)}, f32[2,512,128]{2,1,0:T(8,128)S(1)}, u32[]{:S(2)}, u32[]{:S(2)}) collective-permute-start(f32[2,512,128]{2,1,0:T(8,128)S(1)} %get-tuple-element.50), channel_id=1, source_target_pairs={{0,8},{8,0},{16,24},{24,16},{1,9},{9,1},{17,25},{25,17},{2,10},{10... | collective-permute-start | bytes 1572872 | tf_op jit(solution)/shard_map/ppermute | solution.py:198
  70.5 9.3 %collective-permute-start.14 = (f32[1024,128]{1,0:T(8,128)S(1)}, f32[1024,128]{1,0:T(8,128)S(1)}, u32[]{:S(2)}, u32[]{:S(2)}) collective-permute-start(f32[1024,128]{1,0:T(8,128)S(1)} %collective-permute-done.9.refs_1_), channel_id=1, source_target_pairs={{0,2},{1,3},{2,4},{3,5},{4,6},{5,7},{6,14},{7,15},{8,0},{9,1},{10,... | collective-permute-start | bytes 1572872 | tf_op jit(solution)/shard_map/ppermute | solution.py:236
  73.1 9.3 %collective-permute-start.12 = (f32[1,512,128]{2,1,0:T(8,128)S(1)}, f32[1,512,128]{2,1,0:T(8,128)S(1)}, u32[]{:S(2)}, u32[]{:S(2)}) collective-permute-start(f32[1,512,128]{2,1,0:T(8,128)S(1)} %slice_add_fusion.6), channel_id=1, source_target_pairs={{0,16},{8,24},{16,0},{24,8},{1,17},{9,25},{17,1},{25,9},{2,18},{10... | collective-permute-start | bytes 786440 | tf_op jit(solution)/shard_map/ppermute | solution.py:198
  82.4 2.0 %collective-permute-start.15 = (f32[2,512,128]{2,1,0:T(8,128)S(1)}, f32[2,512,128]{2,1,0:T(8,128)S(1)}, u32[]{:S(2)}, u32[]{:S(2)}) collective-permute-start(f32[2,512,128]{2,1,0:T(8,128)S(1)} %get-tuple-element.54), channel_id=1, source_target_pairs={{0,8},{8,0},{16,24},{24,16},{1,9},{9,1},{17,25},{25,17},{2,10},{10... | collective-permute-start | bytes 1572872 | tf_op jit(solution)/shard_map/ppermute | solution.py:198
  84.5 11.8 %collective-permute-start.16 = (f32[1,512,128]{2,1,0:T(8,128)S(1)}, f32[1,512,128]{2,1,0:T(8,128)S(1)}, u32[]{:S(2)}, u32[]{:S(2)}) collective-permute-start(f32[1,512,128]{2,1,0:T(8,128)S(1)} %slice_add_fusion.4), channel_id=1, source_target_pairs={{0,16},{8,24},{16,0},{24,8},{1,17},{9,25},{17,1},{25,9},{2,18},{10... | collective-permute-start | bytes 786440 | tf_op jit(solution)/shard_map/ppermute | solution.py:198
  86.0 15.4 %collective-permute-start.13 = (f32[512,128]{1,0:T(8,128)S(1)}, f32[512,128]{1,0:T(8,128)S(1)}, u32[]{:S(2)}, u32[]{:S(2)}) collective-permute-start(f32[512,128]{1,0:T(8,128)S(1)} %bitcast.16), channel_id=1, source_target_pairs={{0,0},{1,1},{2,8},{3,9},{4,16},{5,17},{6,24},{7,25},{8,2},{9,3},{1... | collective-permute-start | bytes 786440 | tf_op jit(solution)/shard_map/ppermute | solution.py:273
  96.3 15.2 %collective-permute-start.17 = (f32[512,128]{1,0:T(8,128)S(1)}, f32[512,128]{1,0:T(8,128)S(1)}, u32[]{:S(2)}, u32[]{:S(2)}) collective-permute-start(f32[512,128]{1,0:T(8,128)S(1)} %bitcast.17), channel_id=1, source_target_pairs={{0,4},{1,5},{2,12},{3,13},{4,20},{5,21},{6,28},{7,29},{8,6},{9,7},... | collective-permute-start | bytes 786440 | tf_op jit(solution)/shard_map/ppermute | solution.py:273
  96.4 5.0 %collective-permute-start.19 = (f32[256,128]{1,0:T(8,128)S(1)}, f32[256,128]{1,0:T(8,128)S(1)}, u32[]{:S(2)}, u32[]{:S(2)}) collective-permute-start(f32[256,128]{1,0:T(8,128)S(1)} %get-tuple-element.57), channel_id=1, source_target_pairs={{0,1},{1,0},{2,3},{3,2},{4,5},{5,4},{6,7},{7,6},{8,9},{9,8},{10,11... | collective-permute-start | bytes 393224 | tf_op jit(solution)/shard_map/ppermute | solution.py:277
  98.0 11.3 %collective-permute-start.18 = (f32[256,128]{1,0:T(8,128)S(1)}, f32[256,128]{1,0:T(8,128)S(1)}, u32[]{:S(2)}, u32[]{:S(2)}) collective-permute-start(f32[256,128]{1,0:T(8,128)S(1)} %get-tuple-element.56), channel_id=1, source_target_pairs={{0,16},{1,17},{2,18},{3,19},{4,20},{5,21},{6,22},{7,23},{8,24},{9,... | collective-permute-start | bytes 393224 | tf_op jit(solution)/shard_map/ppermute | solution.py:277
  100.5 11.0 %collective-permute-start.20 = (f32[256,128]{1,0:T(8,128)S(1)}, f32[256,128]{1,0:T(8,128)S(1)}, u32[]{:S(2)}, u32[]{:S(2)}) collective-permute-start(f32[256,128]{1,0:T(8,128)S(1)} %get-tuple-element.55), channel_id=1, source_target_pairs={{0,17},{1,16},{2,19},{3,18},{4,21},{5,20},{6,23},{7,22},{8,25},{9,... | collective-permute-start | bytes 393224 | tf_op jit(solution)/shard_map/ppermute | solution.py:277

commit v6 on v5

--- a/solution.py
+++ b/solution.py
@@ -67,20 +67,23 @@
     def _(tile):
         combine([at * block + tile * 8 for at in range(steps)], True)
 
+    gather(groups, groups // 2, spot_ref, index_ref, mixed, send_ref)
+    if keep_ref is not None:
+        gather(groups, 0, spot_ref, index_ref, mixed, keep_ref)
+
+
+def gather(groups, first, spot_ref, index_ref, mixed, out_ref):
     count = index_ref.shape[0] // groups
     bits = groups.bit_length() - 1
-    half = groups // 2
     unroll = min(128, count)
-    for place in range(groups):
-        out = keep_ref if place < half else send_ref
-        start = (spot_ref[0] ^ bit_reverse(place, bits)) * count
-        to = (place % half) * count
+    for place in range(groups // 2):
+        start = (spot_ref[0] ^ bit_reverse(first + place, bits)) * count
 
         @pl.loop(0, count // unroll)
         def _(chunk):
             for at in range(unroll):
                 source = index_ref[start + chunk * unroll + at]
-                out[pl.ds(to + chunk * unroll + at, 1), :] = mixed[pl.ds(source, 1), :]
+                out_ref[pl.ds(place * count + chunk * unroll + at, 1), :] = mixed[pl.ds(source, 1), :]
 
 
 VMEM = pl.BlockSpec(memory_space=pltpu.VMEM)
@@ -92,18 +95,35 @@
     height = slab.shape[0]
     samples = index.shape[0]
     half = jax.ShapeDtypeStruct((samples // 2, LANES), jnp.float32)
-    return pl.pallas_call(
-        functools.partial(transform_and_pick, groups, strip),
-        out_shape=(half, half),
+    table = jax.ShapeDtypeStruct((2 * height, LANES), jnp.float32)
+    transform = functools.partial(transform_and_pick, groups, strip)
+    if strip:
+        kernel, out_shape, scratch = transform, (half, half), [pltpu.VMEM(table.shape, table.dtype)]
+    else:
+        kernel, out_shape, scratch = lambda *refs: transform(*refs[:4], None, *refs[4:]), (half, table), []
+    first, second = pl.pallas_call(
+        kernel,
+        out_shape=out_shape,
         in_specs=[SMEM, SMEM, VMEM, VMEM],
         out_specs=(VMEM, VMEM),
-        scratch_shapes=[pltpu.VMEM((2 * height, LANES), jnp.float32)],
+        scratch_shapes=scratch,
         compiler_params=pltpu.CompilerParams(vmem_limit_bytes=32 * MIB),
         cost_estimate=pl.CostEstimate(
             flops=16 * height * INNER * LANES, bytes_accessed=16 * LANES * (height + samples), transcendentals=0
         ),
         name="transform_and_pick",
     )(spot, index, sign_bits, slab)
+    if strip:
+        return first, second
+    keep = pl.pallas_call(
+        functools.partial(gather, groups, 0),
+        out_shape=half,
+        in_specs=[SMEM, SMEM, VMEM],
+        out_specs=VMEM,
+        compiler_params=pltpu.CompilerParams(vmem_limit_bytes=32 * MIB),
+        name="pick",
+    )(spot, index, second)
+    return keep, first
 
 
 def two_parts(values):
@@ -113,7 +133,9 @@
 
 def three_products(left, right):
     dot = functools.partial(jnp.dot, preferred_element_type=jnp.float32)
-    return dot(left[0], right[0]) + dot(left[0], right[1]) + dot(left[1], right[0])
+    width = right[0].shape[1]
+    both = dot(left[0], jnp.concatenate(right, axis=1))
+    return both[:, :width] + both[:, width:] + dot(left[1], right[0])
 
 
 def turn_plane(near, strips, spot_ref, *refs):
@@ -215,7 +237,7 @@
     ring = pairs(onward)
 
     plane = [[] for _ in range(near)]
-    remote = []
+    remote, onward_parts = [], []
     for strip in range(strips):
         keep, send = picked_strip(slab, sign_bits, index, spot, groups, strip)
         if strip:
@@ -230,11 +252,14 @@
                 send, side[-1] = after(send, side[-1])
         own = keep + send
         moving, passed = own, []
-        for away in range(1, groups):
+        for away in range(1, groups - 1 if strip else groups):
             if strip and away > 1:
                 moving, remote[-1][away - 1] = after(moving, remote[-1][away - 1])
             moving = lax.ppermute(moving, AXES, ring)
             passed.append(moving)
+        if strip:
+            moving, remote[-1][-1] = after(moving, remote[-1][-1])
+        onward_parts.append(moving)
         remote.append(passed)
         plane[0].append(own)
         for off in range(1, near):
@@ -264,6 +289,9 @@
             compiler_params=pltpu.CompilerParams(vmem_limit_bytes=32 * MIB),
             name="pair_products",
         )(spot, high, low, own_sums, *remote[strip])
+        if strip + 1 < strips:
+            moving, send = after(onward_parts[strip + 1], send)
+            remote[strip + 1].append(lax.ppermute(moving, AXES, ring))
         if strip:
             send, totals[-1] = after(send, totals[-1])
         for at in range(bits):

time: 113 us -> 111 us (0.982)
  waiting for transfers between devices: 59.3 us -> 57.1 us
    ppermute x0 -> x1, waiting for transfers between devices: none -> 5.31 us  [shards(): remote[strip + 1].append(lax.ppermute(moving, AXES, ring))]
    ppermute x6 -> x5, waiting for transfers between devices: 18.5 us -> 13.4 us  [shards(): moving = lax.ppermute(moving, AXES, ring)]
    ppermute x6 -> x5, starting transfers between devices: 10.2 us -> 7.63 us  [shards(): moving = lax.ppermute(moving, AXES, ring)]
    ppermute x8, waiting for transfers between devices: 26.2 us -> 23.8 us  [halve(): got = lax.ppermute(send, 'rows', [(r, r ^ 1 << at) for r in range(groups)])]
    ppermute x0 -> x1, starting transfers between devices: none -> 2.29 us  [shards(): remote[strip + 1].append(lax.ppermute(moving, AXES, ring))]
    pallas_call x2 -> x3, Pallas kernels: 16.7 us -> 17.5 us  [the longest x2 15 us: picked_strip(): pl.pallas_call(kernel, out_shape=out_shape, in_specs=[SMEM, SMEM, VMEM, V...]
    unnamed x4 -> x8, local copies, waits for them, and re-layouts: 4.14 us -> 4.15 us
  transfers between devices with their start and end apart: 21 -> 21, of which waited for: 15 -> 15; matrix products, arithmetic and copies ran while one was open for 0% -> 0% of each run, Pallas kernels for 12% -> 14%
where the time goes in v6:
time: 111 us
  waiting for transfers between devices  57.1 us (51%)
  Pallas kernels  25.3 us (23%)
  starting transfers between devices  22.5 us (20%)
  local copies, waits for them, and re-layouts  4.2 us (4%)
  other arithmetic  1.24 us (1%)
    ppermute x8, waiting for transfers between devices, halve(): got = lax.ppermute(send, 'rows', [(r, r ^ 1 << at) for r in range(groups)])  23.8 us
    pallas_call x2, Pallas kernels, picked_strip(): pl.pallas_call(kernel, out_shape=out_shape, in_specs=[SMEM, SMEM, VMEM, V...  15 us
    ppermute x5, waiting for transfers between devices, shards(): moving = lax.ppermute(moving, AXES, ring)  13.4 us
    ppermute x3, waiting for transfers between devices, shards(): part = lax.ppermute(part, AXES, pairs(lambda r, c: (r ^ flip, c ^ off)))  11 us
    ppermute x5, starting transfers between devices, shards(): moving = lax.ppermute(moving, AXES, ring)  7.63 us
    ppermute x1, waiting for transfers between devices, shards(): remote[strip + 1].append(lax.ppermute(moving, AXES, ring))  5.31 us
    ppermute x8, starting transfers between devices, halve(): got = lax.ppermute(send, 'rows', [(r, r ^ 1 << at) for r in range(groups)])  4.61 us
    pallas_call x2, Pallas kernels, shards(): pl.pallas_call(functools.partial(pair_products, groups, strip, flip), out...  4.16 us
  transfers between devices with their start and end apart: 21, of which 15 were waited for; matrix products, arithmetic and copies ran while one was open for 0% of the time, Pallas kernels for 14%

profile of v6, /device:TPU:18, one launch (start us, length us, event | category | flops | bytes accessed | tf_op | source)
XLA Modules:
  0.0 110.5 jit_solution(3978986579299691147)
XLA Ops:
  0.8 3.4 %copy-done = f32[8192,256]{1,0:T(8,128)S(1)} copy-done((f32[8192,256]{1,0:T(8,128)S(1)}, f32[8192,256]{1,0:T(8,128)}, u32[]{:S(2)}) %copy-start) | copy-done | bytes 8388632
  5.0 6.7 %transform_and_pick.2 = (f32[2048,128]{1,0:T(8,128)S(1)}, f32[16384,128]{1,0:T(8,128)S(1)}) custom-call(s32[3]{0:T(128)S(1)} %pad_add_fusion.refs_0_.spot_ref, s32[4096]{0:T(1024)S(1)} %multiply_add_fusion.refs_1_.index_ref, s32[8,8,128]{2,1,0:T(8,128)S(1)} %bitcast.16, f32[8192,256]{1,0:T(8,128)S(1)} %copy-done), custom_call_target="tpu_custom_call" | custom-call | flops 2147483648 | bytes 25165824 | tf_op jit(solution)/shard_map/transform_and_pick/pallas_call | solution.py:104
  11.7 2.5 %pick.1 = f32[2048,128]{1,0:T(8,128)S(1)} custom-call(s32[3]{0:T(128)S(1)} %pad_add_fusion.refs_0_.spot_ref, s32[4096]{0:T(1024)S(1)} %multiply_add_fusion.refs_1_.index_ref, f32[16384,128]{1,0:T(8,128)S(1)} %get-tuple-element.32.mixed), custom_call_target="tpu_custom_call" | custom-call | tf_op jit(solution)/shard_map/pick/pallas_call | solution.py:118
  15.1 8.3 %transform_and_pick.3 = (f32[2048,128]{1,0:T(8,128)S(1)}, f32[2048,128]{1,0:T(8,128)S(1)}) custom-call(s32[3]{0:T(128)S(1)} %pad_add_fusion.refs_0_.spot_ref, s32[4096]{0:T(1024)S(1)} %multiply_add_fusion.refs_1_.index_ref, s32[8,8,128]{2,1,0:T(8,128)S(1)} %bitcast.17, f32[8192,256]{1,0:T(8,128)S(1)} %bitcast.15), custom_call_target="tpu_custom_call" | custom-call | flops 2147483648 | bytes 25165824 | tf_op jit(solution)/shard_map/transform_and_pick/pallas_call | solution.py:104
  23.4 5.3 %collective-permute-done.1 = f32[1024,128]{1,0:T(8,128)S(1)} collective-permute-done((f32[1024,128]{1,0:T(8,128)S(1)}, f32[1024,128]{1,0:T(8,128)S(1)}, u32[]{:S(2)}, u32[]{:S(2)}) %collective-permute-start.1) | collective-permute-done | bytes 524320 | tf_op jit(solution)/shard_map/ppermute | solution.py:220
  28.9 1.6 %collective-permute-start.4 = (f32[1024,128]{1,0:T(8,128)S(1)}, f32[1024,128]{1,0:T(8,128)S(1)}, u32[]{:S(2)}, u32[]{:S(2)}) collective-permute-start(f32[1024,128]{1,0:T(8,128)S(1)} %fusion.1.refs_0_), channel_id=1, source_target_pairs={{0,2},{1,3},{2,4},{3,5},{4,6},{5,7},{6,14},{7,15},{8,0},{9,1},{10,... | collective-permute-start | bytes 1572872 | tf_op jit(solution)/shard_map/ppermute | solution.py:258
  30.5 1.1 collective-permute-done.2
  32.2 1.5 %collective-permute-start.5 = (f32[1024,128]{1,0:T(8,128)S(1)}, f32[1024,128]{1,0:T(8,128)S(1)}, u32[]{:S(2)}, u32[]{:S(2)}) collective-permute-start(f32[1024,128]{1,0:T(8,128)S(1)} %fusion.1.refs_0_), channel_id=1, source_target_pairs={{0,1},{1,0},{2,3},{3,2},{4,5},{5,4},{6,7},{7,6},{8,9},{9,8},{10,11... | collective-permute-start | bytes 1572872 | tf_op jit(solution)/shard_map/ppermute | solution.py:266
  33.7 4.4 %collective-permute-done.4.refs_0_ = f32[1024,128]{1,0:T(8,128)S(1)} collective-permute-done((f32[1024,128]{1,0:T(8,128)S(1)}, f32[1024,128]{1,0:T(8,128)S(1)}, u32[]{:S(2)}, u32[]{:S(2)}) %collective-permute-start.4) | collective-permute-done | bytes 524320 | tf_op jit(solution)/shard_map/ppermute | solution.py:258
  38.1 1.6 %collective-permute-start.8 = (f32[1024,128]{1,0:T(8,128)S(1)}, f32[1024,128]{1,0:T(8,128)S(1)}, u32[]{:S(2)}, u32[]{:S(2)}) collective-permute-start(f32[1024,128]{1,0:T(8,128)S(1)} %collective-permute-done.4.refs_0_), channel_id=1, source_target_pairs={{0,2},{1,3},{2,4},{3,5},{4,6},{5,7},{6,14},{7,15},{8,0},{9,1},{10,... | collective-permute-start | bytes 1572872 | tf_op jit(solution)/shard_map/ppermute | solution.py:258
  39.6 6.0 %collective-permute-done.3 = f32[1024,128]{1,0:T(8,128)S(1)} collective-permute-done((f32[1024,128]{1,0:T(8,128)S(1)}, f32[1024,128]{1,0:T(8,128)S(1)}, u32[]{:S(2)}, u32[]{:S(2)}) %collective-permute-start.3) | collective-permute-done | bytes 524320 | tf_op jit(solution)/shard_map/ppermute | solution.py:220
  45.9 1.6 %collective-permute-start.7 = (f32[1024,128]{1,0:T(8,128)S(1)}, f32[1024,128]{1,0:T(8,128)S(1)}, u32[]{:S(2)}, u32[]{:S(2)}) collective-permute-start(f32[1024,128]{1,0:T(8,128)S(1)} %fusion.refs_1_), channel_id=1, source_target_pairs={{0,2},{1,3},{2,4},{3,5},{4,6},{5,7},{6,14},{7,15},{8,0},{9,1},{10,... | collective-permute-start | bytes 1572872 | tf_op jit(solution)/shard_map/ppermute | solution.py:258
  47.5 1.3 %collective-permute-start.10 = (f32[1024,128]{1,0:T(8,128)S(1)}, f32[1024,128]{1,0:T(8,128)S(1)}, u32[]{:S(2)}, u32[]{:S(2)}) collective-permute-start(f32[1024,128]{1,0:T(8,128)S(1)} %collective-permute-done.8.refs_1_), channel_id=1, source_target_pairs={{0,2},{1,3},{2,4},{3,5},{4,6},{5,7},{6,14},{7,15},{8,0},{9,1},{10,... | collective-permute-start | bytes 1572872 | tf_op jit(solution)/shard_map/ppermute | solution.py:258
  48.8 1.5 %collective-permute-start.6 = (f32[1024,128]{1,0:T(8,128)S(1)}, f32[1024,128]{1,0:T(8,128)S(1)}, u32[]{:S(2)}, u32[]{:S(2)}) collective-permute-start(f32[1024,128]{1,0:T(8,128)S(1)} %fusion.refs_1_), channel_id=1, source_target_pairs={{0,1},{1,0},{2,3},{3,2},{4,5},{5,4},{6,7},{7,6},{8,9},{9,8},{10,11... | collective-permute-start | bytes 1572872 | tf_op jit(solution)/shard_map/ppermute | solution.py:266
  50.3 4.8 %collective-permute-done.7.refs_0_ = f32[1024,128]{1,0:T(8,128)S(1)} collective-permute-done((f32[1024,128]{1,0:T(8,128)S(1)}, f32[1024,128]{1,0:T(8,128)S(1)}, u32[]{:S(2)}, u32[]{:S(2)}) %collective-permute-start.7) | collective-permute-done | bytes 524320 | tf_op jit(solution)/shard_map/ppermute | solution.py:258
  55.1 1.6 %collective-permute-start.9 = (f32[1024,128]{1,0:T(8,128)S(1)}, f32[1024,128]{1,0:T(8,128)S(1)}, u32[]{:S(2)}, u32[]{:S(2)}) collective-permute-start(f32[1024,128]{1,0:T(8,128)S(1)} %collective-permute-done.7.refs_0_), channel_id=1, source_target_pairs={{0,2},{1,3},{2,4},{3,5},{4,6},{5,7},{6,14},{7,15},{8,0},{9,1},{10,... | collective-permute-start | bytes 1572872 | tf_op jit(solution)/shard_map/ppermute | solution.py:258
  56.7 3.3 %collective-permute-done.6.refs_3_ = f32[1024,128]{1,0:T(8,128)S(1)} collective-permute-done((f32[1024,128]{1,0:T(8,128)S(1)}, f32[1024,128]{1,0:T(8,128)S(1)}, u32[]{:S(2)}, u32[]{:S(2)}) %collective-permute-start.6) | collective-permute-done | bytes 524320 | tf_op jit(solution)/shard_map/ppermute | solution.py:266
  60.0 2.1 %turn_plane.1 = (bf16[512,1024]{1,0:T(8,128)(2,1)S(1)}, bf16[512,1024]{1,0:T(8,128)(2,1)S(1)}, f32[512,256]{1,0:T(8,128)S(1)}) custom-call(s32[3]{0:T(128)S(1)} %pad_add_fusion.refs_0_.spot_ref, f32[1024,128]{1,0:T(8,128)S(1)} %fusion.1.refs_0_, f32[1024,128]{1,0:T(8,128)S(1)} %fusion.refs_1_, f32[1024,128]{1,0:T(8,128)S(1)} %collective-permute-done.5.refs_2_, ...), custom_call_target="tpu_custom_call" | custom-call | tf_op jit(solution)/shard_map/turn_plane/pallas_call | solution.py:271
  62.2 4.2 %collective-permute-done.9.refs_1_ = f32[1024,128]{1,0:T(8,128)S(1)} collective-permute-done((f32[1024,128]{1,0:T(8,128)S(1)}, f32[1024,128]{1,0:T(8,128)S(1)}, u32[]{:S(2)}, u32[]{:S(2)}) %collective-permute-start.9) | collective-permute-done | bytes 524320 | tf_op jit(solution)/shard_map/ppermute | solution.py:258
  66.4 2.1 %pair_products.2 = (f32[2,512,128]{2,1,0:T(8,128)S(1)}, f32[2,512,128]{2,1,0:T(8,128)S(1)}) custom-call(s32[3]{0:T(128)S(1)} %pad_add_fusion.refs_0_.spot_ref, bf16[512,1024]{1,0:T(8,128)(2,1)S(1)} %get-tuple-element.44.high_ref, bf16[512,1024]{1,0:T(8,128)(2,1)S(1)} %get-tuple-element.45.low_ref, f32[512,256]{1,0:T(8,128)S(1)} %get-tuple-element.46.own_ref, ...), custom_call_target="tpu_custom_call" | custom-call | tf_op jit(solution)/shard_map/pair_products/pallas_call | solution.py:284
  68.5 2.3 %collective-permute-start.14 = (f32[1024,128]{1,0:T(8,128)S(1)}, f32[1024,128]{1,0:T(8,128)S(1)}, u32[]{:S(2)}, u32[]{:S(2)}) collective-permute-start(f32[1024,128]{1,0:T(8,128)S(1)} %collective-permute-done.9.refs_1_), channel_id=1, source_target_pairs={{0,2},{1,3},{2,4},{3,5},{4,6},{5,7},{6,14},{7,15},{8,0},{9,1},{10,... | collective-permute-start | bytes 1572872 | tf_op jit(solution)/shard_map/ppermute | solution.py:294
  70.9 1.6 %collective-permute-start.12 = (f32[1,512,128]{2,1,0:T(8,128)S(1)}, f32[1,512,128]{2,1,0:T(8,128)S(1)}, u32[]{:S(2)}, u32[]{:S(2)}) collective-permute-start(f32[1,512,128]{2,1,0:T(8,128)S(1)} %slice_add_fusion.6), channel_id=1, source_target_pairs={{0,16},{8,24},{16,0},{24,8},{1,17},{9,25},{17,1},{25,9},{2,18},{10... | collective-permute-start | bytes 786440 | tf_op jit(solution)/shard_map/ppermute | solution.py:220
  72.4 5.3 %collective-permute-done.14.refs_2_ = f32[1024,128]{1,0:T(8,128)S(1)} collective-permute-done((f32[1024,128]{1,0:T(8,128)S(1)}, f32[1024,128]{1,0:T(8,128)S(1)}, u32[]{:S(2)}, u32[]{:S(2)}) %collective-permute-start.14) | collective-permute-done | bytes 524320 | tf_op jit(solution)/shard_map/ppermute | solution.py:294
  77.7 2.1 %pair_products.3 = (f32[2,512,128]{2,1,0:T(8,128)S(1)}, f32[2,512,128]{2,1,0:T(8,128)S(1)}) custom-call(s32[3]{0:T(128)S(1)} %pad_add_fusion.refs_0_.spot_ref, bf16[512,1024]{1,0:T(8,128)(2,1)S(1)} %get-tuple-element.44.high_ref, bf16[512,1024]{1,0:T(8,128)(2,1)S(1)} %get-tuple-element.45.low_ref, f32[512,256]{1,0:T(8,128)S(1)} %get-tuple-element.46.own_ref, ...), custom_call_target="tpu_custom_call" | custom-call | tf_op jit(solution)/shard_map/pair_products/pallas_call | solution.py:284
  80.0 1.9 %collective-permute-done.15 = f32[2,512,128]{2,1,0:T(8,128)S(1)} collective-permute-done((f32[2,512,128]{2,1,0:T(8,128)S(1)}, f32[2,512,128]{2,1,0:T(8,128)S(1)}, u32[]{:S(2)}, u32[]{:S(2)}) %collective-permute-start.15) | collective-permute-done | bytes 524320 | tf_op jit(solution)/shard_map/ppermute | solution.py:220
  81.9 1.6 %collective-permute-start.16 = (f32[1,512,128]{2,1,0:T(8,128)S(1)}, f32[1,512,128]{2,1,0:T(8,128)S(1)}, u32[]{:S(2)}, u32[]{:S(2)}) collective-permute-start(f32[1,512,128]{2,1,0:T(8,128)S(1)} %slice_add_fusion.4), channel_id=1, source_target_pairs={{0,16},{8,24},{16,0},{24,8},{1,17},{9,25},{17,1},{25,9},{2,18},{10... | collective-permute-start | bytes 786440 | tf_op jit(solution)/shard_map/ppermute | solution.py:220
  84.1 9.5 %collective-permute-done.16 = f32[1,512,128]{2,1,0:T(8,128)S(1)} collective-permute-done((f32[1,512,128]{2,1,0:T(8,128)S(1)}, f32[1,512,128]{2,1,0:T(8,128)S(1)}, u32[]{:S(2)}, u32[]{:S(2)}) %collective-permute-start.16) | collective-permute-done | bytes 262176 | tf_op jit(solution)/shard_map/ppermute | solution.py:220
  93.8 1.6 %collective-permute-start.19 = (f32[256,128]{1,0:T(8,128)S(1)}, f32[256,128]{1,0:T(8,128)S(1)}, u32[]{:S(2)}, u32[]{:S(2)}) collective-permute-start(f32[256,128]{1,0:T(8,128)S(1)} %get-tuple-element.61), channel_id=1, source_target_pairs={{0,1},{1,0},{2,3},{3,2},{4,5},{5,4},{6,7},{7,6},{8,9},{9,8},{10,11... | collective-permute-start | bytes 393224 | tf_op jit(solution)/shard_map/ppermute | solution.py:305
  95.4 2.5 %collective-permute-start.18 = (f32[256,128]{1,0:T(8,128)S(1)}, f32[256,128]{1,0:T(8,128)S(1)}, u32[]{:S(2)}, u32[]{:S(2)}) collective-permute-start(f32[256,128]{1,0:T(8,128)S(1)} %get-tuple-element.60), channel_id=1, source_target_pairs={{0,16},{1,17},{2,18},{3,19},{4,20},{5,21},{6,22},{7,23},{8,24},{9,... | collective-permute-start | bytes 393224 | tf_op jit(solution)/shard_map/ppermute | solution.py:305
  98.8 7.8 %collective-permute-done.18.refs_3_ = f32[256,128]{1,0:T(8,128)S(1)} collective-permute-done((f32[256,128]{1,0:T(8,128)S(1)}, f32[256,128]{1,0:T(8,128)S(1)}, u32[]{:S(2)}, u32[]{:S(2)}) %collective-permute-start.18) | collective-permute-done | bytes 131104 | tf_op jit(solution)/shard_map/ppermute | solution.py:305
  106.6 2.4 %collective-permute-done.20.refs_5_ = f32[256,128]{1,0:T(8,128)S(1)} collective-permute-done((f32[256,128]{1,0:T(8,128)S(1)}, f32[256,128]{1,0:T(8,128)S(1)}, u32[]{:S(2)}, u32[]{:S(2)}) %collective-permute-start.20) | collective-permute-done | bytes 131104 | tf_op jit(solution)/shard_map/ppermute | solution.py:305
  109.0 1.5 %finish.1 = f32[512,256]{1,0:T(8,128)} custom-call(s32[3]{0:T(128)S(1)} %pad_add_fusion.refs_0_.spot_ref, f32[512,128]{1,0:T(8,128)S(1)} %collective-permute-done.13.refs_0_, f32[512,128]{1,0:T(8,128)S(1)} %collective-permute-done.17.refs_1_, f32[256,128]{1,0:T(8,128)S(1)} %get-tuple-element.62.refs_2_, f32[256,128]{1,0:T(8,128)S(1)} %collective-permute-done.18.refs_3_, ...), custom_call_target="tpu_custom_call" | custom-call | tf_op jit(solution)/shard_map/finish/pallas_call | solution.py:309
  (38 shorter events, 5.6 us)
Async XLA Ops:
  0.8 3.4 %copy-start = (f32[8192,256]{1,0:T(8,128)S(1)}, f32[8192,256]{1,0:T(8,128)}, u32[]{:S(2)}) copy-start(f32[8192,256]{1,0:T(8,128)} %slab_ref.1) | copy-start | bytes 25165828
  4.2 0.8 copy-start.1
  5.0 10.1 %slice-start = ((s8[8388608]{0:T(1024)(128)(4,1)}), s8[4194304]{0:T(1024)(128)(4,1)S(1)}, s32[]{:S(2)}) async-start(s8[8388608]{0:T(1024)(128)(4,1)} %bitcast.14), calls=%async_computation | async-start | bytes 8388608
  11.6 2.7 %collective-permute-start = (f32[2048,128]{1,0:T(8,128)S(1)}, f32[2048,128]{1,0:T(8,128)S(1)}, u32[]{:S(2)}, u32[]{:S(2)}) collective-permute-start(f32[2048,128]{1,0:T(8,128)S(1)} %get-tuple-element.33), channel_id=1, source_target_pairs={{0,8},{8,0},{16,24},{24,16},{1,9},{9,1},{17,25},{25,17},{2,10},{10... | collective-permute-start | bytes 3145736 | tf_op jit(solution)/shard_map/ppermute | solution.py:220
  11.7 3.3 %slice-start.1 = ((s8[8388608]{0:T(1024)(128)(4,1)}), s8[4194304]{0:T(1024)(128)(4,1)S(1)}, s32[]{:S(2)}) async-start(s8[8388608]{0:T(1024)(128)(4,1)} %bitcast.14), calls=%async_computation.1 | async-start | bytes 8388608
  14.4 14.3 %collective-permute-start.1 = (f32[1024,128]{1,0:T(8,128)S(1)}, f32[1024,128]{1,0:T(8,128)S(1)}, u32[]{:S(2)}, u32[]{:S(2)}) collective-permute-start(f32[1024,128]{1,0:T(8,128)S(1)} %slice_add_fusion.3), channel_id=1, source_target_pairs={{0,16},{8,24},{16,0},{24,8},{1,17},{9,25},{17,1},{25,9},{2,18},{10... | collective-permute-start | bytes 1572872 | tf_op jit(solution)/shard_map/ppermute | solution.py:220
  28.8 2.7 %collective-permute-start.2 = (f32[2048,128]{1,0:T(8,128)S(1)}, f32[2048,128]{1,0:T(8,128)S(1)}, u32[]{:S(2)}, u32[]{:S(2)}) collective-permute-start(f32[2048,128]{1,0:T(8,128)S(1)} %get-tuple-element.39), channel_id=1, source_target_pairs={{0,8},{8,0},{16,24},{24,16},{1,9},{9,1},{17,25},{25,17},{2,10},{10... | collective-permute-start | bytes 3145736 | tf_op jit(solution)/shard_map/ppermute | solution.py:220
  28.9 9.2 %collective-permute-start.4 = (f32[1024,128]{1,0:T(8,128)S(1)}, f32[1024,128]{1,0:T(8,128)S(1)}, u32[]{:S(2)}, u32[]{:S(2)}) collective-permute-start(f32[1024,128]{1,0:T(8,128)S(1)} %fusion.1.refs_0_), channel_id=1, source_target_pairs={{0,2},{1,3},{2,4},{3,5},{4,6},{5,7},{6,14},{7,15},{8,0},{9,1},{10,... | collective-permute-start | bytes 1572872 | tf_op jit(solution)/shard_map/ppermute | solution.py:258
  31.6 14.0 %collective-permute-start.3 = (f32[1024,128]{1,0:T(8,128)S(1)}, f32[1024,128]{1,0:T(8,128)S(1)}, u32[]{:S(2)}, u32[]{:S(2)}) collective-permute-start(f32[1024,128]{1,0:T(8,128)S(1)} %slice_add_fusion), channel_id=1, source_target_pairs={{0,16},{8,24},{16,0},{24,8},{1,17},{9,25},{17,1},{25,9},{2,18},{10... | collective-permute-start | bytes 1572872 | tf_op jit(solution)/shard_map/ppermute | solution.py:220
  32.2 13.7 %collective-permute-start.5 = (f32[1024,128]{1,0:T(8,128)S(1)}, f32[1024,128]{1,0:T(8,128)S(1)}, u32[]{:S(2)}, u32[]{:S(2)}) collective-permute-start(f32[1024,128]{1,0:T(8,128)S(1)} %fusion.1.refs_0_), channel_id=1, source_target_pairs={{0,1},{1,0},{2,3},{3,2},{4,5},{5,4},{6,7},{7,6},{8,9},{9,8},{10,11... | collective-permute-start | bytes 1572872 | tf_op jit(solution)/shard_map/ppermute | solution.py:266
  38.1 9.5 %collective-permute-start.8 = (f32[1024,128]{1,0:T(8,128)S(1)}, f32[1024,128]{1,0:T(8,128)S(1)}, u32[]{:S(2)}, u32[]{:S(2)}) collective-permute-start(f32[1024,128]{1,0:T(8,128)S(1)} %collective-permute-done.4.refs_0_), channel_id=1, source_target_pairs={{0,2},{1,3},{2,4},{3,5},{4,6},{5,7},{6,14},{7,15},{8,0},{9,1},{10,... | collective-permute-start | bytes 1572872 | tf_op jit(solution)/shard_map/ppermute | solution.py:258
  45.9 9.2 %collective-permute-start.7 = (f32[1024,128]{1,0:T(8,128)S(1)}, f32[1024,128]{1,0:T(8,128)S(1)}, u32[]{:S(2)}, u32[]{:S(2)}) collective-permute-start(f32[1024,128]{1,0:T(8,128)S(1)} %fusion.refs_1_), channel_id=1, source_target_pairs={{0,2},{1,3},{2,4},{3,5},{4,6},{5,7},{6,14},{7,15},{8,0},{9,1},{10,... | collective-permute-start | bytes 1572872 | tf_op jit(solution)/shard_map/ppermute | solution.py:258
  47.5 14.6 %collective-permute-start.10 = (f32[1024,128]{1,0:T(8,128)S(1)}, f32[1024,128]{1,0:T(8,128)S(1)}, u32[]{:S(2)}, u32[]{:S(2)}) collective-permute-start(f32[1024,128]{1,0:T(8,128)S(1)} %collective-permute-done.8.refs_1_), channel_id=1, source_target_pairs={{0,2},{1,3},{2,4},{3,5},{4,6},{5,7},{6,14},{7,15},{8,0},{9,1},{10,... | collective-permute-start | bytes 1572872 | tf_op jit(solution)/shard_map/ppermute | solution.py:258
  48.8 11.2 %collective-permute-start.6 = (f32[1024,128]{1,0:T(8,128)S(1)}, f32[1024,128]{1,0:T(8,128)S(1)}, u32[]{:S(2)}, u32[]{:S(2)}) collective-permute-start(f32[1024,128]{1,0:T(8,128)S(1)} %fusion.refs_1_), channel_id=1, source_target_pairs={{0,1},{1,0},{2,3},{3,2},{4,5},{5,4},{6,7},{7,6},{8,9},{9,8},{10,11... | collective-permute-start | bytes 1572872 | tf_op jit(solution)/shard_map/ppermute | solution.py:266
  55.1 11.2 %collective-permute-start.9 = (f32[1024,128]{1,0:T(8,128)S(1)}, f32[1024,128]{1,0:T(8,128)S(1)}, u32[]{:S(2)}, u32[]{:S(2)}) collective-permute-start(f32[1024,128]{1,0:T(8,128)S(1)} %collective-permute-done.7.refs_0_), channel_id=1, source_target_pairs={{0,2},{1,3},{2,4},{3,5},{4,6},{5,7},{6,14},{7,15},{8,0},{9,1},{10,... | collective-permute-start | bytes 1572872 | tf_op jit(solution)/shard_map/ppermute | solution.py:258
  68.5 2.4 %collective-permute-start.11 = (f32[2,512,128]{2,1,0:T(8,128)S(1)}, f32[2,512,128]{2,1,0:T(8,128)S(1)}, u32[]{:S(2)}, u32[]{:S(2)}) collective-permute-start(f32[2,512,128]{2,1,0:T(8,128)S(1)} %get-tuple-element.54), channel_id=1, source_target_pairs={{0,8},{8,0},{16,24},{24,16},{1,9},{9,1},{17,25},{25,17},{2,10},{10... | collective-permute-start | bytes 1572872 | tf_op jit(solution)/shard_map/ppermute | solution.py:220
  68.5 9.2 %collective-permute-start.14 = (f32[1024,128]{1,0:T(8,128)S(1)}, f32[1024,128]{1,0:T(8,128)S(1)}, u32[]{:S(2)}, u32[]{:S(2)}) collective-permute-start(f32[1024,128]{1,0:T(8,128)S(1)} %collective-permute-done.9.refs_1_), channel_id=1, source_target_pairs={{0,2},{1,3},{2,4},{3,5},{4,6},{5,7},{6,14},{7,15},{8,0},{9,1},{10,... | collective-permute-start | bytes 1572872 | tf_op jit(solution)/shard_map/ppermute | solution.py:294
  70.9 9.0 %collective-permute-start.12 = (f32[1,512,128]{2,1,0:T(8,128)S(1)}, f32[1,512,128]{2,1,0:T(8,128)S(1)}, u32[]{:S(2)}, u32[]{:S(2)}) collective-permute-start(f32[1,512,128]{2,1,0:T(8,128)S(1)} %slice_add_fusion.6), channel_id=1, source_target_pairs={{0,16},{8,24},{16,0},{24,8},{1,17},{9,25},{17,1},{25,9},{2,18},{10... | collective-permute-start | bytes 786440 | tf_op jit(solution)/shard_map/ppermute | solution.py:220
  79.9 2.0 %collective-permute-start.15 = (f32[2,512,128]{2,1,0:T(8,128)S(1)}, f32[2,512,128]{2,1,0:T(8,128)S(1)}, u32[]{:S(2)}, u32[]{:S(2)}) collective-permute-start(f32[2,512,128]{2,1,0:T(8,128)S(1)} %get-tuple-element.58), channel_id=1, source_target_pairs={{0,8},{8,0},{16,24},{24,16},{1,9},{9,1},{17,25},{25,17},{2,10},{10... | collective-permute-start | bytes 1572872 | tf_op jit(solution)/shard_map/ppermute | solution.py:220
  81.9 11.7 %collective-permute-start.16 = (f32[1,512,128]{2,1,0:T(8,128)S(1)}, f32[1,512,128]{2,1,0:T(8,128)S(1)}, u32[]{:S(2)}, u32[]{:S(2)}) collective-permute-start(f32[1,512,128]{2,1,0:T(8,128)S(1)} %slice_add_fusion.4), channel_id=1, source_target_pairs={{0,16},{8,24},{16,0},{24,8},{1,17},{9,25},{17,1},{25,9},{2,18},{10... | collective-permute-start | bytes 786440 | tf_op jit(solution)/shard_map/ppermute | solution.py:220
  83.4 15.4 %collective-permute-start.13 = (f32[512,128]{1,0:T(8,128)S(1)}, f32[512,128]{1,0:T(8,128)S(1)}, u32[]{:S(2)}, u32[]{:S(2)}) collective-permute-start(f32[512,128]{1,0:T(8,128)S(1)} %bitcast.18), channel_id=1, source_target_pairs={{0,0},{1,1},{2,8},{3,9},{4,16},{5,17},{6,24},{7,25},{8,2},{9,3},{1... | collective-permute-start | bytes 786440 | tf_op jit(solution)/shard_map/ppermute | solution.py:301
  93.7 15.3 %collective-permute-start.17 = (f32[512,128]{1,0:T(8,128)S(1)}, f32[512,128]{1,0:T(8,128)S(1)}, u32[]{:S(2)}, u32[]{:S(2)}) collective-permute-start(f32[512,128]{1,0:T(8,128)S(1)} %bitcast.19), channel_id=1, source_target_pairs={{0,4},{1,5},{2,12},{3,13},{4,20},{5,21},{6,28},{7,29},{8,6},{9,7},... | collective-permute-start | bytes 786440 | tf_op jit(solution)/shard_map/ppermute | solution.py:301
  93.8 5.0 %collective-permute-start.19 = (f32[256,128]{1,0:T(8,128)S(1)}, f32[256,128]{1,0:T(8,128)S(1)}, u32[]{:S(2)}, u32[]{:S(2)}) collective-permute-start(f32[256,128]{1,0:T(8,128)S(1)} %get-tuple-element.61), channel_id=1, source_target_pairs={{0,1},{1,0},{2,3},{3,2},{4,5},{5,4},{6,7},{7,6},{8,9},{9,8},{10,11... | collective-permute-start | bytes 393224 | tf_op jit(solution)/shard_map/ppermute | solution.py:305
  95.4 11.2 %collective-permute-start.18 = (f32[256,128]{1,0:T(8,128)S(1)}, f32[256,128]{1,0:T(8,128)S(1)}, u32[]{:S(2)}, u32[]{:S(2)}) collective-permute-start(f32[256,128]{1,0:T(8,128)S(1)} %get-tuple-element.60), channel_id=1, source_target_pairs={{0,16},{1,17},{2,18},{3,19},{4,20},{5,21},{6,22},{7,23},{8,24},{9,... | collective-permute-start | bytes 393224 | tf_op jit(solution)/shard_map/ppermute | solution.py:305
  97.9 11.1 %collective-permute-start.20 = (f32[256,128]{1,0:T(8,128)S(1)}, f32[256,128]{1,0:T(8,128)S(1)}, u32[]{:S(2)}, u32[]{:S(2)}) collective-permute-start(f32[256,128]{1,0:T(8,128)S(1)} %get-tuple-element.59), channel_id=1, source_target_pairs={{0,17},{1,16},{2,19},{3,18},{4,21},{5,20},{6,23},{7,22},{8,25},{9,... | collective-permute-start | bytes 393224 | tf_op jit(solution)/shard_map/ppermute | solution.py:305

commit v7 on v6

--- a/solution.py
+++ b/solution.py
@@ -296,6 +296,9 @@
             send, totals[-1] = after(send, totals[-1])
         for at in range(bits):
             keep, send = halve(keep, send, at)
+        if strip:
+            for side in sideways[1:]:
+                send, side[-1] = after(send, side[-1])
         total = (keep + send)[0]
         totals.append(total)
         directs.append(lax.ppermute(total, AXES, pairs(lambda r, c: (c // near, (r ^ flip) * near + c % near))))

time: 111 us -> 111 us (level)
  waiting for transfers between devices: 57.1 us -> 55.5 us
  starting transfers between devices: 22.5 us -> 24 us
    ppermute x8, waiting for transfers between devices: 23.8 us -> 19 us  [halve(): got = lax.ppermute(send, 'rows', [(r, r ^ 1 << at) for r in range(groups)])]
    ppermute x3, waiting for transfers between devices: 11 us -> 14.3 us  [shards(): part = lax.ppermute(part, AXES, pairs(lambda r, c: (r ^ flip, c ^ off)))]
    ppermute x3, starting transfers between devices: 4.15 us -> 5.66 us  [shards(): part = lax.ppermute(part, AXES, pairs(lambda r, c: (r ^ flip, c ^ off)))]
where the time goes in v7:
time: 111 us; the launch traced here: 110 us
  waiting for transfers between devices  55.5 us (50%)
  Pallas kernels  25.3 us (23%)
  starting transfers between devices  24 us (22%)
  local copies, waits for them, and re-layouts  4.2 us (4%)
  other arithmetic  1.24 us (1%)
    ppermute x8, waiting for transfers between devices, halve(): got = lax.ppermute(send, 'rows', [(r, r ^ 1 << at) for r in range(groups)])  19 us
    pallas_call x2, Pallas kernels, picked_strip(): pl.pallas_call(kernel, out_shape=out_shape, in_specs=[SMEM, SMEM, VMEM, V...  15 us
    ppermute x3, waiting for transfers between devices, shards(): part = lax.ppermute(part, AXES, pairs(lambda r, c: (r ^ flip, c ^ off)))  14.3 us
    ppermute x5, waiting for transfers between devices, shards(): moving = lax.ppermute(moving, AXES, ring)  13.4 us
    ppermute x5, starting transfers between devices, shards(): moving = lax.ppermute(moving, AXES, ring)  7.63 us
    ppermute x3, starting transfers between devices, shards(): part = lax.ppermute(part, AXES, pairs(lambda r, c: (r ^ flip, c ^ off)))  5.66 us
    ppermute x1, waiting for transfers between devices, shards(): remote[strip + 1].append(lax.ppermute(moving, AXES, ring))  5.31 us
    ppermute x8, starting transfers between devices, halve(): got = lax.ppermute(send, 'rows', [(r, r ^ 1 << at) for r in range(groups)])  4.61 us
  transfers between devices with their start and end apart: 21, of which 15 were waited for; matrix products, arithmetic and copies ran while one was open for 0% of the time, Pallas kernels for 14%

profile of v7, /device:TPU:18, one launch (start us, length us, event | category | flops | bytes accessed | tf_op | source)
XLA Modules:
  0.0 110.4 jit_solution(10052030083326354672)
XLA Ops:
  0.8 3.4 %copy-done = f32[8192,256]{1,0:T(8,128)S(1)} copy-done((f32[8192,256]{1,0:T(8,128)S(1)}, f32[8192,256]{1,0:T(8,128)}, u32[]{:S(2)}) %copy-start) | copy-done | bytes 8388632
  5.0 6.7 %transform_and_pick.2 = (f32[2048,128]{1,0:T(8,128)S(1)}, f32[16384,128]{1,0:T(8,128)S(1)}) custom-call(s32[3]{0:T(128)S(1)} %pad_add_fusion.refs_0_.spot_ref, s32[4096]{0:T(1024)S(1)} %multiply_add_fusion.refs_1_.index_ref, s32[8,8,128]{2,1,0:T(8,128)S(1)} %bitcast.16, f32[8192,256]{1,0:T(8,128)S(1)} %copy-done), custom_call_target="tpu_custom_call" | custom-call | flops 2147483648 | bytes 25165824 | tf_op jit(solution)/shard_map/transform_and_pick/pallas_call | solution.py:104
  11.7 2.5 %pick.1 = f32[2048,128]{1,0:T(8,128)S(1)} custom-call(s32[3]{0:T(128)S(1)} %pad_add_fusion.refs_0_.spot_ref, s32[4096]{0:T(1024)S(1)} %multiply_add_fusion.refs_1_.index_ref, f32[16384,128]{1,0:T(8,128)S(1)} %get-tuple-element.34.mixed), custom_call_target="tpu_custom_call" | custom-call | tf_op jit(solution)/shard_map/pick/pallas_call | solution.py:118
  15.1 8.3 %transform_and_pick.3 = (f32[2048,128]{1,0:T(8,128)S(1)}, f32[2048,128]{1,0:T(8,128)S(1)}) custom-call(s32[3]{0:T(128)S(1)} %pad_add_fusion.refs_0_.spot_ref, s32[4096]{0:T(1024)S(1)} %multiply_add_fusion.refs_1_.index_ref, s32[8,8,128]{2,1,0:T(8,128)S(1)} %bitcast.17, f32[8192,256]{1,0:T(8,128)S(1)} %bitcast.15), custom_call_target="tpu_custom_call" | custom-call | flops 2147483648 | bytes 25165824 | tf_op jit(solution)/shard_map/transform_and_pick/pallas_call | solution.py:104
  23.4 5.3 %collective-permute-done.1 = f32[1024,128]{1,0:T(8,128)S(1)} collective-permute-done((f32[1024,128]{1,0:T(8,128)S(1)}, f32[1024,128]{1,0:T(8,128)S(1)}, u32[]{:S(2)}, u32[]{:S(2)}) %collective-permute-start.1) | collective-permute-done | bytes 524320 | tf_op jit(solution)/shard_map/ppermute | solution.py:220
  28.9 1.6 %collective-permute-start.4 = (f32[1024,128]{1,0:T(8,128)S(1)}, f32[1024,128]{1,0:T(8,128)S(1)}, u32[]{:S(2)}, u32[]{:S(2)}) collective-permute-start(f32[1024,128]{1,0:T(8,128)S(1)} %fusion.1.refs_0_), channel_id=1, source_target_pairs={{0,2},{1,3},{2,4},{3,5},{4,6},{5,7},{6,14},{7,15},{8,0},{9,1},{10,... | collective-permute-start | bytes 1572872 | tf_op jit(solution)/shard_map/ppermute | solution.py:258
  32.2 1.5 %collective-permute-start.5 = (f32[1024,128]{1,0:T(8,128)S(1)}, f32[1024,128]{1,0:T(8,128)S(1)}, u32[]{:S(2)}, u32[]{:S(2)}) collective-permute-start(f32[1024,128]{1,0:T(8,128)S(1)} %fusion.1.refs_0_), channel_id=1, source_target_pairs={{0,1},{1,0},{2,3},{3,2},{4,5},{5,4},{6,7},{7,6},{8,9},{9,8},{10,11... | collective-permute-start | bytes 1572872 | tf_op jit(solution)/shard_map/ppermute | solution.py:266
  33.7 4.4 %collective-permute-done.4.refs_0_ = f32[1024,128]{1,0:T(8,128)S(1)} collective-permute-done((f32[1024,128]{1,0:T(8,128)S(1)}, f32[1024,128]{1,0:T(8,128)S(1)}, u32[]{:S(2)}, u32[]{:S(2)}) %collective-permute-start.4) | collective-permute-done | bytes 524320 | tf_op jit(solution)/shard_map/ppermute | solution.py:258
  38.1 1.6 %collective-permute-start.8 = (f32[1024,128]{1,0:T(8,128)S(1)}, f32[1024,128]{1,0:T(8,128)S(1)}, u32[]{:S(2)}, u32[]{:S(2)}) collective-permute-start(f32[1024,128]{1,0:T(8,128)S(1)} %collective-permute-done.4.refs_0_), channel_id=1, source_target_pairs={{0,2},{1,3},{2,4},{3,5},{4,6},{5,7},{6,14},{7,15},{8,0},{9,1},{10,... | collective-permute-start | bytes 1572872 | tf_op jit(solution)/shard_map/ppermute | solution.py:258
  39.6 6.0 %collective-permute-done.3 = f32[1024,128]{1,0:T(8,128)S(1)} collective-permute-done((f32[1024,128]{1,0:T(8,128)S(1)}, f32[1024,128]{1,0:T(8,128)S(1)}, u32[]{:S(2)}, u32[]{:S(2)}) %collective-permute-start.3) | collective-permute-done | bytes 524320 | tf_op jit(solution)/shard_map/ppermute | solution.py:220
  45.9 1.6 %collective-permute-start.7 = (f32[1024,128]{1,0:T(8,128)S(1)}, f32[1024,128]{1,0:T(8,128)S(1)}, u32[]{:S(2)}, u32[]{:S(2)}) collective-permute-start(f32[1024,128]{1,0:T(8,128)S(1)} %fusion.refs_1_), channel_id=1, source_target_pairs={{0,2},{1,3},{2,4},{3,5},{4,6},{5,7},{6,14},{7,15},{8,0},{9,1},{10,... | collective-permute-start | bytes 1572872 | tf_op jit(solution)/shard_map/ppermute | solution.py:258
  48.8 1.5 %collective-permute-start.6 = (f32[1024,128]{1,0:T(8,128)S(1)}, f32[1024,128]{1,0:T(8,128)S(1)}, u32[]{:S(2)}, u32[]{:S(2)}) collective-permute-start(f32[1024,128]{1,0:T(8,128)S(1)} %fusion.refs_1_), channel_id=1, source_target_pairs={{0,1},{1,0},{2,3},{3,2},{4,5},{5,4},{6,7},{7,6},{8,9},{9,8},{10,11... | collective-permute-start | bytes 1572872 | tf_op jit(solution)/shard_map/ppermute | solution.py:266
  50.3 4.8 %collective-permute-done.7.refs_0_ = f32[1024,128]{1,0:T(8,128)S(1)} collective-permute-done((f32[1024,128]{1,0:T(8,128)S(1)}, f32[1024,128]{1,0:T(8,128)S(1)}, u32[]{:S(2)}, u32[]{:S(2)}) %collective-permute-start.7) | collective-permute-done | bytes 524320 | tf_op jit(solution)/shard_map/ppermute | solution.py:258
  55.1 1.6 %collective-permute-start.9 = (f32[1024,128]{1,0:T(8,128)S(1)}, f32[1024,128]{1,0:T(8,128)S(1)}, u32[]{:S(2)}, u32[]{:S(2)}) collective-permute-start(f32[1024,128]{1,0:T(8,128)S(1)} %collective-permute-done.7.refs_0_), channel_id=1, source_target_pairs={{0,2},{1,3},{2,4},{3,5},{4,6},{5,7},{6,14},{7,15},{8,0},{9,1},{10,... | collective-permute-start | bytes 1572872 | tf_op jit(solution)/shard_map/ppermute | solution.py:258
  56.7 3.3 %collective-permute-done.6.refs_3_ = f32[1024,128]{1,0:T(8,128)S(1)} collective-permute-done((f32[1024,128]{1,0:T(8,128)S(1)}, f32[1024,128]{1,0:T(8,128)S(1)}, u32[]{:S(2)}, u32[]{:S(2)}) %collective-permute-start.6) | collective-permute-done | bytes 524320 | tf_op jit(solution)/shard_map/ppermute | solution.py:266
  60.0 2.1 %turn_plane.1 = (bf16[512,1024]{1,0:T(8,128)(2,1)S(1)}, bf16[512,1024]{1,0:T(8,128)(2,1)S(1)}, f32[512,256]{1,0:T(8,128)S(1)}) custom-call(s32[3]{0:T(128)S(1)} %pad_add_fusion.refs_0_.spot_ref, f32[1024,128]{1,0:T(8,128)S(1)} %fusion.1.refs_0_, f32[1024,128]{1,0:T(8,128)S(1)} %fusion.refs_1_, f32[1024,128]{1,0:T(8,128)S(1)} %collective-permute-done.5.refs_2_, ...), custom_call_target="tpu_custom_call" | custom-call | tf_op jit(solution)/shard_map/turn_plane/pallas_call | solution.py:271
  62.2 4.2 %collective-permute-done.9.refs_1_ = f32[1024,128]{1,0:T(8,128)S(1)} collective-permute-done((f32[1024,128]{1,0:T(8,128)S(1)}, f32[1024,128]{1,0:T(8,128)S(1)}, u32[]{:S(2)}, u32[]{:S(2)}) %collective-permute-start.9) | collective-permute-done | bytes 524320 | tf_op jit(solution)/shard_map/ppermute | solution.py:258
  66.4 2.1 %pair_products.2 = (f32[2,512,128]{2,1,0:T(8,128)S(1)}, f32[2,512,128]{2,1,0:T(8,128)S(1)}) custom-call(s32[3]{0:T(128)S(1)} %pad_add_fusion.refs_0_.spot_ref, bf16[512,1024]{1,0:T(8,128)(2,1)S(1)} %get-tuple-element.46.high_ref, bf16[512,1024]{1,0:T(8,128)(2,1)S(1)} %get-tuple-element.47.low_ref, f32[512,256]{1,0:T(8,128)S(1)} %get-tuple-element.48.own_ref, ...), custom_call_target="tpu_custom_call" | custom-call | tf_op jit(solution)/shard_map/pair_products/pallas_call | solution.py:284
  68.5 2.3 %collective-permute-start.14 = (f32[1024,128]{1,0:T(8,128)S(1)}, f32[1024,128]{1,0:T(8,128)S(1)}, u32[]{:S(2)}, u32[]{:S(2)}) collective-permute-start(f32[1024,128]{1,0:T(8,128)S(1)} %collective-permute-done.9.refs_1_), channel_id=1, source_target_pairs={{0,2},{1,3},{2,4},{3,5},{4,6},{5,7},{6,14},{7,15},{8,0},{9,1},{10,... | collective-permute-start | bytes 1572872 | tf_op jit(solution)/shard_map/ppermute | solution.py:294
  70.9 1.6 %collective-permute-start.12 = (f32[1,512,128]{2,1,0:T(8,128)S(1)}, f32[1,512,128]{2,1,0:T(8,128)S(1)}, u32[]{:S(2)}, u32[]{:S(2)}) collective-permute-start(f32[1,512,128]{2,1,0:T(8,128)S(1)} %slice_add_fusion.6), channel_id=1, source_target_pairs={{0,16},{8,24},{16,0},{24,8},{1,17},{9,25},{17,1},{25,9},{2,18},{10... | collective-permute-start | bytes 786440 | tf_op jit(solution)/shard_map/ppermute | solution.py:220
  72.4 5.3 %collective-permute-done.14.refs_2_ = f32[1024,128]{1,0:T(8,128)S(1)} collective-permute-done((f32[1024,128]{1,0:T(8,128)S(1)}, f32[1024,128]{1,0:T(8,128)S(1)}, u32[]{:S(2)}, u32[]{:S(2)}) %collective-permute-start.14) | collective-permute-done | bytes 524320 | tf_op jit(solution)/shard_map/ppermute | solution.py:294
  77.7 2.1 %pair_products.3 = (f32[2,512,128]{2,1,0:T(8,128)S(1)}, f32[2,512,128]{2,1,0:T(8,128)S(1)}) custom-call(s32[3]{0:T(128)S(1)} %pad_add_fusion.refs_0_.spot_ref, bf16[512,1024]{1,0:T(8,128)(2,1)S(1)} %get-tuple-element.46.high_ref, bf16[512,1024]{1,0:T(8,128)(2,1)S(1)} %get-tuple-element.47.low_ref, f32[512,256]{1,0:T(8,128)S(1)} %get-tuple-element.48.own_ref, ...), custom_call_target="tpu_custom_call" | custom-call | tf_op jit(solution)/shard_map/pair_products/pallas_call | solution.py:284
  80.0 1.9 %collective-permute-done.15 = f32[2,512,128]{2,1,0:T(8,128)S(1)} collective-permute-done((f32[2,512,128]{2,1,0:T(8,128)S(1)}, f32[2,512,128]{2,1,0:T(8,128)S(1)}, u32[]{:S(2)}, u32[]{:S(2)}) %collective-permute-start.15) | collective-permute-done | bytes 524320 | tf_op jit(solution)/shard_map/ppermute | solution.py:220
  81.9 1.6 %collective-permute-start.16 = (f32[1,512,128]{2,1,0:T(8,128)S(1)}, f32[1,512,128]{2,1,0:T(8,128)S(1)}, u32[]{:S(2)}, u32[]{:S(2)}) collective-permute-start(f32[1,512,128]{2,1,0:T(8,128)S(1)} %slice_add_fusion.4), channel_id=1, source_target_pairs={{0,16},{8,24},{16,0},{24,8},{1,17},{9,25},{17,1},{25,9},{2,18},{10... | collective-permute-start | bytes 786440 | tf_op jit(solution)/shard_map/ppermute | solution.py:220
  83.5 1.6 %collective-permute-start.17 = (f32[256,128]{1,0:T(8,128)S(1)}, f32[256,128]{1,0:T(8,128)S(1)}, u32[]{:S(2)}, u32[]{:S(2)}) collective-permute-start(f32[256,128]{1,0:T(8,128)S(1)} %get-tuple-element.66), channel_id=1, source_target_pairs={{0,1},{1,0},{2,3},{3,2},{4,5},{5,4},{6,7},{7,6},{8,9},{9,8},{10,11... | collective-permute-start | bytes 393224 | tf_op jit(solution)/shard_map/ppermute | solution.py:308
  85.7 3.1 %collective-permute-done.17.refs_4_ = f32[256,128]{1,0:T(8,128)S(1)} collective-permute-done((f32[256,128]{1,0:T(8,128)S(1)}, f32[256,128]{1,0:T(8,128)S(1)}, u32[]{:S(2)}, u32[]{:S(2)}) %collective-permute-start.17) | collective-permute-done | bytes 131104 | tf_op jit(solution)/shard_map/ppermute | solution.py:308
  88.8 4.6 %collective-permute-done.16 = f32[1,512,128]{2,1,0:T(8,128)S(1)} collective-permute-done((f32[1,512,128]{2,1,0:T(8,128)S(1)}, f32[1,512,128]{2,1,0:T(8,128)S(1)}, u32[]{:S(2)}, u32[]{:S(2)}) %collective-permute-start.16) | collective-permute-done | bytes 262176 | tf_op jit(solution)/shard_map/ppermute | solution.py:220
  93.6 2.7 %collective-permute-start.19 = (f32[256,128]{1,0:T(8,128)S(1)}, f32[256,128]{1,0:T(8,128)S(1)}, u32[]{:S(2)}, u32[]{:S(2)}) collective-permute-start(f32[256,128]{1,0:T(8,128)S(1)} %get-tuple-element.64), channel_id=1, source_target_pairs={{0,16},{1,17},{2,18},{3,19},{4,20},{5,21},{6,22},{7,23},{8,24},{9,... | collective-permute-start | bytes 393224 | tf_op jit(solution)/shard_map/ppermute | solution.py:308
  96.3 1.4 %collective-permute-start.20 = (f32[256,128]{1,0:T(8,128)S(1)}, f32[256,128]{1,0:T(8,128)S(1)}, u32[]{:S(2)}, u32[]{:S(2)}) collective-permute-start(f32[256,128]{1,0:T(8,128)S(1)} %get-tuple-element.63), channel_id=1, source_target_pairs={{0,17},{1,16},{2,19},{3,18},{4,21},{5,20},{6,23},{7,22},{8,25},{9,... | collective-permute-start | bytes 393224 | tf_op jit(solution)/shard_map/ppermute | solution.py:308
  97.6 8.1 %collective-permute-done.19.refs_3_ = f32[256,128]{1,0:T(8,128)S(1)} collective-permute-done((f32[256,128]{1,0:T(8,128)S(1)}, f32[256,128]{1,0:T(8,128)S(1)}, u32[]{:S(2)}, u32[]{:S(2)}) %collective-permute-start.19) | collective-permute-done | bytes 131104 | tf_op jit(solution)/shard_map/ppermute | solution.py:308
  105.7 3.1 %collective-permute-done.20.refs_5_ = f32[256,128]{1,0:T(8,128)S(1)} collective-permute-done((f32[256,128]{1,0:T(8,128)S(1)}, f32[256,128]{1,0:T(8,128)S(1)}, u32[]{:S(2)}, u32[]{:S(2)}) %collective-permute-start.20) | collective-permute-done | bytes 131104 | tf_op jit(solution)/shard_map/ppermute | solution.py:308
  108.9 1.5 %finish.1 = f32[512,256]{1,0:T(8,128)} custom-call(s32[3]{0:T(128)S(1)} %pad_add_fusion.refs_0_.spot_ref, f32[512,128]{1,0:T(8,128)S(1)} %collective-permute-done.13.refs_0_, f32[512,128]{1,0:T(8,128)S(1)} %collective-permute-done.18.refs_1_, f32[256,128]{1,0:T(8,128)S(1)} %get-tuple-element.65.refs_2_, f32[256,128]{1,0:T(8,128)S(1)} %collective-permute-done.19.refs_3_, ...), custom_call_target="tpu_custom_call" | custom-call | tf_op jit(solution)/shard_map/finish/pallas_call | solution.py:312
  (38 shorter events, 7.0 us)
Async XLA Ops:
  0.8 3.4 %copy-start = (f32[8192,256]{1,0:T(8,128)S(1)}, f32[8192,256]{1,0:T(8,128)}, u32[]{:S(2)}) copy-start(f32[8192,256]{1,0:T(8,128)} %slab_ref.1) | copy-start | bytes 25165828
  4.2 0.8 copy-start.1
  5.0 10.1 %slice-start = ((s8[8388608]{0:T(1024)(128)(4,1)}), s8[4194304]{0:T(1024)(128)(4,1)S(1)}, s32[]{:S(2)}) async-start(s8[8388608]{0:T(1024)(128)(4,1)} %bitcast.14), calls=%async_computation | async-start | bytes 8388608
  11.7 2.7 %collective-permute-start = (f32[2048,128]{1,0:T(8,128)S(1)}, f32[2048,128]{1,0:T(8,128)S(1)}, u32[]{:S(2)}, u32[]{:S(2)}) collective-permute-start(f32[2048,128]{1,0:T(8,128)S(1)} %get-tuple-element.35), channel_id=1, source_target_pairs={{0,8},{8,0},{16,24},{24,16},{1,9},{9,1},{17,25},{25,17},{2,10},{10... | collective-permute-start | bytes 3145736 | tf_op jit(solution)/shard_map/ppermute | solution.py:220
  11.7 3.3 %slice-start.1 = ((s8[8388608]{0:T(1024)(128)(4,1)}), s8[4194304]{0:T(1024)(128)(4,1)S(1)}, s32[]{:S(2)}) async-start(s8[8388608]{0:T(1024)(128)(4,1)} %bitcast.14), calls=%async_computation.1 | async-start | bytes 8388608
  14.4 14.3 %collective-permute-start.1 = (f32[1024,128]{1,0:T(8,128)S(1)}, f32[1024,128]{1,0:T(8,128)S(1)}, u32[]{:S(2)}, u32[]{:S(2)}) collective-permute-start(f32[1024,128]{1,0:T(8,128)S(1)} %slice_add_fusion.3), channel_id=1, source_target_pairs={{0,16},{8,24},{16,0},{24,8},{1,17},{9,25},{17,1},{25,9},{2,18},{10... | collective-permute-start | bytes 1572872 | tf_op jit(solution)/shard_map/ppermute | solution.py:220
  28.8 2.7 %collective-permute-start.2 = (f32[2048,128]{1,0:T(8,128)S(1)}, f32[2048,128]{1,0:T(8,128)S(1)}, u32[]{:S(2)}, u32[]{:S(2)}) collective-permute-start(f32[2048,128]{1,0:T(8,128)S(1)} %get-tuple-element.41), channel_id=1, source_target_pairs={{0,8},{8,0},{16,24},{24,16},{1,9},{9,1},{17,25},{25,17},{2,10},{10... | collective-permute-start | bytes 3145736 | tf_op jit(solution)/shard_map/ppermute | solution.py:220
  28.9 9.2 %collective-permute-start.4 = (f32[1024,128]{1,0:T(8,128)S(1)}, f32[1024,128]{1,0:T(8,128)S(1)}, u32[]{:S(2)}, u32[]{:S(2)}) collective-permute-start(f32[1024,128]{1,0:T(8,128)S(1)} %fusion.1.refs_0_), channel_id=1, source_target_pairs={{0,2},{1,3},{2,4},{3,5},{4,6},{5,7},{6,14},{7,15},{8,0},{9,1},{10,... | collective-permute-start | bytes 1572872 | tf_op jit(solution)/shard_map/ppermute | solution.py:258
  31.6 14.0 %collective-permute-start.3 = (f32[1024,128]{1,0:T(8,128)S(1)}, f32[1024,128]{1,0:T(8,128)S(1)}, u32[]{:S(2)}, u32[]{:S(2)}) collective-permute-start(f32[1024,128]{1,0:T(8,128)S(1)} %slice_add_fusion), channel_id=1, source_target_pairs={{0,16},{8,24},{16,0},{24,8},{1,17},{9,25},{17,1},{25,9},{2,18},{10... | collective-permute-start | bytes 1572872 | tf_op jit(solution)/shard_map/ppermute | solution.py:220
  32.2 13.7 %collective-permute-start.5 = (f32[1024,128]{1,0:T(8,128)S(1)}, f32[1024,128]{1,0:T(8,128)S(1)}, u32[]{:S(2)}, u32[]{:S(2)}) collective-permute-start(f32[1024,128]{1,0:T(8,128)S(1)} %fusion.1.refs_0_), channel_id=1, source_target_pairs={{0,1},{1,0},{2,3},{3,2},{4,5},{5,4},{6,7},{7,6},{8,9},{9,8},{10,11... | collective-permute-start | bytes 1572872 | tf_op jit(solution)/shard_map/ppermute | solution.py:266
  38.1 9.5 %collective-permute-start.8 = (f32[1024,128]{1,0:T(8,128)S(1)}, f32[1024,128]{1,0:T(8,128)S(1)}, u32[]{:S(2)}, u32[]{:S(2)}) collective-permute-start(f32[1024,128]{1,0:T(8,128)S(1)} %collective-permute-done.4.refs_0_), channel_id=1, source_target_pairs={{0,2},{1,3},{2,4},{3,5},{4,6},{5,7},{6,14},{7,15},{8,0},{9,1},{10,... | collective-permute-start | bytes 1572872 | tf_op jit(solution)/shard_map/ppermute | solution.py:258
  45.9 9.2 %collective-permute-start.7 = (f32[1024,128]{1,0:T(8,128)S(1)}, f32[1024,128]{1,0:T(8,128)S(1)}, u32[]{:S(2)}, u32[]{:S(2)}) collective-permute-start(f32[1024,128]{1,0:T(8,128)S(1)} %fusion.refs_1_), channel_id=1, source_target_pairs={{0,2},{1,3},{2,4},{3,5},{4,6},{5,7},{6,14},{7,15},{8,0},{9,1},{10,... | collective-permute-start | bytes 1572872 | tf_op jit(solution)/shard_map/ppermute | solution.py:258
  47.5 14.6 %collective-permute-start.10 = (f32[1024,128]{1,0:T(8,128)S(1)}, f32[1024,128]{1,0:T(8,128)S(1)}, u32[]{:S(2)}, u32[]{:S(2)}) collective-permute-start(f32[1024,128]{1,0:T(8,128)S(1)} %collective-permute-done.8.refs_1_), channel_id=1, source_target_pairs={{0,2},{1,3},{2,4},{3,5},{4,6},{5,7},{6,14},{7,15},{8,0},{9,1},{10,... | collective-permute-start | bytes 1572872 | tf_op jit(solution)/shard_map/ppermute | solution.py:258
  48.8 11.2 %collective-permute-start.6 = (f32[1024,128]{1,0:T(8,128)S(1)}, f32[1024,128]{1,0:T(8,128)S(1)}, u32[]{:S(2)}, u32[]{:S(2)}) collective-permute-start(f32[1024,128]{1,0:T(8,128)S(1)} %fusion.refs_1_), channel_id=1, source_target_pairs={{0,1},{1,0},{2,3},{3,2},{4,5},{5,4},{6,7},{7,6},{8,9},{9,8},{10,11... | collective-permute-start | bytes 1572872 | tf_op jit(solution)/shard_map/ppermute | solution.py:266
  55.1 11.2 %collective-permute-start.9 = (f32[1024,128]{1,0:T(8,128)S(1)}, f32[1024,128]{1,0:T(8,128)S(1)}, u32[]{:S(2)}, u32[]{:S(2)}) collective-permute-start(f32[1024,128]{1,0:T(8,128)S(1)} %collective-permute-done.7.refs_0_), channel_id=1, source_target_pairs={{0,2},{1,3},{2,4},{3,5},{4,6},{5,7},{6,14},{7,15},{8,0},{9,1},{10,... | collective-permute-start | bytes 1572872 | tf_op jit(solution)/shard_map/ppermute | solution.py:258
  68.5 2.4 %collective-permute-start.11 = (f32[2,512,128]{2,1,0:T(8,128)S(1)}, f32[2,512,128]{2,1,0:T(8,128)S(1)}, u32[]{:S(2)}, u32[]{:S(2)}) collective-permute-start(f32[2,512,128]{2,1,0:T(8,128)S(1)} %get-tuple-element.56), channel_id=1, source_target_pairs={{0,8},{8,0},{16,24},{24,16},{1,9},{9,1},{17,25},{25,17},{2,10},{10... | collective-permute-start | bytes 1572872 | tf_op jit(solution)/shard_map/ppermute | solution.py:220
  68.5 9.2 %collective-permute-start.14 = (f32[1024,128]{1,0:T(8,128)S(1)}, f32[1024,128]{1,0:T(8,128)S(1)}, u32[]{:S(2)}, u32[]{:S(2)}) collective-permute-start(f32[1024,128]{1,0:T(8,128)S(1)} %collective-permute-done.9.refs_1_), channel_id=1, source_target_pairs={{0,2},{1,3},{2,4},{3,5},{4,6},{5,7},{6,14},{7,15},{8,0},{9,1},{10,... | collective-permute-start | bytes 1572872 | tf_op jit(solution)/shard_map/ppermute | solution.py:294
  70.9 9.0 %collective-permute-start.12 = (f32[1,512,128]{2,1,0:T(8,128)S(1)}, f32[1,512,128]{2,1,0:T(8,128)S(1)}, u32[]{:S(2)}, u32[]{:S(2)}) collective-permute-start(f32[1,512,128]{2,1,0:T(8,128)S(1)} %slice_add_fusion.6), channel_id=1, source_target_pairs={{0,16},{8,24},{16,0},{24,8},{1,17},{9,25},{17,1},{25,9},{2,18},{10... | collective-permute-start | bytes 786440 | tf_op jit(solution)/shard_map/ppermute | solution.py:220
  79.9 2.0 %collective-permute-start.15 = (f32[2,512,128]{2,1,0:T(8,128)S(1)}, f32[2,512,128]{2,1,0:T(8,128)S(1)}, u32[]{:S(2)}, u32[]{:S(2)}) collective-permute-start(f32[2,512,128]{2,1,0:T(8,128)S(1)} %get-tuple-element.60), channel_id=1, source_target_pairs={{0,8},{8,0},{16,24},{24,16},{1,9},{9,1},{17,25},{25,17},{2,10},{10... | collective-permute-start | bytes 1572872 | tf_op jit(solution)/shard_map/ppermute | solution.py:220
  81.9 11.5 %collective-permute-start.16 = (f32[1,512,128]{2,1,0:T(8,128)S(1)}, f32[1,512,128]{2,1,0:T(8,128)S(1)}, u32[]{:S(2)}, u32[]{:S(2)}) collective-permute-start(f32[1,512,128]{2,1,0:T(8,128)S(1)} %slice_add_fusion.4), channel_id=1, source_target_pairs={{0,16},{8,24},{16,0},{24,8},{1,17},{9,25},{17,1},{25,9},{2,18},{10... | collective-permute-start | bytes 786440 | tf_op jit(solution)/shard_map/ppermute | solution.py:220
  83.5 5.3 %collective-permute-start.17 = (f32[256,128]{1,0:T(8,128)S(1)}, f32[256,128]{1,0:T(8,128)S(1)}, u32[]{:S(2)}, u32[]{:S(2)}) collective-permute-start(f32[256,128]{1,0:T(8,128)S(1)} %get-tuple-element.66), channel_id=1, source_target_pairs={{0,1},{1,0},{2,3},{3,2},{4,5},{5,4},{6,7},{7,6},{8,9},{9,8},{10,11... | collective-permute-start | bytes 393224 | tf_op jit(solution)/shard_map/ppermute | solution.py:308
  85.1 12.6 %collective-permute-start.13 = (f32[512,128]{1,0:T(8,128)S(1)}, f32[512,128]{1,0:T(8,128)S(1)}, u32[]{:S(2)}, u32[]{:S(2)}) collective-permute-start(f32[512,128]{1,0:T(8,128)S(1)} %bitcast.18), channel_id=1, source_target_pairs={{0,0},{1,1},{2,8},{3,9},{4,16},{5,17},{6,24},{7,25},{8,2},{9,3},{1... | collective-permute-start | bytes 786440 | tf_op jit(solution)/shard_map/ppermute | solution.py:304
  93.5 15.4 %collective-permute-start.18 = (f32[512,128]{1,0:T(8,128)S(1)}, f32[512,128]{1,0:T(8,128)S(1)}, u32[]{:S(2)}, u32[]{:S(2)}) collective-permute-start(f32[512,128]{1,0:T(8,128)S(1)} %bitcast.19), channel_id=1, source_target_pairs={{0,4},{1,5},{2,12},{3,13},{4,20},{5,21},{6,28},{7,29},{8,6},{9,7},... | collective-permute-start | bytes 786440 | tf_op jit(solution)/shard_map/ppermute | solution.py:304
  93.6 12.2 %collective-permute-start.19 = (f32[256,128]{1,0:T(8,128)S(1)}, f32[256,128]{1,0:T(8,128)S(1)}, u32[]{:S(2)}, u32[]{:S(2)}) collective-permute-start(f32[256,128]{1,0:T(8,128)S(1)} %get-tuple-element.64), channel_id=1, source_target_pairs={{0,16},{1,17},{2,18},{3,19},{4,20},{5,21},{6,22},{7,23},{8,24},{9,... | collective-permute-start | bytes 393224 | tf_op jit(solution)/shard_map/ppermute | solution.py:308
  96.3 12.6 %collective-permute-start.20 = (f32[256,128]{1,0:T(8,128)S(1)}, f32[256,128]{1,0:T(8,128)S(1)}, u32[]{:S(2)}, u32[]{:S(2)}) collective-permute-start(f32[256,128]{1,0:T(8,128)S(1)} %get-tuple-element.63), channel_id=1, source_target_pairs={{0,17},{1,16},{2,19},{3,18},{4,21},{5,20},{6,23},{7,22},{8,25},{9,... | collective-permute-start | bytes 393224 | tf_op jit(solution)/shard_map/ppermute | solution.py:308

commit v8 on v7

--- a/solution.py
+++ b/solution.py
@@ -59,11 +59,11 @@
                 signed, jnp.concatenate(two_parts(slab_ref[rows, columns]), axis=0), preferred_element_type=jnp.float32
             )
 
-        @pl.loop(0, INNER // 8, unroll=4)
+        @pl.loop(0, INNER // 8, unroll=8)
         def _(tile):
             combine([base + at * INNER + tile * 8 for at in range(inner_blocks)], False)
 
-    @pl.loop(0, block // 8, unroll=4)
+    @pl.loop(0, block // 8, unroll=8)
     def _(tile):
         combine([at * block + tile * 8 for at in range(steps)], True)
 
@@ -75,7 +75,7 @@
 def gather(groups, first, spot_ref, index_ref, mixed, out_ref):
     count = index_ref.shape[0] // groups
     bits = groups.bit_length() - 1
-    unroll = min(128, count)
+    unroll = min(256, count)
     for place in range(groups // 2):
         start = (spot_ref[0] ^ bit_reverse(first + place, bits)) * count
 

time: 111 us -> 110 us (level)
  transfers between devices with their start and end apart: 21 -> 21, of which waited for: 15 -> 15; matrix products, arithmetic and copies ran while one was open for 0% -> 0% of each run, Pallas kernels for 14% -> 13%
where the time goes in v8:
time: 110 us
  waiting for transfers between devices  55.9 us (51%)
  Pallas kernels  24.8 us (23%)
  starting transfers between devices  23.8 us (22%)
  local copies, waits for them, and re-layouts  4.2 us (4%)
  other arithmetic  1.24 us (1%)
    ppermute x8, waiting for transfers between devices, halve(): got = lax.ppermute(send, 'rows', [(r, r ^ 1 << at) for r in range(groups)])  19.3 us
    pallas_call x2, Pallas kernels, picked_strip(): pl.pallas_call(kernel, out_shape=out_shape, in_specs=[SMEM, SMEM, VMEM, V...  14.5 us
    ppermute x3, waiting for transfers between devices, shards(): part = lax.ppermute(part, AXES, pairs(lambda r, c: (r ^ flip, c ^ off)))  14.3 us
    ppermute x5, waiting for transfers between devices, shards(): moving = lax.ppermute(moving, AXES, ring)  13.4 us
    ppermute x5, starting transfers between devices, shards(): moving = lax.ppermute(moving, AXES, ring)  7.58 us
    ppermute x3, starting transfers between devices, shards(): part = lax.ppermute(part, AXES, pairs(lambda r, c: (r ^ flip, c ^ off)))  5.59 us
    ppermute x1, waiting for transfers between devices, shards(): remote[strip + 1].append(lax.ppermute(moving, AXES, ring))  5.33 us
    ppermute x8, starting transfers between devices, halve(): got = lax.ppermute(send, 'rows', [(r, r ^ 1 << at) for r in range(groups)])  4.58 us
  transfers between devices with their start and end apart: 21, of which 15 were waited for; matrix products, arithmetic and copies ran while one was open for 0% of the time, Pallas kernels for 13%

profile of v8, /device:TPU:18, one launch (start us, length us, event | category | flops | bytes accessed | tf_op | source)
XLA Modules:
  0.0 110.1 jit_solution(16462157385033424688)
XLA Ops:
  0.8 3.4 %copy-done = f32[8192,256]{1,0:T(8,128)S(1)} copy-done((f32[8192,256]{1,0:T(8,128)S(1)}, f32[8192,256]{1,0:T(8,128)}, u32[]{:S(2)}) %copy-start) | copy-done | bytes 8388632
  5.0 6.5 %transform_and_pick.2 = (f32[2048,128]{1,0:T(8,128)S(1)}, f32[16384,128]{1,0:T(8,128)S(1)}) custom-call(s32[3]{0:T(128)S(1)} %pad_add_fusion.refs_0_.spot_ref, s32[4096]{0:T(1024)S(1)} %multiply_add_fusion.refs_1_.index_ref, s32[8,8,128]{2,1,0:T(8,128)S(1)} %bitcast.16, f32[8192,256]{1,0:T(8,128)S(1)} %copy-done), custom_call_target="tpu_custom_call" | custom-call | flops 2147483648 | bytes 25165824 | tf_op jit(solution)/shard_map/transform_and_pick/pallas_call | solution.py:104
  11.5 2.5 %pick.1 = f32[2048,128]{1,0:T(8,128)S(1)} custom-call(s32[3]{0:T(128)S(1)} %pad_add_fusion.refs_0_.spot_ref, s32[4096]{0:T(1024)S(1)} %multiply_add_fusion.refs_1_.index_ref, f32[16384,128]{1,0:T(8,128)S(1)} %get-tuple-element.34.mixed), custom_call_target="tpu_custom_call" | custom-call | tf_op jit(solution)/shard_map/pick/pallas_call | solution.py:118
  14.8 8.1 %transform_and_pick.3 = (f32[2048,128]{1,0:T(8,128)S(1)}, f32[2048,128]{1,0:T(8,128)S(1)}) custom-call(s32[3]{0:T(128)S(1)} %pad_add_fusion.refs_0_.spot_ref, s32[4096]{0:T(1024)S(1)} %multiply_add_fusion.refs_1_.index_ref, s32[8,8,128]{2,1,0:T(8,128)S(1)} %bitcast.17, f32[8192,256]{1,0:T(8,128)S(1)} %bitcast.15), custom_call_target="tpu_custom_call" | custom-call | flops 2147483648 | bytes 25165824 | tf_op jit(solution)/shard_map/transform_and_pick/pallas_call | solution.py:104
  22.9 5.5 %collective-permute-done.1 = f32[1024,128]{1,0:T(8,128)S(1)} collective-permute-done((f32[1024,128]{1,0:T(8,128)S(1)}, f32[1024,128]{1,0:T(8,128)S(1)}, u32[]{:S(2)}, u32[]{:S(2)}) %collective-permute-start.1) | collective-permute-done | bytes 524320 | tf_op jit(solution)/shard_map/ppermute | solution.py:220
  28.6 1.6 %collective-permute-start.4 = (f32[1024,128]{1,0:T(8,128)S(1)}, f32[1024,128]{1,0:T(8,128)S(1)}, u32[]{:S(2)}, u32[]{:S(2)}) collective-permute-start(f32[1024,128]{1,0:T(8,128)S(1)} %fusion.1.refs_0_), channel_id=1, source_target_pairs={{0,2},{1,3},{2,4},{3,5},{4,6},{5,7},{6,14},{7,15},{8,0},{9,1},{10,... | collective-permute-start | bytes 1572872 | tf_op jit(solution)/shard_map/ppermute | solution.py:258
  31.9 1.5 %collective-permute-start.5 = (f32[1024,128]{1,0:T(8,128)S(1)}, f32[1024,128]{1,0:T(8,128)S(1)}, u32[]{:S(2)}, u32[]{:S(2)}) collective-permute-start(f32[1024,128]{1,0:T(8,128)S(1)} %fusion.1.refs_0_), channel_id=1, source_target_pairs={{0,1},{1,0},{2,3},{3,2},{4,5},{5,4},{6,7},{7,6},{8,9},{9,8},{10,11... | collective-permute-start | bytes 1572872 | tf_op jit(solution)/shard_map/ppermute | solution.py:266
  33.4 4.4 %collective-permute-done.4.refs_0_ = f32[1024,128]{1,0:T(8,128)S(1)} collective-permute-done((f32[1024,128]{1,0:T(8,128)S(1)}, f32[1024,128]{1,0:T(8,128)S(1)}, u32[]{:S(2)}, u32[]{:S(2)}) %collective-permute-start.4) | collective-permute-done | bytes 524320 | tf_op jit(solution)/shard_map/ppermute | solution.py:258
  37.8 1.6 %collective-permute-start.8 = (f32[1024,128]{1,0:T(8,128)S(1)}, f32[1024,128]{1,0:T(8,128)S(1)}, u32[]{:S(2)}, u32[]{:S(2)}) collective-permute-start(f32[1024,128]{1,0:T(8,128)S(1)} %collective-permute-done.4.refs_0_), channel_id=1, source_target_pairs={{0,2},{1,3},{2,4},{3,5},{4,6},{5,7},{6,14},{7,15},{8,0},{9,1},{10,... | collective-permute-start | bytes 1572872 | tf_op jit(solution)/shard_map/ppermute | solution.py:258
  39.4 6.0 %collective-permute-done.3 = f32[1024,128]{1,0:T(8,128)S(1)} collective-permute-done((f32[1024,128]{1,0:T(8,128)S(1)}, f32[1024,128]{1,0:T(8,128)S(1)}, u32[]{:S(2)}, u32[]{:S(2)}) %collective-permute-start.3) | collective-permute-done | bytes 524320 | tf_op jit(solution)/shard_map/ppermute | solution.py:220
  45.7 1.6 %collective-permute-start.7 = (f32[1024,128]{1,0:T(8,128)S(1)}, f32[1024,128]{1,0:T(8,128)S(1)}, u32[]{:S(2)}, u32[]{:S(2)}) collective-permute-start(f32[1024,128]{1,0:T(8,128)S(1)} %fusion.refs_1_), channel_id=1, source_target_pairs={{0,2},{1,3},{2,4},{3,5},{4,6},{5,7},{6,14},{7,15},{8,0},{9,1},{10,... | collective-permute-start | bytes 1572872 | tf_op jit(solution)/shard_map/ppermute | solution.py:258
  48.5 1.5 %collective-permute-start.6 = (f32[1024,128]{1,0:T(8,128)S(1)}, f32[1024,128]{1,0:T(8,128)S(1)}, u32[]{:S(2)}, u32[]{:S(2)}) collective-permute-start(f32[1024,128]{1,0:T(8,128)S(1)} %fusion.refs_1_), channel_id=1, source_target_pairs={{0,1},{1,0},{2,3},{3,2},{4,5},{5,4},{6,7},{7,6},{8,9},{9,8},{10,11... | collective-permute-start | bytes 1572872 | tf_op jit(solution)/shard_map/ppermute | solution.py:266
  50.1 4.8 %collective-permute-done.7.refs_0_ = f32[1024,128]{1,0:T(8,128)S(1)} collective-permute-done((f32[1024,128]{1,0:T(8,128)S(1)}, f32[1024,128]{1,0:T(8,128)S(1)}, u32[]{:S(2)}, u32[]{:S(2)}) %collective-permute-start.7) | collective-permute-done | bytes 524320 | tf_op jit(solution)/shard_map/ppermute | solution.py:258
  54.9 1.6 %collective-permute-start.9 = (f32[1024,128]{1,0:T(8,128)S(1)}, f32[1024,128]{1,0:T(8,128)S(1)}, u32[]{:S(2)}, u32[]{:S(2)}) collective-permute-start(f32[1024,128]{1,0:T(8,128)S(1)} %collective-permute-done.7.refs_0_), channel_id=1, source_target_pairs={{0,2},{1,3},{2,4},{3,5},{4,6},{5,7},{6,14},{7,15},{8,0},{9,1},{10,... | collective-permute-start | bytes 1572872 | tf_op jit(solution)/shard_map/ppermute | solution.py:258
  56.4 3.3 %collective-permute-done.6.refs_3_ = f32[1024,128]{1,0:T(8,128)S(1)} collective-permute-done((f32[1024,128]{1,0:T(8,128)S(1)}, f32[1024,128]{1,0:T(8,128)S(1)}, u32[]{:S(2)}, u32[]{:S(2)}) %collective-permute-start.6) | collective-permute-done | bytes 524320 | tf_op jit(solution)/shard_map/ppermute | solution.py:266
  59.7 2.1 %turn_plane.1 = (bf16[512,1024]{1,0:T(8,128)(2,1)S(1)}, bf16[512,1024]{1,0:T(8,128)(2,1)S(1)}, f32[512,256]{1,0:T(8,128)S(1)}) custom-call(s32[3]{0:T(128)S(1)} %pad_add_fusion.refs_0_.spot_ref, f32[1024,128]{1,0:T(8,128)S(1)} %fusion.1.refs_0_, f32[1024,128]{1,0:T(8,128)S(1)} %fusion.refs_1_, f32[1024,128]{1,0:T(8,128)S(1)} %collective-permute-done.5.refs_2_, ...), custom_call_target="tpu_custom_call" | custom-call | tf_op jit(solution)/shard_map/turn_plane/pallas_call | solution.py:271
  61.9 4.2 %collective-permute-done.9.refs_1_ = f32[1024,128]{1,0:T(8,128)S(1)} collective-permute-done((f32[1024,128]{1,0:T(8,128)S(1)}, f32[1024,128]{1,0:T(8,128)S(1)}, u32[]{:S(2)}, u32[]{:S(2)}) %collective-permute-start.9) | collective-permute-done | bytes 524320 | tf_op jit(solution)/shard_map/ppermute | solution.py:258
  66.1 2.1 %pair_products.2 = (f32[2,512,128]{2,1,0:T(8,128)S(1)}, f32[2,512,128]{2,1,0:T(8,128)S(1)}) custom-call(s32[3]{0:T(128)S(1)} %pad_add_fusion.refs_0_.spot_ref, bf16[512,1024]{1,0:T(8,128)(2,1)S(1)} %get-tuple-element.46.high_ref, bf16[512,1024]{1,0:T(8,128)(2,1)S(1)} %get-tuple-element.47.low_ref, f32[512,256]{1,0:T(8,128)S(1)} %get-tuple-element.48.own_ref, ...), custom_call_target="tpu_custom_call" | custom-call | tf_op jit(solution)/shard_map/pair_products/pallas_call | solution.py:284
  68.3 2.3 %collective-permute-start.14 = (f32[1024,128]{1,0:T(8,128)S(1)}, f32[1024,128]{1,0:T(8,128)S(1)}, u32[]{:S(2)}, u32[]{:S(2)}) collective-permute-start(f32[1024,128]{1,0:T(8,128)S(1)} %collective-permute-done.9.refs_1_), channel_id=1, source_target_pairs={{0,2},{1,3},{2,4},{3,5},{4,6},{5,7},{6,14},{7,15},{8,0},{9,1},{10,... | collective-permute-start | bytes 1572872 | tf_op jit(solution)/shard_map/ppermute | solution.py:294
  70.6 1.5 %collective-permute-start.12 = (f32[1,512,128]{2,1,0:T(8,128)S(1)}, f32[1,512,128]{2,1,0:T(8,128)S(1)}, u32[]{:S(2)}, u32[]{:S(2)}) collective-permute-start(f32[1,512,128]{2,1,0:T(8,128)S(1)} %slice_add_fusion.6), channel_id=1, source_target_pairs={{0,16},{8,24},{16,0},{24,8},{1,17},{9,25},{17,1},{25,9},{2,18},{10... | collective-permute-start | bytes 786440 | tf_op jit(solution)/shard_map/ppermute | solution.py:220
  72.1 5.3 %collective-permute-done.14.refs_2_ = f32[1024,128]{1,0:T(8,128)S(1)} collective-permute-done((f32[1024,128]{1,0:T(8,128)S(1)}, f32[1024,128]{1,0:T(8,128)S(1)}, u32[]{:S(2)}, u32[]{:S(2)}) %collective-permute-start.14) | collective-permute-done | bytes 524320 | tf_op jit(solution)/shard_map/ppermute | solution.py:294
  77.5 2.1 %pair_products.3 = (f32[2,512,128]{2,1,0:T(8,128)S(1)}, f32[2,512,128]{2,1,0:T(8,128)S(1)}) custom-call(s32[3]{0:T(128)S(1)} %pad_add_fusion.refs_0_.spot_ref, bf16[512,1024]{1,0:T(8,128)(2,1)S(1)} %get-tuple-element.46.high_ref, bf16[512,1024]{1,0:T(8,128)(2,1)S(1)} %get-tuple-element.47.low_ref, f32[512,256]{1,0:T(8,128)S(1)} %get-tuple-element.48.own_ref, ...), custom_call_target="tpu_custom_call" | custom-call | tf_op jit(solution)/shard_map/pair_products/pallas_call | solution.py:284
  79.7 1.9 %collective-permute-done.15 = f32[2,512,128]{2,1,0:T(8,128)S(1)} collective-permute-done((f32[2,512,128]{2,1,0:T(8,128)S(1)}, f32[2,512,128]{2,1,0:T(8,128)S(1)}, u32[]{:S(2)}, u32[]{:S(2)}) %collective-permute-start.15) | collective-permute-done | bytes 524320 | tf_op jit(solution)/shard_map/ppermute | solution.py:220
  81.6 1.6 %collective-permute-start.16 = (f32[1,512,128]{2,1,0:T(8,128)S(1)}, f32[1,512,128]{2,1,0:T(8,128)S(1)}, u32[]{:S(2)}, u32[]{:S(2)}) collective-permute-start(f32[1,512,128]{2,1,0:T(8,128)S(1)} %slice_add_fusion.4), channel_id=1, source_target_pairs={{0,16},{8,24},{16,0},{24,8},{1,17},{9,25},{17,1},{25,9},{2,18},{10... | collective-permute-start | bytes 786440 | tf_op jit(solution)/shard_map/ppermute | solution.py:220
  83.2 1.6 %collective-permute-start.17 = (f32[256,128]{1,0:T(8,128)S(1)}, f32[256,128]{1,0:T(8,128)S(1)}, u32[]{:S(2)}, u32[]{:S(2)}) collective-permute-start(f32[256,128]{1,0:T(8,128)S(1)} %get-tuple-element.66), channel_id=1, source_target_pairs={{0,1},{1,0},{2,3},{3,2},{4,5},{5,4},{6,7},{7,6},{8,9},{9,8},{10,11... | collective-permute-start | bytes 393224 | tf_op jit(solution)/shard_map/ppermute | solution.py:308
  85.5 3.1 %collective-permute-done.17.refs_4_ = f32[256,128]{1,0:T(8,128)S(1)} collective-permute-done((f32[256,128]{1,0:T(8,128)S(1)}, f32[256,128]{1,0:T(8,128)S(1)}, u32[]{:S(2)}, u32[]{:S(2)}) %collective-permute-start.17) | collective-permute-done | bytes 131104 | tf_op jit(solution)/shard_map/ppermute | solution.py:308
  88.5 4.7 %collective-permute-done.16 = f32[1,512,128]{2,1,0:T(8,128)S(1)} collective-permute-done((f32[1,512,128]{2,1,0:T(8,128)S(1)}, f32[1,512,128]{2,1,0:T(8,128)S(1)}, u32[]{:S(2)}, u32[]{:S(2)}) %collective-permute-start.16) | collective-permute-done | bytes 262176 | tf_op jit(solution)/shard_map/ppermute | solution.py:220
  93.3 2.7 %collective-permute-start.19 = (f32[256,128]{1,0:T(8,128)S(1)}, f32[256,128]{1,0:T(8,128)S(1)}, u32[]{:S(2)}, u32[]{:S(2)}) collective-permute-start(f32[256,128]{1,0:T(8,128)S(1)} %get-tuple-element.64), channel_id=1, source_target_pairs={{0,16},{1,17},{2,18},{3,19},{4,20},{5,21},{6,22},{7,23},{8,24},{9,... | collective-permute-start | bytes 393224 | tf_op jit(solution)/shard_map/ppermute | solution.py:308
  96.0 1.3 %collective-permute-start.20 = (f32[256,128]{1,0:T(8,128)S(1)}, f32[256,128]{1,0:T(8,128)S(1)}, u32[]{:S(2)}, u32[]{:S(2)}) collective-permute-start(f32[256,128]{1,0:T(8,128)S(1)} %get-tuple-element.63), channel_id=1, source_target_pairs={{0,17},{1,16},{2,19},{3,18},{4,21},{5,20},{6,23},{7,22},{8,25},{9,... | collective-permute-start | bytes 393224 | tf_op jit(solution)/shard_map/ppermute | solution.py:308
  97.4 8.1 %collective-permute-done.19.refs_3_ = f32[256,128]{1,0:T(8,128)S(1)} collective-permute-done((f32[256,128]{1,0:T(8,128)S(1)}, f32[256,128]{1,0:T(8,128)S(1)}, u32[]{:S(2)}, u32[]{:S(2)}) %collective-permute-start.19) | collective-permute-done | bytes 131104 | tf_op jit(solution)/shard_map/ppermute | solution.py:308
  105.5 3.1 %collective-permute-done.20.refs_5_ = f32[256,128]{1,0:T(8,128)S(1)} collective-permute-done((f32[256,128]{1,0:T(8,128)S(1)}, f32[256,128]{1,0:T(8,128)S(1)}, u32[]{:S(2)}, u32[]{:S(2)}) %collective-permute-start.20) | collective-permute-done | bytes 131104 | tf_op jit(solution)/shard_map/ppermute | solution.py:308
  108.6 1.5 %finish.1 = f32[512,256]{1,0:T(8,128)} custom-call(s32[3]{0:T(128)S(1)} %pad_add_fusion.refs_0_.spot_ref, f32[512,128]{1,0:T(8,128)S(1)} %collective-permute-done.13.refs_0_, f32[512,128]{1,0:T(8,128)S(1)} %collective-permute-done.18.refs_1_, f32[256,128]{1,0:T(8,128)S(1)} %get-tuple-element.65.refs_2_, f32[256,128]{1,0:T(8,128)S(1)} %collective-permute-done.19.refs_3_, ...), custom_call_target="tpu_custom_call" | custom-call | tf_op jit(solution)/shard_map/finish/pallas_call | solution.py:312
  (38 shorter events, 7.0 us)
Async XLA Ops:
  0.8 3.4 %copy-start = (f32[8192,256]{1,0:T(8,128)S(1)}, f32[8192,256]{1,0:T(8,128)}, u32[]{:S(2)}) copy-start(f32[8192,256]{1,0:T(8,128)} %slab_ref.1) | copy-start | bytes 25165828
  4.2 0.8 copy-start.1
  5.0 9.9 %slice-start = ((s8[8388608]{0:T(1024)(128)(4,1)}), s8[4194304]{0:T(1024)(128)(4,1)S(1)}, s32[]{:S(2)}) async-start(s8[8388608]{0:T(1024)(128)(4,1)} %bitcast.14), calls=%async_computation | async-start | bytes 8388608
  11.4 2.7 %collective-permute-start = (f32[2048,128]{1,0:T(8,128)S(1)}, f32[2048,128]{1,0:T(8,128)S(1)}, u32[]{:S(2)}, u32[]{:S(2)}) collective-permute-start(f32[2048,128]{1,0:T(8,128)S(1)} %get-tuple-element.35), channel_id=1, source_target_pairs={{0,8},{8,0},{16,24},{24,16},{1,9},{9,1},{17,25},{25,17},{2,10},{10... | collective-permute-start | bytes 3145736 | tf_op jit(solution)/shard_map/ppermute | solution.py:220
  11.5 3.3 %slice-start.1 = ((s8[8388608]{0:T(1024)(128)(4,1)}), s8[4194304]{0:T(1024)(128)(4,1)S(1)}, s32[]{:S(2)}) async-start(s8[8388608]{0:T(1024)(128)(4,1)} %bitcast.14), calls=%async_computation.1 | async-start | bytes 8388608
  14.2 14.2 %collective-permute-start.1 = (f32[1024,128]{1,0:T(8,128)S(1)}, f32[1024,128]{1,0:T(8,128)S(1)}, u32[]{:S(2)}, u32[]{:S(2)}) collective-permute-start(f32[1024,128]{1,0:T(8,128)S(1)} %slice_add_fusion.3), channel_id=1, source_target_pairs={{0,16},{8,24},{16,0},{24,8},{1,17},{9,25},{17,1},{25,9},{2,18},{10... | collective-permute-start | bytes 1572872 | tf_op jit(solution)/shard_map/ppermute | solution.py:220
  28.5 2.7 %collective-permute-start.2 = (f32[2048,128]{1,0:T(8,128)S(1)}, f32[2048,128]{1,0:T(8,128)S(1)}, u32[]{:S(2)}, u32[]{:S(2)}) collective-permute-start(f32[2048,128]{1,0:T(8,128)S(1)} %get-tuple-element.41), channel_id=1, source_target_pairs={{0,8},{8,0},{16,24},{24,16},{1,9},{9,1},{17,25},{25,17},{2,10},{10... | collective-permute-start | bytes 3145736 | tf_op jit(solution)/shard_map/ppermute | solution.py:220
  28.6 9.2 %collective-permute-start.4 = (f32[1024,128]{1,0:T(8,128)S(1)}, f32[1024,128]{1,0:T(8,128)S(1)}, u32[]{:S(2)}, u32[]{:S(2)}) collective-permute-start(f32[1024,128]{1,0:T(8,128)S(1)} %fusion.1.refs_0_), channel_id=1, source_target_pairs={{0,2},{1,3},{2,4},{3,5},{4,6},{5,7},{6,14},{7,15},{8,0},{9,1},{10,... | collective-permute-start | bytes 1572872 | tf_op jit(solution)/shard_map/ppermute | solution.py:258
  31.3 14.0 %collective-permute-start.3 = (f32[1024,128]{1,0:T(8,128)S(1)}, f32[1024,128]{1,0:T(8,128)S(1)}, u32[]{:S(2)}, u32[]{:S(2)}) collective-permute-start(f32[1024,128]{1,0:T(8,128)S(1)} %slice_add_fusion), channel_id=1, source_target_pairs={{0,16},{8,24},{16,0},{24,8},{1,17},{9,25},{17,1},{25,9},{2,18},{10... | collective-permute-start | bytes 1572872 | tf_op jit(solution)/shard_map/ppermute | solution.py:220
  31.9 13.7 %collective-permute-start.5 = (f32[1024,128]{1,0:T(8,128)S(1)}, f32[1024,128]{1,0:T(8,128)S(1)}, u32[]{:S(2)}, u32[]{:S(2)}) collective-permute-start(f32[1024,128]{1,0:T(8,128)S(1)} %fusion.1.refs_0_), channel_id=1, source_target_pairs={{0,1},{1,0},{2,3},{3,2},{4,5},{5,4},{6,7},{7,6},{8,9},{9,8},{10,11... | collective-permute-start | bytes 1572872 | tf_op jit(solution)/shard_map/ppermute | solution.py:266
  37.8 9.5 %collective-permute-start.8 = (f32[1024,128]{1,0:T(8,128)S(1)}, f32[1024,128]{1,0:T(8,128)S(1)}, u32[]{:S(2)}, u32[]{:S(2)}) collective-permute-start(f32[1024,128]{1,0:T(8,128)S(1)} %collective-permute-done.4.refs_0_), channel_id=1, source_target_pairs={{0,2},{1,3},{2,4},{3,5},{4,6},{5,7},{6,14},{7,15},{8,0},{9,1},{10,... | collective-permute-start | bytes 1572872 | tf_op jit(solution)/shard_map/ppermute | solution.py:258
  45.7 9.2 %collective-permute-start.7 = (f32[1024,128]{1,0:T(8,128)S(1)}, f32[1024,128]{1,0:T(8,128)S(1)}, u32[]{:S(2)}, u32[]{:S(2)}) collective-permute-start(f32[1024,128]{1,0:T(8,128)S(1)} %fusion.refs_1_), channel_id=1, source_target_pairs={{0,2},{1,3},{2,4},{3,5},{4,6},{5,7},{6,14},{7,15},{8,0},{9,1},{10,... | collective-permute-start | bytes 1572872 | tf_op jit(solution)/shard_map/ppermute | solution.py:258
  47.3 14.6 %collective-permute-start.10 = (f32[1024,128]{1,0:T(8,128)S(1)}, f32[1024,128]{1,0:T(8,128)S(1)}, u32[]{:S(2)}, u32[]{:S(2)}) collective-permute-start(f32[1024,128]{1,0:T(8,128)S(1)} %collective-permute-done.8.refs_1_), channel_id=1, source_target_pairs={{0,2},{1,3},{2,4},{3,5},{4,6},{5,7},{6,14},{7,15},{8,0},{9,1},{10,... | collective-permute-start | bytes 1572872 | tf_op jit(solution)/shard_map/ppermute | solution.py:258
  48.5 11.2 %collective-permute-start.6 = (f32[1024,128]{1,0:T(8,128)S(1)}, f32[1024,128]{1,0:T(8,128)S(1)}, u32[]{:S(2)}, u32[]{:S(2)}) collective-permute-start(f32[1024,128]{1,0:T(8,128)S(1)} %fusion.refs_1_), channel_id=1, source_target_pairs={{0,1},{1,0},{2,3},{3,2},{4,5},{5,4},{6,7},{7,6},{8,9},{9,8},{10,11... | collective-permute-start | bytes 1572872 | tf_op jit(solution)/shard_map/ppermute | solution.py:266
  54.9 11.2 %collective-permute-start.9 = (f32[1024,128]{1,0:T(8,128)S(1)}, f32[1024,128]{1,0:T(8,128)S(1)}, u32[]{:S(2)}, u32[]{:S(2)}) collective-permute-start(f32[1024,128]{1,0:T(8,128)S(1)} %collective-permute-done.7.refs_0_), channel_id=1, source_target_pairs={{0,2},{1,3},{2,4},{3,5},{4,6},{5,7},{6,14},{7,15},{8,0},{9,1},{10,... | collective-permute-start | bytes 1572872 | tf_op jit(solution)/shard_map/ppermute | solution.py:258
  68.2 2.4 %collective-permute-start.11 = (f32[2,512,128]{2,1,0:T(8,128)S(1)}, f32[2,512,128]{2,1,0:T(8,128)S(1)}, u32[]{:S(2)}, u32[]{:S(2)}) collective-permute-start(f32[2,512,128]{2,1,0:T(8,128)S(1)} %get-tuple-element.56), channel_id=1, source_target_pairs={{0,8},{8,0},{16,24},{24,16},{1,9},{9,1},{17,25},{25,17},{2,10},{10... | collective-permute-start | bytes 1572872 | tf_op jit(solution)/shard_map/ppermute | solution.py:220
  68.3 9.2 %collective-permute-start.14 = (f32[1024,128]{1,0:T(8,128)S(1)}, f32[1024,128]{1,0:T(8,128)S(1)}, u32[]{:S(2)}, u32[]{:S(2)}) collective-permute-start(f32[1024,128]{1,0:T(8,128)S(1)} %collective-permute-done.9.refs_1_), channel_id=1, source_target_pairs={{0,2},{1,3},{2,4},{3,5},{4,6},{5,7},{6,14},{7,15},{8,0},{9,1},{10,... | collective-permute-start | bytes 1572872 | tf_op jit(solution)/shard_map/ppermute | solution.py:294
  70.6 9.0 %collective-permute-start.12 = (f32[1,512,128]{2,1,0:T(8,128)S(1)}, f32[1,512,128]{2,1,0:T(8,128)S(1)}, u32[]{:S(2)}, u32[]{:S(2)}) collective-permute-start(f32[1,512,128]{2,1,0:T(8,128)S(1)} %slice_add_fusion.6), channel_id=1, source_target_pairs={{0,16},{8,24},{16,0},{24,8},{1,17},{9,25},{17,1},{25,9},{2,18},{10... | collective-permute-start | bytes 786440 | tf_op jit(solution)/shard_map/ppermute | solution.py:220
  79.6 2.0 %collective-permute-start.15 = (f32[2,512,128]{2,1,0:T(8,128)S(1)}, f32[2,512,128]{2,1,0:T(8,128)S(1)}, u32[]{:S(2)}, u32[]{:S(2)}) collective-permute-start(f32[2,512,128]{2,1,0:T(8,128)S(1)} %get-tuple-element.60), channel_id=1, source_target_pairs={{0,8},{8,0},{16,24},{24,16},{1,9},{9,1},{17,25},{25,17},{2,10},{10... | collective-permute-start | bytes 1572872 | tf_op jit(solution)/shard_map/ppermute | solution.py:220
  81.6 11.6 %collective-permute-start.16 = (f32[1,512,128]{2,1,0:T(8,128)S(1)}, f32[1,512,128]{2,1,0:T(8,128)S(1)}, u32[]{:S(2)}, u32[]{:S(2)}) collective-permute-start(f32[1,512,128]{2,1,0:T(8,128)S(1)} %slice_add_fusion.4), channel_id=1, source_target_pairs={{0,16},{8,24},{16,0},{24,8},{1,17},{9,25},{17,1},{25,9},{2,18},{10... | collective-permute-start | bytes 786440 | tf_op jit(solution)/shard_map/ppermute | solution.py:220
  83.2 5.3 %collective-permute-start.17 = (f32[256,128]{1,0:T(8,128)S(1)}, f32[256,128]{1,0:T(8,128)S(1)}, u32[]{:S(2)}, u32[]{:S(2)}) collective-permute-start(f32[256,128]{1,0:T(8,128)S(1)} %get-tuple-element.66), channel_id=1, source_target_pairs={{0,1},{1,0},{2,3},{3,2},{4,5},{5,4},{6,7},{7,6},{8,9},{9,8},{10,11... | collective-permute-start | bytes 393224 | tf_op jit(solution)/shard_map/ppermute | solution.py:308
  84.8 12.6 %collective-permute-start.13 = (f32[512,128]{1,0:T(8,128)S(1)}, f32[512,128]{1,0:T(8,128)S(1)}, u32[]{:S(2)}, u32[]{:S(2)}) collective-permute-start(f32[512,128]{1,0:T(8,128)S(1)} %bitcast.18), channel_id=1, source_target_pairs={{0,0},{1,1},{2,8},{3,9},{4,16},{5,17},{6,24},{7,25},{8,2},{9,3},{1... | collective-permute-start | bytes 786440 | tf_op jit(solution)/shard_map/ppermute | solution.py:304
  93.2 15.3 %collective-permute-start.18 = (f32[512,128]{1,0:T(8,128)S(1)}, f32[512,128]{1,0:T(8,128)S(1)}, u32[]{:S(2)}, u32[]{:S(2)}) collective-permute-start(f32[512,128]{1,0:T(8,128)S(1)} %bitcast.19), channel_id=1, source_target_pairs={{0,4},{1,5},{2,12},{3,13},{4,20},{5,21},{6,28},{7,29},{8,6},{9,7},... | collective-permute-start | bytes 786440 | tf_op jit(solution)/shard_map/ppermute | solution.py:304
  93.3 12.1 %collective-permute-start.19 = (f32[256,128]{1,0:T(8,128)S(1)}, f32[256,128]{1,0:T(8,128)S(1)}, u32[]{:S(2)}, u32[]{:S(2)}) collective-permute-start(f32[256,128]{1,0:T(8,128)S(1)} %get-tuple-element.64), channel_id=1, source_target_pairs={{0,16},{1,17},{2,18},{3,19},{4,20},{5,21},{6,22},{7,23},{8,24},{9,... | collective-permute-start | bytes 393224 | tf_op jit(solution)/shard_map/ppermute | solution.py:308
  96.0 12.5 %collective-permute-start.20 = (f32[256,128]{1,0:T(8,128)S(1)}, f32[256,128]{1,0:T(8,128)S(1)}, u32[]{:S(2)}, u32[]{:S(2)}) collective-permute-start(f32[256,128]{1,0:T(8,128)S(1)} %get-tuple-element.63), channel_id=1, source_target_pairs={{0,17},{1,16},{2,19},{3,18},{4,21},{5,20},{6,23},{7,22},{8,25},{9,... | collective-permute-start | bytes 393224 | tf_op jit(solution)/shard_map/ppermute | solution.py:308
